TPU v7x, 512 devices: a whole 4x8x8 slice. The times are simulated.
512 devices in a mesh: member: 8 (over y), sx: 8 (over z_hi, core), sy: 8 (over z_lo, x).
Axes of the slice: x: 4, y: 8, z: 8 (z_hi: 4, z_lo: 2; z = z_hi * 2 + z_lo), core: 2. Of those that a mesh axis runs over, the one named last changes fastest.
Arguments:
- states: bfloat16 [8, 256, 128, 512], P('member', 'sx', 'sy'), may hold values from -6 to 6
- noises: float32 [8, 32], P('member'), may hold values from -4 to 4
- codes: int32 [256, 128, 6], P('sx', 'sy'), may hold values from 0 to 8
- target: bfloat16 [256, 128, 128], P('sx', 'sy'), may hold values from -6 to 6
- w_self: bfloat16 [2, 512, 512], replicated, may hold values from -0.25 to 0.25
- w_nbr: bfloat16 [2, 512, 512], replicated, may hold values from -0.25 to 0.25
- w_out: bfloat16 [2, 512, 512], replicated, may hold values from -0.25 to 0.25
- w_scale: float32 [2, 32, 512], replicated, may hold values from -0.5 to 0.5
- w_shift: float32 [2, 32, 512], replicated, may hold values from -0.5 to 0.5
- w_dec: bfloat16 [512, 128], replicated, may hold values from -0.25 to 0.25
Outputs:
- preds: bfloat16 [8, 256, 128, 128], P('member', 'sx', 'sy')
- ranked_probability_score: float32 [256, 128, 128], P('sx', 'sy')
All inputs are finite; a program needn't handle non-finite values.
Results may differ from a plain program's by a relative error of at most 0.009.
Values may be sent and summed in bfloat16 or wider, within the bound.
No kernel may reach another device: no remote copies, remote signals or barrier semaphores. Data moves between devices by JAX's collectives and lax.ppermute only.
A program may use at most 64 MiB of HBM per device.

v0:
```python
import jax
import jax.numpy as jnp
from jax import lax
from jax.sharding import PartitionSpec as P


def padded_2(shard, sides, width):
    for axis, dim in sides:
        peers, length = (lax.axis_size(axis), shard.shape[dim])
        up = [(i, (i + 1) % peers) for i in range(peers - 1)]
        down = [(j, i) for i, j in up]
        last = lax.slice_in_dim(shard, length - width, length, axis=dim)
        initial = lax.slice_in_dim(shard, 0, width, axis=dim)
        before = lax.ppermute(last, axis, up)
        after = lax.ppermute(initial, axis, down)
        shard = jnp.concatenate([before, shard, after], axis=dim)
    return shard


def norm_rows(x):
    mean = jnp.mean(x, axis=-1, keepdims=True)
    var = jnp.mean((x - mean) ** 2, axis=-1, keepdims=True)
    return (x - mean) / jnp.sqrt(var + 1e-05)


def local(states, noises, codes, target, w_self, w_nbr, w_out, w_scale, w_shift, w_dec):
    x = states[0].astype(jnp.float32)
    noise = noises[0]
    line_indices_eastward, line_indices_northward = (x.shape[0], x.shape[1])
    rows = line_indices_eastward * line_indices_northward
    degree = codes.shape[2]
    counts = [
        jnp.sum((codes == code).astype(jnp.float32), axis=-1, keepdims=True) for code in range(9)
    ]
    for layer in range(w_self.shape[0]):
        scale = jnp.dot(noise, w_scale[layer], precision=lax.Precision.HIGHEST)
        shift = jnp.dot(noise, w_shift[layer], precision=lax.Precision.HIGHEST)
        normed = (norm_rows(x) * (1.0 + scale) + shift).astype(jnp.bfloat16)
        padded = padded_2(normed, (("sx", 0), ("sy", 1)), 1)
        total = jnp.zeros(normed.shape, jnp.float32)
        for code in range(9):
            displacement_east, displacement_north = (code // 3, code % 3)
            view = padded[
                displacement_east : displacement_east + line_indices_eastward,
                displacement_north : displacement_north + line_indices_northward,
            ]
            total = total + counts[code] * view.astype(jnp.float32)
        mixed = (total / degree).astype(jnp.bfloat16)
        pre = jnp.dot(normed.reshape(rows, -1), w_self[layer], preferred_element_type=jnp.float32)
        pre = pre + jnp.dot(
            mixed.reshape(rows, -1), w_nbr[layer], preferred_element_type=jnp.float32
        )
        hidden = jax.nn.silu(pre).astype(jnp.bfloat16)
        x = x + jnp.dot(hidden, w_out[layer], preferred_element_type=jnp.float32).reshape(x.shape)
    final = norm_rows(x).astype(jnp.bfloat16).reshape(rows, -1)
    raveled_outputs = jnp.dot(final, w_dec, preferred_element_type=jnp.float32).astype(jnp.bfloat16)
    predicted_grid = raveled_outputs.reshape(1, line_indices_eastward, line_indices_northward, -1)
    truth = target.astype(jnp.float32)
    ensemble_entries = lax.axis_size("member")
    denom = 2.0 * ensemble_entries * (ensemble_entries - 1)
    ensemble_wide_total = lax.all_gather(predicted_grid, "member", axis=0, tiled=True).astype(
        jnp.float32
    )
    skill = jnp.zeros(truth.shape, jnp.float32)
    spread = jnp.zeros(truth.shape, jnp.float32)
    for first in range(ensemble_entries):
        skill = skill + jnp.abs(ensemble_wide_total[first] - truth)
        spread = spread + jnp.sum(
            jnp.abs(ensemble_wide_total[first][None] - ensemble_wide_total), axis=0
        )
    ranked_probability_score = skill / ensemble_entries - spread / denom
    return (predicted_grid, ranked_probability_score)


def solution(mesh):
    placed = (
        P("member", "sx", "sy", None),
        P("member", None),
        P("sx", "sy", None),
        P("sx", "sy", None),
        P(),
        P(),
        P(),
        P(),
        P(),
        P(),
    )
    return jax.shard_map(
        local,
        mesh=mesh,
        in_specs=placed,
        out_specs=(P("member", "sx", "sy", None), P("sx", "sy", None)),
        check_vma=False,
    )
```

profile of v0, /device:TPU:2, one launch (start us, length us, event | category | flops | bytes accessed | tf_op | source)
XLA Modules:
  0.0 122.9 jit_solution(5587259322028620552)
XLA Ops:
  7.2 0.0 copy-start
  7.2 0.0 copy-start.9
  7.2 0.0 copy-start.7
  7.2 0.0 copy-start.1
  7.2 0.0 all-gather.2.cloned.1.call-start
  7.3 1.1 fusion.64
  8.4 1.0 fusion.62
  9.4 1.2 convert_reduce_fusion
  10.7 1.3 %fusion.19 = f32[32,16]{1,0:T(8,128)S(1)} fusion(bf16[1,32,16,512]{3,2,1,0:T(8,128)(2,1)} %param.10, f32[32,16]{1,0:T(8,128)S(1)} %broadcast_multiply_fusion.2), kind=kLoop, calls=%fused_computation.35 | loop fusion | flops 1048064 | bytes 528384 | tf_op jit(solution)/shard_map/reduce_sum | solution.py:22
  12.0 1.3 %fusion.22 = bf16[32,16,512]{2,1,0:T(8,128)(2,1)S(1)} fusion(bf16[1,32,16,512]{3,2,1,0:T(8,128)(2,1)} %param.10, f32[512]{0:T(512)S(1)} %bitcast.128, f32[512]{0:T(512)S(1)} %broadcast_add_fusion.1, f32[32,16]{1,0:T(8,128)S(1)} %add_sqrt_fusion.2, f32[32,16]{1,0:T(8,128)S(1)} %broadcast_multiply_fusion.2), kind=kLoop, calls=%fused_computation.38 | loop fusion | flops 1572864 | bytes 1056768 | tf_op jit(solution)/shard_map/convert_element_type | solution.py:38
  13.3 0.0 copy-start.8
  13.3 1.7 %collective-permute-start = (bf16[1,16,512]{2,1,0:T(8,128)(2,1)S(1)}, bf16[1,16,512]{2,1,0:T(8,128)(2,1)S(1)}, u32[]{:S(2)}, u32[]{:S(2)}) collective-permute-start(bf16[1,16,512]{2,1,0:T(8,128)(2,1)S(1)} %get-tuple-element.37), channel_id=1, source_target_pairs={{0,8},{8,16},{16,24},{24,32},{32,40},{40,48},{48,56},{1,9},{9,17},... | collective-permute-start | bytes 49160 | tf_op jit(solution)/shard_map/ppermute | solution.py:14
  15.1 1.3 %collective-permute-start.1 = (bf16[1,16,512]{2,1,0:T(8,128)(2,1)S(1)}, bf16[1,16,512]{2,1,0:T(8,128)(2,1)S(1)}, u32[]{:S(2)}, u32[]{:S(2)}) collective-permute-start(bf16[1,16,512]{2,1,0:T(8,128)(2,1)S(1)} %get-tuple-element.38), channel_id=1, source_target_pairs={{8,0},{16,8},{24,16},{32,24},{40,32},{48,40},{56,48},{9,1},{17,9},... | collective-permute-start | bytes 49160 | tf_op jit(solution)/shard_map/ppermute | solution.py:15
  16.4 0.1 fusion.60
  16.6 0.2 fusion.58
  16.7 0.3 fusion.26
  17.0 0.4 fusion.33
  17.5 0.0 collective-permute-done
  17.5 4.7 %collective-permute-done.1 = bf16[1,16,512]{2,1,0:T(8,128)(2,1)S(1)} collective-permute-done((bf16[1,16,512]{2,1,0:T(8,128)(2,1)S(1)}, bf16[1,16,512]{2,1,0:T(8,128)(2,1)S(1)}, u32[]{:S(2)}, u32[]{:S(2)}) %collective-permute-start.1) | collective-permute-done | bytes 16416 | tf_op jit(solution)/shard_map/ppermute | solution.py:15
  22.1 0.8 pad_maximum_fusion.11
  22.9 3.4 %collective-permute-start.2 = (bf16[34,1,512]{2,1,0:T(2,128)(2,1)}, bf16[34,1,512]{2,1,0:T(2,128)(2,1)S(1)}, u32[]{:S(2)}, u32[]{:S(2)}) collective-permute-start(bf16[34,1,512]{2,1,0:T(2,128)(2,1)} %get-tuple-element.33), channel_id=1, source_target_pairs={{0,1},{1,2},{2,3},{3,4},{4,5},{5,6},{6,7},{8,9},{9,10},{10,11},{11... | collective-permute-start | bytes 104456 | tf_op jit(solution)/shard_map/ppermute | solution.py:14
  26.3 2.4 %collective-permute-start.3 = (bf16[34,1,512]{2,1,0:T(2,128)(2,1)}, bf16[34,1,512]{2,1,0:T(2,128)(2,1)}, u32[]{:S(2)}, u32[]{:S(2)}) collective-permute-start(bf16[34,1,512]{2,1,0:T(2,128)(2,1)} %get-tuple-element.34), channel_id=1, source_target_pairs={{1,0},{2,1},{3,2},{4,3},{5,4},{6,5},{7,6},{9,8},{10,9},{11,10},{12... | collective-permute-start | bytes 104456 | tf_op jit(solution)/shard_map/ppermute | solution.py:15
  28.7 0.1 convert_reduce_fusion.9
  28.8 0.1 copy.12
  28.9 0.1 copy.18
  29.0 0.1 copy.17
  29.0 0.1 copy.16
  29.1 0.1 copy.15
  29.2 0.1 copy.14
  29.3 0.1 copy.13
  29.3 0.1 copy.20
  29.4 0.1 copy.19
  29.5 3.3 %collective-permute-done.3 = bf16[34,1,512]{2,1,0:T(2,128)(2,1)} collective-permute-done((bf16[34,1,512]{2,1,0:T(2,128)(2,1)}, bf16[34,1,512]{2,1,0:T(2,128)(2,1)}, u32[]{:S(2)}, u32[]{:S(2)}) %collective-permute-start.3) | collective-permute-done | bytes 34848 | tf_op jit(solution)/shard_map/ppermute | solution.py:15
  32.8 1.3 %maximum_maximum_fusion = (bf16[34,17,512]{2,1,0:T(8,128)(2,1)S(1)}, bf16[34,17,512]{2,1,0:T(8,128)(2,1)S(1)}) fusion(bf16[1,16,512]{2,1,0:T(8,128)(2,1)S(1)} %collective-permute-done.1, bf16[32,16,512]{2,1,0:T(8,128)(2,1)S(1)} %fusion.22, bf16[1,16,512]{2,1,0:T(8,128)(2,1)S(1)} %collective-permute-done, bf16[34,1,512]{2,1,0:T(2,128)(2,1)S(1)} %collective-permute-done.2, ...), kind=kLoop, calls=%fused_computation.51 | loop fusion | flops 4734976 | bytes 1810432 | tf_op jit(solution)/shard_map/concatenate | solution.py:16
  34.2 0.0 copy-start.10
  34.2 1.6 %multiply_convert_fusion.3 = bf16[32,16,512]{2,1,0:T(8,128)(2,1)S(1)} fusion(bf16[32,16,512]{2,1,0:T(8,128)(2,1)S(1)} %fusion.22, bf16[34,17,512]{2,1,0:T(8,128)(2,1)S(1)} %get-tuple-element.32, bf16[1,16,512]{2,1,0:T(8,128)(2,1)S(1)} %collective-permute-done.1, bf16[34,17,512]{2,1,0:T(8,128)(2,1)S(1)} %get-tuple-element.31, ...), kind=kLoop, calls=%fused_computation.50 | loop fusion | flops 7864320 | bytes 4245504 | tf_op jit(solution)/shard_map/convert_element_type | solution.py:48
  35.8 0.0 copy-start.3
  35.8 0.6 multiply_convert_fusion.2
  36.4 0.6 copy-done.3
  37.0 0.5 fusion.76
  37.6 0.3 multiply_reduce_fusion.1
  37.8 0.2 add_convert_fusion
  38.1 3.9 %collective-permute-start.4 = (bf16[1,16,512]{2,1,0:T(8,128)(2,1)S(1)}, bf16[1,16,512]{2,1,0:T(8,128)(2,1)S(1)}, u32[]{:S(2)}, u32[]{:S(2)}) collective-permute-start(bf16[1,16,512]{2,1,0:T(8,128)(2,1)S(1)} %get-tuple-element.35), channel_id=1, source_target_pairs={{0,8},{8,16},{16,24},{24,32},{32,40},{40,48},{48,56},{1,9},{9,17},... | collective-permute-start | bytes 49160 | tf_op jit(solution)/shard_map/ppermute | solution.py:14
  42.0 1.3 %collective-permute-start.5 = (bf16[1,16,512]{2,1,0:T(8,128)(2,1)S(1)}, bf16[1,16,512]{2,1,0:T(8,128)(2,1)S(1)}, u32[]{:S(2)}, u32[]{:S(2)}) collective-permute-start(bf16[1,16,512]{2,1,0:T(8,128)(2,1)S(1)} %get-tuple-element.36), channel_id=1, source_target_pairs={{8,0},{16,8},{24,16},{32,24},{40,32},{48,40},{56,48},{9,1},{17,9},... | collective-permute-start | bytes 49160 | tf_op jit(solution)/shard_map/ppermute | solution.py:15
  43.3 4.8 %collective-permute-done.5 = bf16[1,16,512]{2,1,0:T(8,128)(2,1)S(1)} collective-permute-done((bf16[1,16,512]{2,1,0:T(8,128)(2,1)S(1)}, bf16[1,16,512]{2,1,0:T(8,128)(2,1)S(1)}, u32[]{:S(2)}, u32[]{:S(2)}) %collective-permute-start.5) | collective-permute-done | bytes 16416 | tf_op jit(solution)/shard_map/ppermute | solution.py:15
  48.1 0.1 pad_maximum_fusion.8
  48.2 3.1 %collective-permute-start.6 = (bf16[34,1,512]{2,1,0:T(2,128)(2,1)S(1)}, bf16[34,1,512]{2,1,0:T(2,128)(2,1)S(1)}, u32[]{:S(2)}, u32[]{:S(2)}) collective-permute-start(bf16[34,1,512]{2,1,0:T(2,128)(2,1)S(1)} %get-tuple-element.29), channel_id=1, source_target_pairs={{0,1},{1,2},{2,3},{3,4},{4,5},{5,6},{6,7},{8,9},{9,10},{10,11},{11... | collective-permute-start | bytes 104456 | tf_op jit(solution)/shard_map/ppermute | solution.py:14
  51.3 2.7 %collective-permute-start.7 = (bf16[34,1,512]{2,1,0:T(2,128)(2,1)S(1)}, bf16[34,1,512]{2,1,0:T(2,128)(2,1)S(1)}, u32[]{:S(2)}, u32[]{:S(2)}) collective-permute-start(bf16[34,1,512]{2,1,0:T(2,128)(2,1)S(1)} %get-tuple-element.30), channel_id=1, source_target_pairs={{1,0},{2,1},{3,2},{4,3},{5,4},{6,5},{7,6},{9,8},{10,9},{11,10},{12... | collective-permute-start | bytes 104456 | tf_op jit(solution)/shard_map/ppermute | solution.py:15
  54.1 0.4 fusion.29
  54.5 4.5 %collective-permute-done.7 = bf16[34,1,512]{2,1,0:T(2,128)(2,1)S(1)} collective-permute-done((bf16[34,1,512]{2,1,0:T(2,128)(2,1)S(1)}, bf16[34,1,512]{2,1,0:T(2,128)(2,1)S(1)}, u32[]{:S(2)}, u32[]{:S(2)}) %collective-permute-start.7) | collective-permute-done | bytes 34848 | tf_op jit(solution)/shard_map/ppermute | solution.py:15
  59.0 0.5 maximum_maximum_fusion.1
  59.5 1.6 %multiply_convert_fusion.1 = bf16[32,16,512]{2,1,0:T(8,128)(2,1)S(1)} fusion(bf16[32,16,512]{2,1,0:T(8,128)(2,1)S(1)} %add_convert_fusion, bf16[34,17,512]{2,1,0:T(8,128)(2,1)S(1)} %get-tuple-element.28, bf16[1,16,512]{2,1,0:T(8,128)(2,1)S(1)} %collective-permute-done.5, bf16[34,17,512]{2,1,0:T(8,128)(2,1)S(1)} %get-tuple-element.27, ...), kind=kLoop, calls=%fused_computation.46 | loop fusion | flops 7864320 | bytes 4245504 | tf_op jit(solution)/shard_map/convert_element_type | solution.py:48
  61.1 0.6 multiply_convert_fusion
  61.7 0.5 fusion.77
  62.3 0.2 multiply_reduce_fusion
  62.5 0.2 divide_convert_fusion
  62.8 1.0 convolution_convert_fusion
  63.7 0.0 all-gather.2.cloned.1.call-update
  63.7 47.0 %all-gather.2.cloned.1.call-done = bf16[8,32,16,128]{3,2,1,0:T(8,128)(2,1)} async-done(((bf16[1,32,16,128]{3,2,1,0:T(8,128)(2,1)}), bf16[8,32,16,128]{3,2,1,0:T(8,128)(2,1)}) %all-gather.2.cloned.1.call-update) | async-done | bytes 1048592 | tf_op jit(solution)/shard_map/all_gather | solution.py:61
  110.7 1.4 %convert_element_type.164 = f32[8,32,16,128]{3,2,1,0:T(8,128)S(1)} convert(bf16[8,32,16,128]{3,2,1,0:T(8,128)(2,1)} %all-gather.2.cloned.1.call-done) | non-fusion elementwise | flops 524288 | bytes 3145728 | tf_op jit(solution)/shard_map/convert_element_type | solution.py:61
  112.1 0.1 slice_bitcast_fusion
  112.3 1.1 copy-done.2
  113.4 1.7 %fusion.3 = (f32[32,16,128]{2,1,0:T(8,128)S(1)}, f32[32,16,128]{2,1,0:T(8,128)S(1)}, f32[32,16,128]{2,1,0:T(8,128)S(1)}, f32[32,16,128]{2,1,0:T(8,128)S(1)}, f32...) fusion(bf16[8,32,16,128]{3,2,1,0:T(8,128)(2,1)S(1)} %copy-done., ...), kind=kLoop, calls=%fused_computation.11 | loop fusion | flops 12582912 | bytes 5242880 | tf_op jit(solution)/shard_map/reduce_sum | solution.py:68
  115.1 1.0 fusion.50
  (26 shorter events, 0.1 us)
Async XLA Ops:
  7.2 55.6 %copy-start = (bf16[512,128]{1,0:T(8,128)(2,1)S(1)}, bf16[512,128]{1,0:T(8,128)(2,1)}, u32[]{:S(2)}) copy-start(bf16[512,128]{1,0:T(8,128)(2,1)} %param.19) | copy-start | bytes 393220
  7.2 9.2 %copy-start.9 = (f32[1,32]{1,0:T(1,128)S(1)}, f32[1,32]{1,0:T(1,128)}, u32[]{:S(2)}) copy-start(f32[1,32]{1,0:T(1,128)} %param.11) | copy-start | bytes 388
  7.2 9.2 %copy-start.6 = (f32[2,32,512]{2,1,0:T(8,128)S(1)}, f32[2,32,512]{2,1,0:T(8,128)}, u32[]{:S(2)}) copy-start(f32[2,32,512]{2,1,0:T(8,128)} %param.17) | copy-start | bytes 393220
  7.2 9.3 %copy-start.7 = (f32[2,32,512]{2,1,0:T(8,128)S(1)}, f32[2,32,512]{2,1,0:T(8,128)}, u32[]{:S(2)}) copy-start(f32[2,32,512]{2,1,0:T(8,128)} %param.18) | copy-start | bytes 393220
  7.2 9.5 %copy-start.1 = (bf16[1,32,16,512]{3,2,1,0:T(8,128)(2,1)S(1)}, bf16[1,32,16,512]{3,2,1,0:T(8,128)(2,1)}, u32[]{:S(2)}) copy-start(bf16[1,32,16,512]{3,2,1,0:T(8,128)(2,1)} %param.10) | copy-start | bytes 1572868
  7.2 9.8 %copy-start.4 = (bf16[2,512,512]{2,1,0:T(8,128)(2,1)S(1)}, bf16[2,512,512]{2,1,0:T(8,128)(2,1)}, u32[]{:S(2)}) copy-start(bf16[2,512,512]{2,1,0:T(8,128)(2,1)} %param.14) | copy-start | bytes 3145732
  7.2 103.5 %all-gather.2.cloned.1.call-start = ((), (), s32[]{:S(2)}) async-start(), calls=%async_computation | async-start | bytes 1179648 | tf_op jit(solution)/shard_map/all_gather | solution.py:61
  13.3 15.4 %copy-start.8 = (s32[32,16,6]{0,1,2:T(8,128)S(1)}, s32[32,16,6]{0,1,2:T(8,128)}, u32[]{:S(2)}) copy-start(s32[32,16,6]{0,1,2:T(8,128)} %param.12) | copy-start | bytes 36868
  13.3 4.1 %collective-permute-start = (bf16[1,16,512]{2,1,0:T(8,128)(2,1)S(1)}, bf16[1,16,512]{2,1,0:T(8,128)(2,1)S(1)}, u32[]{:S(2)}, u32[]{:S(2)}) collective-permute-start(bf16[1,16,512]{2,1,0:T(8,128)(2,1)S(1)} %get-tuple-element.37), channel_id=1, source_target_pairs={{0,8},{8,16},{16,24},{24,32},{32,40},{40,48},{48,56},{1,9},{9,17},... | collective-permute-start | bytes 49160 | tf_op jit(solution)/shard_map/ppermute | solution.py:14
  15.1 7.0 %collective-permute-start.1 = (bf16[1,16,512]{2,1,0:T(8,128)(2,1)S(1)}, bf16[1,16,512]{2,1,0:T(8,128)(2,1)S(1)}, u32[]{:S(2)}, u32[]{:S(2)}) collective-permute-start(bf16[1,16,512]{2,1,0:T(8,128)(2,1)S(1)} %get-tuple-element.38), channel_id=1, source_target_pairs={{8,0},{16,8},{24,16},{32,24},{40,32},{48,40},{56,48},{9,1},{17,9},... | collective-permute-start | bytes 49160 | tf_op jit(solution)/shard_map/ppermute | solution.py:15
  22.9 6.6 %collective-permute-start.2 = (bf16[34,1,512]{2,1,0:T(2,128)(2,1)}, bf16[34,1,512]{2,1,0:T(2,128)(2,1)S(1)}, u32[]{:S(2)}, u32[]{:S(2)}) collective-permute-start(bf16[34,1,512]{2,1,0:T(2,128)(2,1)} %get-tuple-element.33), channel_id=1, source_target_pairs={{0,1},{1,2},{2,3},{3,4},{4,5},{5,6},{6,7},{8,9},{9,10},{10,11},{11... | collective-permute-start | bytes 104456 | tf_op jit(solution)/shard_map/ppermute | solution.py:14
  26.3 6.5 %collective-permute-start.3 = (bf16[34,1,512]{2,1,0:T(2,128)(2,1)}, bf16[34,1,512]{2,1,0:T(2,128)(2,1)}, u32[]{:S(2)}, u32[]{:S(2)}) collective-permute-start(bf16[34,1,512]{2,1,0:T(2,128)(2,1)} %get-tuple-element.34), channel_id=1, source_target_pairs={{1,0},{2,1},{3,2},{4,3},{5,4},{6,5},{7,6},{9,8},{10,9},{11,10},{12... | collective-permute-start | bytes 104456 | tf_op jit(solution)/shard_map/ppermute | solution.py:15
  34.2 1.6 %copy-start.10 = (bf16[2,512,512]{2,1,0:T(8,128)(2,1)S(1)}, bf16[2,512,512]{2,1,0:T(8,128)(2,1)}, u32[]{:S(2)}) copy-start(bf16[2,512,512]{2,1,0:T(8,128)(2,1)} %param.15) | copy-start | bytes 3145732
  35.8 1.2 copy-start.3
  38.1 5.2 %collective-permute-start.4 = (bf16[1,16,512]{2,1,0:T(8,128)(2,1)S(1)}, bf16[1,16,512]{2,1,0:T(8,128)(2,1)S(1)}, u32[]{:S(2)}, u32[]{:S(2)}) collective-permute-start(bf16[1,16,512]{2,1,0:T(8,128)(2,1)S(1)} %get-tuple-element.35), channel_id=1, source_target_pairs={{0,8},{8,16},{16,24},{24,32},{32,40},{40,48},{48,56},{1,9},{9,17},... | collective-permute-start | bytes 49160 | tf_op jit(solution)/shard_map/ppermute | solution.py:14
  42.0 6.1 %collective-permute-start.5 = (bf16[1,16,512]{2,1,0:T(8,128)(2,1)S(1)}, bf16[1,16,512]{2,1,0:T(8,128)(2,1)S(1)}, u32[]{:S(2)}, u32[]{:S(2)}) collective-permute-start(bf16[1,16,512]{2,1,0:T(8,128)(2,1)S(1)} %get-tuple-element.36), channel_id=1, source_target_pairs={{8,0},{16,8},{24,16},{32,24},{40,32},{48,40},{56,48},{9,1},{17,9},... | collective-permute-start | bytes 49160 | tf_op jit(solution)/shard_map/ppermute | solution.py:15
  48.2 6.3 %collective-permute-start.6 = (bf16[34,1,512]{2,1,0:T(2,128)(2,1)S(1)}, bf16[34,1,512]{2,1,0:T(2,128)(2,1)S(1)}, u32[]{:S(2)}, u32[]{:S(2)}) collective-permute-start(bf16[34,1,512]{2,1,0:T(2,128)(2,1)S(1)} %get-tuple-element.29), channel_id=1, source_target_pairs={{0,1},{1,2},{2,3},{3,4},{4,5},{5,6},{6,7},{8,9},{9,10},{10,11},{11... | collective-permute-start | bytes 104456 | tf_op jit(solution)/shard_map/ppermute | solution.py:14
  51.3 7.7 %collective-permute-start.7 = (bf16[34,1,512]{2,1,0:T(2,128)(2,1)S(1)}, bf16[34,1,512]{2,1,0:T(2,128)(2,1)S(1)}, u32[]{:S(2)}, u32[]{:S(2)}) collective-permute-start(bf16[34,1,512]{2,1,0:T(2,128)(2,1)S(1)} %get-tuple-element.30), channel_id=1, source_target_pairs={{1,0},{2,1},{3,2},{4,3},{5,4},{6,5},{7,6},{9,8},{10,9},{11,10},{12... | collective-permute-start | bytes 104456 | tf_op jit(solution)/shard_map/ppermute | solution.py:15
  112.1 1.2 copy-start.2
  113.4 1.7 %copy-start.5 = (bf16[32,16,128]{2,1,0:T(8,128)(2,1)S(1)}, bf16[32,16,128]{2,1,0:T(8,128)(2,1)}, u32[]{:S(2)}) copy-start(bf16[32,16,128]{2,1,0:T(8,128)(2,1)} %param.13) | copy-start | bytes 393220
Sparse Core Ops, SparseCore 0:
  63.9 46.8 all-gather.1
where the time goes:
time: 124 us; the launch traced here: 123 us
  waiting for transfers between devices  64.3 us (52%)
  starting transfers between devices  19.9 us (16%)
  other arithmetic  15.2 us (12%)
  between operations  14.5 us (12%)
  matrix products  6.49 us (5%)
  local copies, waits for them, and re-layouts  2.56 us (2%)
    all_gather x1, waiting for transfers between devices, local(): lax.all_gather(predicted_grid, 'member', axis=0, tiled=True)  47 us
    ppermute x4, waiting for transfers between devices, padded_2(): after = lax.ppermute(initial, axis, down)  17.3 us
    ppermute x4, starting transfers between devices, padded_2(): before = lax.ppermute(last, axis, up)  12.1 us
    ppermute x4, starting transfers between devices, padded_2(): after = lax.ppermute(initial, axis, down)  7.77 us
    convert_element_type x2, other arithmetic, local(): mixed = (total / degree).astype(jnp.bfloat16)  3.24 us
  transfers between devices with their start and end apart: 9, of which 5 were waited for; matrix products, arithmetic and copies ran while one was open for 2% of the time, Pallas kernels for 0%

commit v1 on v0

--- a/solution.py
+++ b/solution.py
@@ -58,17 +58,23 @@
     truth = target.astype(jnp.float32)
     ensemble_entries = lax.axis_size("member")
     denom = 2.0 * ensemble_entries * (ensemble_entries - 1)
-    ensemble_wide_total = lax.all_gather(predicted_grid, "member", axis=0, tiled=True).astype(
-        jnp.float32
-    )
+    variables = raveled_outputs.shape[-1]
+    share = rows // ensemble_entries
+    member = lax.axis_index("member")
+    mine = lax.all_to_all(
+        raveled_outputs.reshape(ensemble_entries, share, variables), "member", 0, 0
+    ).astype(jnp.float32)
+    truth = lax.dynamic_slice_in_dim(truth.reshape(rows, variables), member * share, share, 0)
     skill = jnp.zeros(truth.shape, jnp.float32)
     spread = jnp.zeros(truth.shape, jnp.float32)
     for first in range(ensemble_entries):
-        skill = skill + jnp.abs(ensemble_wide_total[first] - truth)
-        spread = spread + jnp.sum(
-            jnp.abs(ensemble_wide_total[first][None] - ensemble_wide_total), axis=0
-        )
-    ranked_probability_score = skill / ensemble_entries - spread / denom
+        skill = skill + jnp.abs(mine[first] - truth)
+        for second in range(first):
+            spread = spread + jnp.abs(mine[first] - mine[second])
+    score = (skill / ensemble_entries - 2.0 * spread / denom).astype(jnp.bfloat16)
+    copies = jnp.broadcast_to(score[None], (ensemble_entries,) + score.shape)
+    scores = lax.all_to_all(copies, "member", 0, 0)
+    ranked_probability_score = scores.astype(jnp.float32).reshape(target.shape)
     return (predicted_grid, ranked_probability_score)
 
 

time: 124 us -> 88.2 us (0.71)
  the two profiles are of different devices: /device:TPU:2 before, /device:TPU:135 now
where the time goes in v1:
time: 88.2 us; the launch traced here: 87.6 us
  starting transfers between devices  33 us (37%)
  waiting for transfers between devices  25.1 us (28%)
  other arithmetic  11.7 us (13%)
  blocking collectives  10.7 us (12%)
  matrix products  4.65 us (5%)
  local copies, waits for them, and re-layouts  1.36 us (2%)
  between operations  1.05 us (1%)
    ppermute x4, waiting for transfers between devices, padded_2(): after = lax.ppermute(initial, axis, down)  17.2 us
    ppermute x4, starting transfers between devices, padded_2(): before = lax.ppermute(last, axis, up)  16.7 us
    all_to_all x1, blocking collectives, local(): scores = lax.all_to_all(copies, 'member', 0, 0)  10.7 us
    ppermute x4, starting transfers between devices, padded_2(): after = lax.ppermute(initial, axis, down)  9.47 us
    all_to_all x1, waiting for transfers between devices, local(): lax.all_to_all(raveled_outputs.reshape(ensemble_entries, share, variables...  7.93 us
    all_to_all x1, starting transfers between devices, local(): lax.all_to_all(raveled_outputs.reshape(ensemble_entries, share, variables...  6.82 us
    convert_element_type x2, other arithmetic, local(): mixed = (total / degree).astype(jnp.bfloat16)  3.24 us
    reduce_sum x3, other arithmetic, norm_rows(): var = jnp.mean((x - mean) ** 2, axis=-1, keepdims=True)  1.81 us
  transfers between devices with their start and end apart: 9, of which 5 were waited for; matrix products, arithmetic and copies ran while one was open for 2% of the time, Pallas kernels for 0%

profile of v1, /device:TPU:135, one launch (start us, length us, event | category | flops | bytes accessed | tf_op | source)
XLA Modules:
  0.0 87.6 jit_solution(97993554533513524)
XLA Ops:
  0.6 0.0 copy-start
  0.6 0.0 copy-start.1
  0.7 0.0 copy-start.7
  0.7 0.0 copy-start.4
  0.7 0.0 copy-start.5
  0.7 1.3 %convert_reduce_fusion = f32[32,16]{1,0:T(8,128)S(1)} fusion(bf16[1,32,16,512]{3,2,1,0:T(8,128)(2,1)} %param.10), kind=kLoop, calls=%fused_computation.1 | loop fusion | flops 523776 | bytes 526336 | tf_op jit(solution)/shard_map/reduce_sum | solution.py:21
  2.0 1.3 %fusion.3 = f32[32,16]{1,0:T(8,128)S(1)} fusion(bf16[1,32,16,512]{3,2,1,0:T(8,128)(2,1)} %param.10, f32[32,16]{1,0:T(8,128)S(1)} %broadcast_multiply_fusion.2), kind=kLoop, calls=%fused_computation.11 | loop fusion | flops 1048064 | bytes 528384 | tf_op jit(solution)/shard_map/reduce_sum | solution.py:22
  3.3 0.1 fusion.31
  3.5 0.2 fusion.29
  3.6 0.3 fusion.6
  3.9 7.7 %collective-permute-start = (bf16[1,16,512]{2,1,0:T(8,128)(2,1)S(1)}, bf16[1,16,512]{2,1,0:T(8,128)(2,1)S(1)}, u32[]{:S(2)}, u32[]{:S(2)}) collective-permute-start(bf16[1,16,512]{2,1,0:T(8,128)(2,1)S(1)} %get-tuple-element.21), channel_id=1, source_target_pairs={{0,8},{8,16},{16,24},{24,32},{32,40},{40,48},{48,56},{1,9},{9,17},... | collective-permute-start | bytes 49160 | tf_op jit(solution)/shard_map/ppermute | solution.py:14
  11.7 1.9 %collective-permute-start.1 = (bf16[1,16,512]{2,1,0:T(8,128)(2,1)S(1)}, bf16[1,16,512]{2,1,0:T(8,128)(2,1)S(1)}, u32[]{:S(2)}, u32[]{:S(2)}) collective-permute-start(bf16[1,16,512]{2,1,0:T(8,128)(2,1)S(1)} %get-tuple-element.22), channel_id=1, source_target_pairs={{8,0},{16,8},{24,16},{32,24},{40,32},{48,40},{56,48},{9,1},{17,9},... | collective-permute-start | bytes 49160 | tf_op jit(solution)/shard_map/ppermute | solution.py:15
  13.6 0.3 fusion.10
  13.9 0.1 fusion.27
  14.0 0.2 fusion.25
  14.2 0.4 fusion.17
  14.6 0.0 collective-permute-done
  14.6 4.2 %collective-permute-done.1 = bf16[1,16,512]{2,1,0:T(8,128)(2,1)S(1)} collective-permute-done((bf16[1,16,512]{2,1,0:T(8,128)(2,1)S(1)}, bf16[1,16,512]{2,1,0:T(8,128)(2,1)S(1)}, u32[]{:S(2)}, u32[]{:S(2)}) %collective-permute-start.1) | collective-permute-done | bytes 16416 | tf_op jit(solution)/shard_map/ppermute | solution.py:15
  18.8 0.8 pad_maximum_fusion.11
  19.6 3.0 %collective-permute-start.2 = (bf16[34,1,512]{2,1,0:T(2,128)(2,1)}, bf16[34,1,512]{2,1,0:T(2,128)(2,1)S(1)}, u32[]{:S(2)}, u32[]{:S(2)}) collective-permute-start(bf16[34,1,512]{2,1,0:T(2,128)(2,1)} %get-tuple-element.17), channel_id=1, source_target_pairs={{0,1},{1,2},{2,3},{3,4},{4,5},{5,6},{6,7},{8,9},{9,10},{10,11},{11... | collective-permute-start | bytes 104456 | tf_op jit(solution)/shard_map/ppermute | solution.py:14
  22.6 2.3 %collective-permute-start.3 = (bf16[34,1,512]{2,1,0:T(2,128)(2,1)}, bf16[34,1,512]{2,1,0:T(2,128)(2,1)}, u32[]{:S(2)}, u32[]{:S(2)}) collective-permute-start(bf16[34,1,512]{2,1,0:T(2,128)(2,1)} %get-tuple-element.18), channel_id=1, source_target_pairs={{1,0},{2,1},{3,2},{4,3},{5,4},{6,5},{7,6},{9,8},{10,9},{11,10},{12... | collective-permute-start | bytes 104456 | tf_op jit(solution)/shard_map/ppermute | solution.py:15
  24.9 0.1 convert_reduce_fusion.9
  25.0 0.1 copy.12
  25.0 0.1 copy.13
  25.1 0.1 copy.14
  25.2 0.1 copy.15
  25.3 0.1 copy.16
  25.3 0.1 copy.17
  25.4 0.1 copy.18
  25.5 0.1 copy.19
  25.6 0.1 copy.20
  25.6 0.0 collective-permute-done.2
  25.6 4.5 %collective-permute-done.3 = bf16[34,1,512]{2,1,0:T(2,128)(2,1)} collective-permute-done((bf16[34,1,512]{2,1,0:T(2,128)(2,1)}, bf16[34,1,512]{2,1,0:T(2,128)(2,1)}, u32[]{:S(2)}, u32[]{:S(2)}) %collective-permute-start.3) | collective-permute-done | bytes 34848 | tf_op jit(solution)/shard_map/ppermute | solution.py:15
  30.1 1.3 %maximum_maximum_fusion = (bf16[34,17,512]{2,1,0:T(8,128)(2,1)S(1)}, bf16[34,17,512]{2,1,0:T(8,128)(2,1)S(1)}) fusion(bf16[1,16,512]{2,1,0:T(8,128)(2,1)S(1)} %collective-permute-done.1, bf16[32,16,512]{2,1,0:T(8,128)(2,1)S(1)} %fusion.6, bf16[1,16,512]{2,1,0:T(8,128)(2,1)S(1)} %collective-permute-done, bf16[34,1,512]{2,1,0:T(2,128)(2,1)S(1)} %collective-permute-done.2, ...), kind=kLoop, calls=%fused_computation.27 | loop fusion | flops 4734976 | bytes 1810432 | tf_op jit(solution)/shard_map/concatenate | solution.py:16
  31.4 0.0 copy-start.8
  31.4 1.6 %multiply_convert_fusion.3 = bf16[32,16,512]{2,1,0:T(8,128)(2,1)S(1)} fusion(bf16[32,16,512]{2,1,0:T(8,128)(2,1)S(1)} %fusion.6, bf16[34,17,512]{2,1,0:T(8,128)(2,1)S(1)} %get-tuple-element.16, bf16[1,16,512]{2,1,0:T(8,128)(2,1)S(1)} %collective-permute-done.1, bf16[34,17,512]{2,1,0:T(8,128)(2,1)S(1)} %get-tuple-element.15, ...), kind=kLoop, calls=%fused_computation.26 | loop fusion | flops 7864320 | bytes 4245504 | tf_op jit(solution)/shard_map/convert_element_type | solution.py:48
  33.1 0.0 copy-start.2
  33.1 0.6 multiply_convert_fusion.2
  33.7 0.6 copy-done.2
  34.3 0.5 fusion.61
  34.8 0.3 multiply_reduce_fusion.1
  35.1 0.2 add_convert_fusion
  35.4 4.1 %collective-permute-start.4 = (bf16[1,16,512]{2,1,0:T(8,128)(2,1)S(1)}, bf16[1,16,512]{2,1,0:T(8,128)(2,1)S(1)}, u32[]{:S(2)}, u32[]{:S(2)}) collective-permute-start(bf16[1,16,512]{2,1,0:T(8,128)(2,1)S(1)} %get-tuple-element.19), channel_id=1, source_target_pairs={{0,8},{8,16},{16,24},{24,32},{32,40},{40,48},{48,56},{1,9},{9,17},... | collective-permute-start | bytes 49160 | tf_op jit(solution)/shard_map/ppermute | solution.py:14
  39.5 1.9 %collective-permute-start.5 = (bf16[1,16,512]{2,1,0:T(8,128)(2,1)S(1)}, bf16[1,16,512]{2,1,0:T(8,128)(2,1)S(1)}, u32[]{:S(2)}, u32[]{:S(2)}) collective-permute-start(bf16[1,16,512]{2,1,0:T(8,128)(2,1)S(1)} %get-tuple-element.20), channel_id=1, source_target_pairs={{8,0},{16,8},{24,16},{32,24},{40,32},{48,40},{56,48},{9,1},{17,9},... | collective-permute-start | bytes 49160 | tf_op jit(solution)/shard_map/ppermute | solution.py:15
  41.4 0.0 collective-permute-done.4
  41.4 5.2 %collective-permute-done.5 = bf16[1,16,512]{2,1,0:T(8,128)(2,1)S(1)} collective-permute-done((bf16[1,16,512]{2,1,0:T(8,128)(2,1)S(1)}, bf16[1,16,512]{2,1,0:T(8,128)(2,1)S(1)}, u32[]{:S(2)}, u32[]{:S(2)}) %collective-permute-start.5) | collective-permute-done | bytes 16416 | tf_op jit(solution)/shard_map/ppermute | solution.py:15
  46.6 0.1 pad_maximum_fusion.8
  46.8 1.9 %collective-permute-start.6 = (bf16[34,1,512]{2,1,0:T(2,128)(2,1)S(1)}, bf16[34,1,512]{2,1,0:T(2,128)(2,1)S(1)}, u32[]{:S(2)}, u32[]{:S(2)}) collective-permute-start(bf16[34,1,512]{2,1,0:T(2,128)(2,1)S(1)} %get-tuple-element.13), channel_id=1, source_target_pairs={{0,1},{1,2},{2,3},{3,4},{4,5},{5,6},{6,7},{8,9},{9,10},{10,11},{11... | collective-permute-start | bytes 104456 | tf_op jit(solution)/shard_map/ppermute | solution.py:14
  48.7 3.4 %collective-permute-start.7 = (bf16[34,1,512]{2,1,0:T(2,128)(2,1)S(1)}, bf16[34,1,512]{2,1,0:T(2,128)(2,1)S(1)}, u32[]{:S(2)}, u32[]{:S(2)}) collective-permute-start(bf16[34,1,512]{2,1,0:T(2,128)(2,1)S(1)} %get-tuple-element.14), channel_id=1, source_target_pairs={{1,0},{2,1},{3,2},{4,3},{5,4},{6,5},{7,6},{9,8},{10,9},{11,10},{12... | collective-permute-start | bytes 104456 | tf_op jit(solution)/shard_map/ppermute | solution.py:15
  52.1 0.4 fusion.13
  52.5 0.0 collective-permute-done.6
  52.5 3.3 %collective-permute-done.7 = bf16[34,1,512]{2,1,0:T(2,128)(2,1)S(1)} collective-permute-done((bf16[34,1,512]{2,1,0:T(2,128)(2,1)S(1)}, bf16[34,1,512]{2,1,0:T(2,128)(2,1)S(1)}, u32[]{:S(2)}, u32[]{:S(2)}) %collective-permute-start.7) | collective-permute-done | bytes 34848 | tf_op jit(solution)/shard_map/ppermute | solution.py:15
  55.9 0.5 maximum_maximum_fusion.1
  56.3 1.6 %multiply_convert_fusion.1 = bf16[32,16,512]{2,1,0:T(8,128)(2,1)S(1)} fusion(bf16[32,16,512]{2,1,0:T(8,128)(2,1)S(1)} %add_convert_fusion, bf16[34,17,512]{2,1,0:T(8,128)(2,1)S(1)} %get-tuple-element.12, bf16[1,16,512]{2,1,0:T(8,128)(2,1)S(1)} %collective-permute-done.5, bf16[34,17,512]{2,1,0:T(8,128)(2,1)S(1)} %get-tuple-element.11, ...), kind=kLoop, calls=%fused_computation.22 | loop fusion | flops 7864320 | bytes 4245504 | tf_op jit(solution)/shard_map/convert_element_type | solution.py:48
  58.0 0.6 multiply_convert_fusion
  58.6 0.5 fusion.62
  59.1 0.2 multiply_reduce_fusion
  59.4 0.2 divide_convert_fusion
  59.6 1.0 %convolution_convert_fusion = bf16[512,128]{1,0:T(8,128)(2,1)} fusion(bf16[512,512]{1,0:T(8,128)(2,1)S(1)} %bitcast.125, bf16[512,128]{1,0:T(8,128)(2,1)S(1)} %copy-done), kind=kOutput, calls=%fused_computation.10 | convolution fusion | flops 67174400 | bytes 786432 | tf_op jit(solution)/shard_map/dot_general | solution.py:56
  60.5 6.8 %all-to-all-start = ((bf16[8,64,128]{2,1,0:T(8,128)(2,1)}), bf16[8,64,128]{2,1,0:T(8,128)(2,1)S(1)}, u32[]{:S(2)}, u32[]{:S(2)}) async-start(bf16[8,64,128]{2,1,0:T(8,128)(2,1)} %bitcast.30), calls=%async_computation | async-start | bytes 262144 | tf_op jit(solution)/shard_map/all_to_all | solution.py:64
  67.4 7.9 %all-to-all-done = bf16[8,64,128]{2,1,0:T(8,128)(2,1)S(1)} async-done(((bf16[8,64,128]{2,1,0:T(8,128)(2,1)}), bf16[8,64,128]{2,1,0:T(8,128)(2,1)S(1)}, u32[]{:S(2)}, u32[]{:S(2)}) %all-to-all-start) | async-done | bytes 131104 | tf_op jit(solution)/shard_map/all_to_all | solution.py:64
  75.3 0.9 fusion.41
  76.2 10.7 %all_to_all.10 = bf16[8,64,128]{2,1,0:T(8,128)(2,1)S(1)} all-to-all(bf16[8,64,128]{2,1,0:T(8,128)(2,1)S(1)} %broadcast_in_dim.2), channel_id=1, replica_groups=mesh['member'=8,'sx'=8,'sy'=8] {'member'}, dimensions={0} | all-to-all | bytes 262144 | tf_op jit(solution)/shard_map/all_to_all | solution.py:76
  86.9 0.7 convert.3
  (22 shorter events, 0.1 us)
Async XLA Ops:
  0.6 59.0 %copy-start = (bf16[512,128]{1,0:T(8,128)(2,1)S(1)}, bf16[512,128]{1,0:T(8,128)(2,1)}, u32[]{:S(2)}) copy-start(bf16[512,128]{1,0:T(8,128)(2,1)} %param.19) | copy-start | bytes 393220
  0.6 3.0 %copy-start.1 = (bf16[1,32,16,512]{3,2,1,0:T(8,128)(2,1)S(1)}, bf16[1,32,16,512]{3,2,1,0:T(8,128)(2,1)}, u32[]{:S(2)}) copy-start(bf16[1,32,16,512]{3,2,1,0:T(8,128)(2,1)} %param.10) | copy-start | bytes 1572868
  0.7 2.6 %copy-start.7 = (f32[1,32]{1,0:T(1,128)S(1)}, f32[1,32]{1,0:T(1,128)}, u32[]{:S(2)}) copy-start(f32[1,32]{1,0:T(1,128)} %param.11) | copy-start | bytes 388
  0.7 2.6 %copy-start.4 = (f32[2,32,512]{2,1,0:T(8,128)S(1)}, f32[2,32,512]{2,1,0:T(8,128)}, u32[]{:S(2)}) copy-start(f32[2,32,512]{2,1,0:T(8,128)} %param.17) | copy-start | bytes 393220
  0.7 2.8 %copy-start.5 = (f32[2,32,512]{2,1,0:T(8,128)S(1)}, f32[2,32,512]{2,1,0:T(8,128)}, u32[]{:S(2)}) copy-start(f32[2,32,512]{2,1,0:T(8,128)} %param.18) | copy-start | bytes 393220
  3.6 10.5 %copy-start.3 = (bf16[2,512,512]{2,1,0:T(8,128)(2,1)S(1)}, bf16[2,512,512]{2,1,0:T(8,128)(2,1)}, u32[]{:S(2)}) copy-start(bf16[2,512,512]{2,1,0:T(8,128)(2,1)} %param.14) | copy-start | bytes 3145732
  3.9 10.7 %collective-permute-start = (bf16[1,16,512]{2,1,0:T(8,128)(2,1)S(1)}, bf16[1,16,512]{2,1,0:T(8,128)(2,1)S(1)}, u32[]{:S(2)}, u32[]{:S(2)}) collective-permute-start(bf16[1,16,512]{2,1,0:T(8,128)(2,1)S(1)} %get-tuple-element.21), channel_id=1, source_target_pairs={{0,8},{8,16},{16,24},{24,32},{32,40},{40,48},{48,56},{1,9},{9,17},... | collective-permute-start | bytes 49160 | tf_op jit(solution)/shard_map/ppermute | solution.py:14
  11.7 7.2 %collective-permute-start.1 = (bf16[1,16,512]{2,1,0:T(8,128)(2,1)S(1)}, bf16[1,16,512]{2,1,0:T(8,128)(2,1)S(1)}, u32[]{:S(2)}, u32[]{:S(2)}) collective-permute-start(bf16[1,16,512]{2,1,0:T(8,128)(2,1)S(1)} %get-tuple-element.22), channel_id=1, source_target_pairs={{8,0},{16,8},{24,16},{32,24},{40,32},{48,40},{56,48},{9,1},{17,9},... | collective-permute-start | bytes 49160 | tf_op jit(solution)/shard_map/ppermute | solution.py:15
  14.2 10.7 %copy-start.6 = (s32[32,16,6]{0,1,2:T(8,128)S(1)}, s32[32,16,6]{0,1,2:T(8,128)}, u32[]{:S(2)}) copy-start(s32[32,16,6]{0,1,2:T(8,128)} %param.12) | copy-start | bytes 36868
  19.6 6.0 %collective-permute-start.2 = (bf16[34,1,512]{2,1,0:T(2,128)(2,1)}, bf16[34,1,512]{2,1,0:T(2,128)(2,1)S(1)}, u32[]{:S(2)}, u32[]{:S(2)}) collective-permute-start(bf16[34,1,512]{2,1,0:T(2,128)(2,1)} %get-tuple-element.17), channel_id=1, source_target_pairs={{0,1},{1,2},{2,3},{3,4},{4,5},{5,6},{6,7},{8,9},{9,10},{10,11},{11... | collective-permute-start | bytes 104456 | tf_op jit(solution)/shard_map/ppermute | solution.py:14
  22.6 7.5 %collective-permute-start.3 = (bf16[34,1,512]{2,1,0:T(2,128)(2,1)}, bf16[34,1,512]{2,1,0:T(2,128)(2,1)}, u32[]{:S(2)}, u32[]{:S(2)}) collective-permute-start(bf16[34,1,512]{2,1,0:T(2,128)(2,1)} %get-tuple-element.18), channel_id=1, source_target_pairs={{1,0},{2,1},{3,2},{4,3},{5,4},{6,5},{7,6},{9,8},{10,9},{11,10},{12... | collective-permute-start | bytes 104456 | tf_op jit(solution)/shard_map/ppermute | solution.py:15
  31.4 1.6 %copy-start.8 = (bf16[2,512,512]{2,1,0:T(8,128)(2,1)S(1)}, bf16[2,512,512]{2,1,0:T(8,128)(2,1)}, u32[]{:S(2)}) copy-start(bf16[2,512,512]{2,1,0:T(8,128)(2,1)} %param.15) | copy-start | bytes 3145732
  33.1 1.2 %copy-start.2 = (bf16[2,512,512]{2,1,0:T(8,128)(2,1)S(1)}, bf16[2,512,512]{2,1,0:T(8,128)(2,1)}, u32[]{:S(2)}) copy-start(bf16[2,512,512]{2,1,0:T(8,128)(2,1)} %param.16) | copy-start | bytes 3145732
  35.4 6.0 %collective-permute-start.4 = (bf16[1,16,512]{2,1,0:T(8,128)(2,1)S(1)}, bf16[1,16,512]{2,1,0:T(8,128)(2,1)S(1)}, u32[]{:S(2)}, u32[]{:S(2)}) collective-permute-start(bf16[1,16,512]{2,1,0:T(8,128)(2,1)S(1)} %get-tuple-element.19), channel_id=1, source_target_pairs={{0,8},{8,16},{16,24},{24,32},{32,40},{40,48},{48,56},{1,9},{9,17},... | collective-permute-start | bytes 49160 | tf_op jit(solution)/shard_map/ppermute | solution.py:14
  39.5 7.2 %collective-permute-start.5 = (bf16[1,16,512]{2,1,0:T(8,128)(2,1)S(1)}, bf16[1,16,512]{2,1,0:T(8,128)(2,1)S(1)}, u32[]{:S(2)}, u32[]{:S(2)}) collective-permute-start(bf16[1,16,512]{2,1,0:T(8,128)(2,1)S(1)} %get-tuple-element.20), channel_id=1, source_target_pairs={{8,0},{16,8},{24,16},{32,24},{40,32},{48,40},{56,48},{9,1},{17,9},... | collective-permute-start | bytes 49160 | tf_op jit(solution)/shard_map/ppermute | solution.py:15
  46.8 5.7 %collective-permute-start.6 = (bf16[34,1,512]{2,1,0:T(2,128)(2,1)S(1)}, bf16[34,1,512]{2,1,0:T(2,128)(2,1)S(1)}, u32[]{:S(2)}, u32[]{:S(2)}) collective-permute-start(bf16[34,1,512]{2,1,0:T(2,128)(2,1)S(1)} %get-tuple-element.13), channel_id=1, source_target_pairs={{0,1},{1,2},{2,3},{3,4},{4,5},{5,6},{6,7},{8,9},{9,10},{10,11},{11... | collective-permute-start | bytes 104456 | tf_op jit(solution)/shard_map/ppermute | solution.py:14
  48.7 7.2 %collective-permute-start.7 = (bf16[34,1,512]{2,1,0:T(2,128)(2,1)S(1)}, bf16[34,1,512]{2,1,0:T(2,128)(2,1)S(1)}, u32[]{:S(2)}, u32[]{:S(2)}) collective-permute-start(bf16[34,1,512]{2,1,0:T(2,128)(2,1)S(1)} %get-tuple-element.14), channel_id=1, source_target_pairs={{1,0},{2,1},{3,2},{4,3},{5,4},{6,5},{7,6},{9,8},{10,9},{11,10},{12... | collective-permute-start | bytes 104456 | tf_op jit(solution)/shard_map/ppermute | solution.py:15
  60.5 14.8 %all-to-all-start = ((bf16[8,64,128]{2,1,0:T(8,128)(2,1)}), bf16[8,64,128]{2,1,0:T(8,128)(2,1)S(1)}, u32[]{:S(2)}, u32[]{:S(2)}) async-start(bf16[8,64,128]{2,1,0:T(8,128)(2,1)} %bitcast.30), calls=%async_computation | async-start | bytes 262144 | tf_op jit(solution)/shard_map/all_to_all | solution.py:64

commit v2 on v0

v2 whole, which is shorter than its diff:
```python
import functools

import jax
import jax.numpy as jnp
from jax import lax
from jax.experimental import pallas as pl
from jax.experimental.pallas import tpu as pltpu
from jax.sharding import PartitionSpec as P

EAST = 32
NORTH = 16
OWN = EAST * NORTH
LONG = EAST + 4
PAD = 48
CODED = 40
FAR = 56
SIDE = 96
LANES = 128
OUT = OWN + 2 * NORTH + 2 * PAD
ALL = OUT + 2 * NORTH + 2 * PAD
EPS = 1e-05


def place(row, column):
    inner = jnp.where(
        (row >= 0) & (row < EAST),
        row * NORTH + column,
        jnp.where(
            row == -1,
            OWN + column,
            jnp.where(
                row == EAST,
                OWN + NORTH + column,
                jnp.where(row == -2, OUT + column, OUT + NORTH + column),
            ),
        ),
    )
    side = jnp.where(
        column == -1,
        OWN + 2 * NORTH,
        jnp.where(
            column == NORTH,
            OWN + 2 * NORTH + PAD,
            jnp.where(column == -2, OUT + 2 * NORTH, OUT + 2 * NORTH + PAD),
        ),
    )
    return jnp.where((column >= 0) & (column < NORTH), inner, side + row + 2)


def neighbours(codes, row, column, spot, sizes):
    third = (codes >= 3).astype(jnp.int32) + (codes >= 6).astype(jnp.int32)
    to_row = row + third - 1
    to_column = column + (codes - 3 * third) - 1
    east = spot[0] * EAST + to_row
    north = spot[1] * NORTH + to_column
    real = (east >= 0) & (east < sizes[0]) & (north >= 0) & (north < sizes[1])
    real = real & (row >= -1) & (row <= EAST)
    return jnp.where(real, place(to_row, to_column), -1)


def counted(index, width, degree):
    lanes = lax.broadcasted_iota(jnp.int32, (index.shape[0], width), 1)
    total = jnp.zeros(lanes.shape, jnp.float32)
    for slot in range(degree):
        total = total + jnp.where(lanes == index[:, slot : slot + 1], 1.0, 0.0)
    return total.astype(jnp.bfloat16)


def norm(x):
    away = x - jnp.mean(x, axis=-1, keepdims=True)
    var = jnp.mean(away * away, axis=-1, keepdims=True)
    return away * lax.rsqrt(var + EPS)


def dot(a, b):
    return jnp.dot(a, b, preferred_element_type=jnp.float32)


def rows_out(degree, top, bottom, codes, initial, last):
    for out, nodes, row in ((initial, top, 0), (last, bottom, EAST - 1)):
        lane = lax.broadcasted_iota(jnp.int32, (NORTH, LANES), 1)
        held = jnp.zeros((NORTH, LANES), jnp.int32)
        for slot in range(degree):
            held = jnp.where(lane == slot, codes[slot, :, row : row + 1], held)
        out[: 2 * NORTH] = nodes[...]
        out[2 * NORTH :] = jnp.zeros((NORTH, out.shape[1]), jnp.bfloat16)
        out[2 * NORTH :, :LANES] = held.astype(jnp.float32).astype(jnp.bfloat16)


def prepare(
    sizes, degree, spot, x, codes, noise, w_scale, w_shift, first, links, gains, sides, named
):
    for layer in range(w_scale.shape[0]):
        scale = jnp.sum(noise[...] * w_scale[layer], axis=0, keepdims=True)
        shift = jnp.sum(noise[...] * w_shift[layer], axis=0, keepdims=True)
        gains[2 * layer : 2 * layer + 1] = 1.0 + scale
        gains[2 * layer + 1 : 2 * layer + 2] = shift
    sides[...] = jnp.zeros(sides.shape, jnp.float32)
    named[...] = jnp.zeros(named.shape, jnp.float32)
    lines = 8
    rows = lines * NORTH
    for part in range(EAST // lines):
        here = slice(part * rows, (part + 1) * rows)
        state = x[here].astype(jnp.float32)
        held = codes[here]
        grid = state.reshape(lines, NORTH, state.shape[1])
        coded = held.astype(jnp.float32).reshape(lines, NORTH, degree)
        at = 2 + part * lines
        for side, (near, far) in enumerate(((0, 1), (NORTH - 1, NORTH - 2))):
            sides[side, at : at + lines] = grid[:, near]
            sides[side, FAR + at : FAR + at + lines] = grid[:, far]
            named[side, at : at + lines, :degree] = coded[:, near]
        first[here] = (norm(state) * gains[0:1] + gains[1:2]).astype(jnp.bfloat16)
        node = lax.broadcasted_iota(jnp.int32, (rows, degree), 0) + part * rows
        index = neighbours(held, node // NORTH, node % NORTH, (spot[0], spot[1]), sizes)
        links[here] = counted(index, OUT, degree)
    for side in range(2):
        for part in range(PAD // 16):
            sides[side, CODED:FAR, part * LANES : (part + 1) * LANES] = named[
                side, part * 16 : (part + 1) * 16
            ]


def columns_out(sides, before, after, initial, last, lines):
    top, bottom = (before[...].astype(jnp.float32), after[...].astype(jnp.float32))
    for side, (out, near, far) in enumerate(
        ((initial, 0, 1), (last, NORTH - 1, NORTH - 2))
    ):
        lines[...] = sides[side]
        for at, column in ((0, near), (FAR, far)):
            for step, source, row in (
                (0, top, 0), (1, top, 1), (EAST + 2, bottom, 0), (EAST + 3, bottom, 1)
            ):
                picked = row * NORTH + column
                lines[at + step : at + step + 1] = source[picked : picked + 1]
        picked = 2 * NORTH + near
        lines[CODED + 1 : CODED + 2, :LANES] = top[picked : picked + 1, :LANES]
        part, line = divmod(EAST + 2, 16)
        lines[CODED + line : CODED + line + 1, part * LANES : (part + 1) * LANES] = bottom[
            picked : picked + 1, :LANES
        ]
        out[...] = lines[...].astype(jnp.bfloat16)


def advance(
    sizes, degree, spot, x, first, links, gains, before, after, left, right,
    w_self, w_nbr, w_out, w_dec, preds, a, g, state,
):
    place_here = (spot[0], spot[1])
    gain, offset = gains[0:1], gains[1:2]

    def active(v):
        return (norm(v.astype(jnp.float32)) * gain + offset).astype(jnp.bfloat16)

    top, bottom, west, east = (
        arrived[...].astype(jnp.float32) for arrived in (before, after, left, right)
    )
    state[0:OWN] = x[...].astype(jnp.float32)
    at = OWN
    for ring_part in (top[NORTH : 2 * NORTH], bottom[:NORTH], west[:PAD], east[:PAD]):
        state[at : at + ring_part.shape[0]] = ring_part
        at += ring_part.shape[0]
    a[0:OWN] = first[...]
    a[OWN:OUT] = active(state[OWN:OUT])
    gap = jnp.zeros((PAD - SIDE + FAR, west.shape[1]), jnp.float32)
    second = [top[:NORTH], bottom[NORTH : 2 * NORTH], west[FAR:], gap, east[FAR:], gap]
    a[OUT:] = active(jnp.concatenate(second, axis=0))

    ring = []
    for arrived, row0, column0 in ((top, -1, 0), (bottom, EAST, 0), (west, -2, -1), (east, -2, NORTH)):
        if column0 == 0:
            held = arrived[2 * NORTH : 3 * NORTH, :LANES]
        else:
            held = jnp.concatenate(
                [arrived[CODED:FAR, i * LANES : (i + 1) * LANES] for i in range(PAD // 16)], axis=0
            )
        held = held[:, :degree].astype(jnp.int32)
        step = lax.broadcasted_iota(jnp.int32, held.shape, 0)
        if column0 == 0:
            row, column = (jnp.full(held.shape, row0, jnp.int32), step)
        else:
            row, column = (row0 + step, jnp.full(held.shape, column0, jnp.int32))
        index = neighbours(held, row, column, place_here, sizes)
        ring.append(counted(index, ALL, degree))
    ring = jnp.concatenate(ring, axis=0)

    sixth = 1.0 / degree
    g[0:OWN] = (dot(links[...], a[0:OUT]) * sixth).astype(jnp.bfloat16)
    g[OWN:OUT] = (dot(ring, a[...]) * sixth).astype(jnp.bfloat16)
    pre = dot(a[0:OUT], w_self[0]) + dot(g[...], w_nbr[0])
    hidden = jax.nn.silu(pre).astype(jnp.bfloat16)
    state[...] = state[...] + dot(hidden, w_out[0])

    gain, offset = gains[2:3], gains[3:4]
    a[0:OUT] = active(state[...])
    g[0:OWN] = (dot(links[...], a[0:OUT]) * sixth).astype(jnp.bfloat16)
    pre = dot(a[0:OWN], w_self[1]) + dot(g[0:OWN], w_nbr[1])
    hidden = jax.nn.silu(pre).astype(jnp.bfloat16)
    final = norm(state[0:OWN] + dot(hidden, w_out[1])).astype(jnp.bfloat16)
    preds[...] = dot(final, w_dec[...]).astype(jnp.bfloat16)


def score_share(mine, truth, copies):
    members = mine.shape[0]
    denom = 2.0 * members * (members - 1)
    held = [mine[one].astype(jnp.float32) for one in range(members)]
    goal = truth[...].astype(jnp.float32)
    skill = jnp.zeros(goal.shape, jnp.float32)
    spread = jnp.zeros(goal.shape, jnp.float32)
    for one in range(members):
        skill = skill + jnp.abs(held[one] - goal)
        for two in range(one):
            spread = spread + jnp.abs(held[one] - held[two])
    score = (skill * (1.0 / members) - spread * (2.0 / denom)).astype(jnp.bfloat16)
    for one in range(members):
        copies[one] = score


def swap(last, initial, axis):
    peers = lax.axis_size(axis)
    up = [(i, i + 1) for i in range(peers - 1)]
    down = [(j, i) for i, j in up]
    return lax.ppermute(last, axis, up), lax.ppermute(initial, axis, down)


def local(states, noises, codes, target, w_self, w_nbr, w_out, w_scale, w_shift, w_dec):
    width = states.shape[-1]
    degree = codes.shape[-1]
    variables = w_dec.shape[-1]
    layers = w_self.shape[0]
    x = states.reshape(OWN, width)
    sizes = (lax.axis_size("sx") * EAST, lax.axis_size("sy") * NORTH)
    spot = jnp.stack([lax.axis_index("sx"), lax.axis_index("sy")]).astype(jnp.int32)
    smem = pl.BlockSpec(memory_space=pltpu.SMEM)
    vmem = pl.BlockSpec(memory_space=pltpu.VMEM)

    def like(shape, dtype=jnp.bfloat16):
        return jax.ShapeDtypeStruct(shape, dtype)

    def limits(mib):
        return pltpu.CompilerParams(vmem_limit_bytes=mib << 20)

    def cost(flops, size):
        return pl.CostEstimate(flops=flops, bytes_accessed=size, transcendentals=0)

    initial, last = pl.pallas_call(
        functools.partial(rows_out, degree),
        grid=(1,),
        out_shape=(like((3 * NORTH, width)),) * 2,
        in_specs=[
            pl.BlockSpec((2 * NORTH, width), lambda i: (0, 0)),
            pl.BlockSpec((2 * NORTH, width), lambda i: (OWN // (2 * NORTH) - 1, 0)),
            pl.BlockSpec((degree, NORTH, EAST), lambda i: (0, 0, 0)),
        ],
        out_specs=(pl.BlockSpec((3 * NORTH, width), lambda i: (0, 0)),) * 2,
        compiler_params=limits(8),
        name="rows_out",
    )(x, x, codes.transpose(2, 1, 0))
    before, after = swap(last, initial, "sx")

    first, links, gains, sides = pl.pallas_call(
        functools.partial(prepare, sizes, degree),
        out_shape=(
            like((OWN, width)),
            like((OWN, OUT)),
            like((2 * layers, width), jnp.float32),
            like((2, SIDE, width), jnp.float32),
        ),
        in_specs=[smem] + [vmem] * 5,
        out_specs=(vmem,) * 4,
        scratch_shapes=[pltpu.VMEM((2, PAD, LANES), jnp.float32)],
        compiler_params=limits(16),
        cost_estimate=cost(1 << 24, 1 << 21),
        name="prepare",
    )(spot, x, codes.reshape(OWN, degree), noises.reshape(-1, 1), w_scale, w_shift)

    initial, last = pl.pallas_call(
        columns_out,
        out_shape=(like((SIDE, width)),) * 2,
        in_specs=[vmem] * 3,
        out_specs=(vmem,) * 2,
        scratch_shapes=[pltpu.VMEM((SIDE, width), jnp.float32)],
        compiler_params=limits(8),
        name="columns_out",
    )(sides, before, after)
    left, right = swap(last, initial, "sy")

    preds = pl.pallas_call(
        functools.partial(advance, sizes, degree),
        out_shape=like((OWN, variables)),
        in_specs=[smem] + [vmem] * 12,
        out_specs=vmem,
        scratch_shapes=[
            pltpu.VMEM((ALL, width), jnp.bfloat16),
            pltpu.VMEM((OUT, width), jnp.bfloat16),
            pltpu.VMEM((OUT, width), jnp.float32),
        ],
        compiler_params=limits(32),
        cost_estimate=cost(1 << 31, 1 << 23),
        name="advance",
    )(spot, x, first, links, gains, before, after, left, right, w_self, w_nbr, w_out, w_dec)

    members = lax.axis_size("member")
    share = OWN // members
    mine = lax.all_to_all(preds.reshape(members, share, variables), "member", 0, 0)
    truth = lax.dynamic_slice_in_dim(
        target.reshape(OWN, variables), lax.axis_index("member") * share, share, 0
    )
    copies = pl.pallas_call(
        score_share,
        out_shape=like(mine.shape),
        in_specs=[vmem] * 2,
        out_specs=vmem,
        compiler_params=limits(8),
        name="score_share",
    )(mine, truth)
    scores = lax.all_to_all(copies, "member", 0, 0).astype(jnp.float32)
    return (preds.reshape(1, EAST, NORTH, variables), scores.reshape(target.shape))


def solution(mesh):
    placed = (
        P("member", "sx", "sy", None),
        P("member", None),
        P("sx", "sy", None),
        P("sx", "sy", None),
        P(),
        P(),
        P(),
        P(),
        P(),
        P(),
    )
    return jax.shard_map(
        local,
        mesh=mesh,
        in_specs=placed,
        out_specs=(P("member", "sx", "sy", None), P("sx", "sy", None)),
        check_vma=False,
    )
```

time: 124 us -> 64.4 us (0.52)
  the two profiles are of different devices: /device:TPU:2 before, /device:TPU:135 now
where the time goes in v2:
time: 64.4 us; the launch traced here: 63.9 us
  starting transfers between devices  21.9 us (34%)
  waiting for transfers between devices  15.1 us (23%)
  blocking collectives  11.6 us (18%)
  Pallas kernels  8.56 us (13%)
  local copies, waits for them, and re-layouts  5.31 us (8%)
  other arithmetic  0.8 us (1%)
  between operations  0.75 us (1%)
    ppermute x4, starting transfers between devices, swap(): return (lax.ppermute(last, axis, up), lax.ppermute(initial, axis, down))  15 us
    all_to_all x1, blocking collectives, local(): scores = lax.all_to_all(copies, 'member', 0, 0).astype(jnp.float32)  11.6 us
    all_to_all x1, waiting for transfers between devices, local(): lax.all_to_all(preds.reshape(members, share, variables), 'member', 0, 0)  8.17 us
    ppermute x4, waiting for transfers between devices, swap(): return (lax.ppermute(last, axis, up), lax.ppermute(initial, axis, down))  6.93 us
    all_to_all x1, starting transfers between devices, local(): lax.all_to_all(preds.reshape(members, share, variables), 'member', 0, 0)  6.83 us
    pallas_call x1, Pallas kernels, local(): pl.pallas_call(functools.partial(advance, sizes, degree), out_shape=like(...  5.28 us
    unnamed x25, local copies, waits for them, and re-layouts  5.21 us
    pallas_call x1, Pallas kernels, local(): pl.pallas_call(functools.partial(prepare, sizes, degree), out_shape=(like...  3 us
  transfers between devices with their start and end apart: 5, of which 4 were waited for; matrix products, arithmetic and copies ran while one was open for 1% of the time, Pallas kernels for 5%

profile of v2, /device:TPU:135, one launch (start us, length us, event | category | flops | bytes accessed | tf_op | source)
XLA Modules:
  0.0 63.9 jit_solution(15587077891208894242)
XLA Ops:
  0.6 0.0 copy-start
  0.6 0.0 copy-start.1
  0.7 1.1 %copy-done.1 = bf16[1,32,16,512]{3,2,1,0:T(8,128)(2,1)S(1)} copy-done((bf16[1,32,16,512]{3,2,1,0:T(8,128)(2,1)S(1)}, bf16[1,32,16,512]{3,2,1,0:T(8,128)(2,1)}, u32[]{:S(2)}) %copy-start.1) | copy-done | bytes 524312
  1.7 0.0 copy-start.3
  1.7 0.8 %copy-done.3 = s32[32,16,6]{0,1,2:T(8,128)S(1)} copy-done((s32[32,16,6]{0,1,2:T(8,128)S(1)}, s32[32,16,6]{0,1,2:T(8,128)}, u32[]{:S(2)}) %copy-start.3) | copy-done | bytes 12312
  2.5 0.0 copy-start.4
  2.5 0.0 copy-start.2
  2.5 0.1 rows_out.1
  2.6 7.7 %collective-permute-start = (bf16[48,512]{1,0:T(8,128)(2,1)S(1)}, bf16[48,512]{1,0:T(8,128)(2,1)S(1)}, u32[]{:S(2)}, u32[]{:S(2)}) collective-permute-start(bf16[48,512]{1,0:T(8,128)(2,1)S(1)} %get-tuple-element.13), channel_id=1, source_target_pairs={{0,8},{8,16},{16,24},{24,32},{32,40},{40,48},{48,56},{1,9},{9,17},... | collective-permute-start | bytes 147464 | tf_op jit(solution)/shard_map/ppermute | solution.py:223
  10.3 1.9 %collective-permute-start.1 = (bf16[48,512]{1,0:T(8,128)(2,1)S(1)}, bf16[48,512]{1,0:T(8,128)(2,1)S(1)}, u32[]{:S(2)}, u32[]{:S(2)}) collective-permute-start(bf16[48,512]{1,0:T(8,128)(2,1)S(1)} %get-tuple-element.14), channel_id=1, source_target_pairs={{8,0},{16,8},{24,16},{32,24},{40,32},{48,40},{56,48},{9,1},{17,9},... | collective-permute-start | bytes 147464 | tf_op jit(solution)/shard_map/ppermute | solution.py:223
  12.3 0.0 copy-start.11
  12.3 0.1 pad_add_fusion.spot
  12.4 0.0 copy-done.4
  12.4 0.0 copy-start.5
  12.4 0.0 copy-start.6
  12.4 0.0 copy-start.7
  12.4 0.2 copy.12
  12.6 0.3 copy-done.11
  12.9 0.1 copy.13.noise
  13.0 0.0 copy-done.2
  13.0 0.2 copy-done.5
  13.3 0.1 copy-done.6
  13.3 3.0 %prepare.1 = (bf16[512,512]{1,0:T(8,128)(2,1)S(1)}, bf16[512,640]{1,0:T(8,128)(2,1)S(1)}, f32[4,512]{1,0:T(4,128)S(1)}, f32[2,96,512]{2,1,0:T(8,128)S(1)}) custom-call(s32[2]{0:T(128)S(1)} %pad_add_fusion.spot, bf16[512,512]{1,0:T(8,128)(2,1)S(1)} %bitcast.14, s32[512,6]{1,0:T(8,128)S(1)} %bitcast.16, f32[32,1]{1,0:T(8,128)S(1)} %copy.13.noise, ...), custom_call_target="tpu_custom_call" | custom-call | flops 16777216 | bytes 2097152 | tf_op jit(solution)/shard_map/prepare/pallas_call | solution.py:261
  16.4 0.0 collective-permute-done.before
  16.4 1.5 %collective-permute-done.1.after = bf16[48,512]{1,0:T(8,128)(2,1)S(1)} collective-permute-done((bf16[48,512]{1,0:T(8,128)(2,1)S(1)}, bf16[48,512]{1,0:T(8,128)(2,1)S(1)}, u32[]{:S(2)}, u32[]{:S(2)}) %collective-permute-start.1) | collective-permute-done | bytes 49184 | tf_op jit(solution)/shard_map/ppermute | solution.py:223
  17.9 0.0 copy-start.10
  17.9 3.4 %collective-permute-start.2 = (bf16[96,512]{1,0:T(8,128)(2,1)S(1)}, bf16[96,512]{1,0:T(8,128)(2,1)S(1)}, u32[]{:S(2)}, u32[]{:S(2)}) collective-permute-start(bf16[96,512]{1,0:T(8,128)(2,1)S(1)} %get-tuple-element.16), channel_id=1, source_target_pairs={{0,1},{1,2},{2,3},{3,4},{4,5},{5,6},{6,7},{8,9},{9,10},{10,11},{11... | collective-permute-start | bytes 294920 | tf_op jit(solution)/shard_map/ppermute | solution.py:223
  21.3 2.0 %collective-permute-start.3 = (bf16[96,512]{1,0:T(8,128)(2,1)S(1)}, bf16[96,512]{1,0:T(8,128)(2,1)S(1)}, u32[]{:S(2)}, u32[]{:S(2)}) collective-permute-start(bf16[96,512]{1,0:T(8,128)(2,1)S(1)} %get-tuple-element.17), channel_id=1, source_target_pairs={{1,0},{2,1},{3,2},{4,3},{5,4},{6,5},{7,6},{9,8},{10,9},{11,10},{12... | collective-permute-start | bytes 294920 | tf_op jit(solution)/shard_map/ppermute | solution.py:223
  23.3 0.1 collective-permute-done.2.left
  23.4 5.4 %collective-permute-done.3.right = bf16[96,512]{1,0:T(8,128)(2,1)S(1)} collective-permute-done((bf16[96,512]{1,0:T(8,128)(2,1)S(1)}, bf16[96,512]{1,0:T(8,128)(2,1)S(1)}, u32[]{:S(2)}, u32[]{:S(2)}) %collective-permute-start.3) | collective-permute-done | bytes 98336 | tf_op jit(solution)/shard_map/ppermute | solution.py:223
  28.8 0.0 copy-done.7
  28.8 0.0 copy-done.10
  28.8 0.0 copy-start.8
  28.8 1.2 %copy-done.8 = bf16[2,512,512]{2,1,0:T(8,128)(2,1)S(1)} copy-done((bf16[2,512,512]{2,1,0:T(8,128)(2,1)S(1)}, bf16[2,512,512]{2,1,0:T(8,128)(2,1)}, u32[]{:S(2)}) %copy-start.8) | copy-done | bytes 1048600
  30.0 0.0 copy-start.9
  30.0 1.2 %copy-done.9 = bf16[2,512,512]{2,1,0:T(8,128)(2,1)S(1)} copy-done((bf16[2,512,512]{2,1,0:T(8,128)(2,1)S(1)}, bf16[2,512,512]{2,1,0:T(8,128)(2,1)}, u32[]{:S(2)}) %copy-start.9) | copy-done | bytes 1048600
  31.2 5.3 %advance.1 = bf16[512,128]{1,0:T(8,128)(2,1)} custom-call(s32[2]{0:T(128)S(1)} %pad_add_fusion.spot, bf16[512,512]{1,0:T(8,128)(2,1)S(1)} %bitcast.15, bf16[512,512]{1,0:T(8,128)(2,1)S(1)} %get-tuple-element.10.first, bf16[512,640]{1,0:T(8,128)(2,1)S(1)} %get-tuple-element.11.links, f32[4,512]{1,0:T(4,128)S(1)} %get-tuple-element.12.gains, ...), custom_call_target="tpu_custom_call" | custom-call | flops 2147483648 | bytes 8388608 | tf_op jit(solution)/shard_map/advance/pallas_call | solution.py:288
  36.5 6.8 %all-to-all-start = ((bf16[8,64,128]{2,1,0:T(8,128)(2,1)}), bf16[8,64,128]{2,1,0:T(8,128)(2,1)S(1)}, u32[]{:S(2)}, u32[]{:S(2)}) async-start(bf16[8,64,128]{2,1,0:T(8,128)(2,1)} %bitcast.19), calls=%async_computation | async-start | bytes 262144 | tf_op jit(solution)/shard_map/all_to_all | solution.py:305
  43.3 0.0 copy-done
  43.4 8.2 %all-to-all-done.mine = bf16[8,64,128]{2,1,0:T(8,128)(2,1)S(1)} async-done(((bf16[8,64,128]{2,1,0:T(8,128)(2,1)}), bf16[8,64,128]{2,1,0:T(8,128)(2,1)S(1)}, u32[]{:S(2)}, u32[]{:S(2)}) %all-to-all-start) | async-done | bytes 131104 | tf_op jit(solution)/shard_map/all_to_all | solution.py:305
  51.5 0.1 score_share.1
  51.7 11.6 %all_to_all.10 = bf16[8,64,128]{2,1,0:T(8,128)(2,1)S(1)} all-to-all(bf16[8,64,128]{2,1,0:T(8,128)(2,1)S(1)} %score_share.1), channel_id=1, replica_groups=mesh['member'=8,'sx'=8,'sy'=8] {'member'}, dimensions={0} | all-to-all | bytes 262144 | tf_op jit(solution)/shard_map/all_to_all | solution.py:317
  63.2 0.7 %convert.1 = f32[32,16,128]{2,1,0:T(8,128)} convert(bf16[32,16,128]{2,1,0:T(8,128)(2,1)S(1)} %bitcast.18) | non-fusion elementwise | flops 65536 | bytes 393216 | tf_op jit(solution)/shard_map/reshape | solution.py:318
  (2 shorter events, 0.1 us)
Async XLA Ops:
  0.6 42.7 %copy-start = (bf16[32,16,128]{2,1,0:T(8,128)(2,1)S(1)}, bf16[32,16,128]{2,1,0:T(8,128)(2,1)}, u32[]{:S(2)}) copy-start(bf16[32,16,128]{2,1,0:T(8,128)(2,1)} %param.13) | copy-start | bytes 393220
  0.6 1.1 %copy-start.1 = (bf16[1,32,16,512]{3,2,1,0:T(8,128)(2,1)S(1)}, bf16[1,32,16,512]{3,2,1,0:T(8,128)(2,1)}, u32[]{:S(2)}) copy-start(bf16[1,32,16,512]{3,2,1,0:T(8,128)(2,1)} %param.10) | copy-start | bytes 1572868
  1.7 0.8 %copy-start.3 = (s32[32,16,6]{0,1,2:T(8,128)S(1)}, s32[32,16,6]{0,1,2:T(8,128)}, u32[]{:S(2)}) copy-start(s32[32,16,6]{0,1,2:T(8,128)} %param.12) | copy-start | bytes 36868
  2.5 9.8 %copy-start.4 = (s32[32,16,6]{0,1,2:T(8,128)S(1)}, s32[32,16,6]{0,1,2:T(8,128)}, u32[]{:S(2)}) copy-start(s32[32,16,6]{0,1,2:T(8,128)} %param.12) | copy-start | bytes 36868
  2.5 10.5 %copy-start.2 = (bf16[1,32,16,512]{3,2,1,0:T(8,128)(2,1)S(1)}, bf16[1,32,16,512]{3,2,1,0:T(8,128)(2,1)}, u32[]{:S(2)}) copy-start(bf16[1,32,16,512]{3,2,1,0:T(8,128)(2,1)} %param.10) | copy-start | bytes 1572868
  2.6 13.7 %collective-permute-start = (bf16[48,512]{1,0:T(8,128)(2,1)S(1)}, bf16[48,512]{1,0:T(8,128)(2,1)S(1)}, u32[]{:S(2)}, u32[]{:S(2)}) collective-permute-start(bf16[48,512]{1,0:T(8,128)(2,1)S(1)} %get-tuple-element.13), channel_id=1, source_target_pairs={{0,8},{8,16},{16,24},{24,32},{32,40},{40,48},{48,56},{1,9},{9,17},... | collective-permute-start | bytes 147464 | tf_op jit(solution)/shard_map/ppermute | solution.py:223
  10.3 7.5 %collective-permute-start.1 = (bf16[48,512]{1,0:T(8,128)(2,1)S(1)}, bf16[48,512]{1,0:T(8,128)(2,1)S(1)}, u32[]{:S(2)}, u32[]{:S(2)}) collective-permute-start(bf16[48,512]{1,0:T(8,128)(2,1)S(1)} %get-tuple-element.14), channel_id=1, source_target_pairs={{8,0},{16,8},{24,16},{32,24},{40,32},{48,40},{56,48},{9,1},{17,9},... | collective-permute-start | bytes 147464 | tf_op jit(solution)/shard_map/ppermute | solution.py:223
  12.3 0.7 %copy-start.11 = (f32[1,32]{1,0:T(1,128)S(1)}, f32[1,32]{1,0:T(1,128)}, u32[]{:S(2)}) copy-start(f32[1,32]{1,0:T(1,128)} %param.11) | copy-start | bytes 388
  12.4 0.9 %copy-start.5 = (f32[2,32,512]{2,1,0:T(8,128)S(1)}, f32[2,32,512]{2,1,0:T(8,128)}, u32[]{:S(2)}) copy-start(f32[2,32,512]{2,1,0:T(8,128)} %w_scale.1) | copy-start | bytes 393220
  12.4 1.0 %copy-start.6 = (f32[2,32,512]{2,1,0:T(8,128)S(1)}, f32[2,32,512]{2,1,0:T(8,128)}, u32[]{:S(2)}) copy-start(f32[2,32,512]{2,1,0:T(8,128)} %w_shift.1) | copy-start | bytes 393220
  12.4 16.4 %copy-start.7 = (bf16[2,512,512]{2,1,0:T(8,128)(2,1)S(1)}, bf16[2,512,512]{2,1,0:T(8,128)(2,1)}, u32[]{:S(2)}) copy-start(bf16[2,512,512]{2,1,0:T(8,128)(2,1)} %w_self.1) | copy-start | bytes 3145732
  17.9 10.9 %copy-start.10 = (bf16[512,128]{1,0:T(8,128)(2,1)S(1)}, bf16[512,128]{1,0:T(8,128)(2,1)}, u32[]{:S(2)}) copy-start(bf16[512,128]{1,0:T(8,128)(2,1)} %w_dec.1) | copy-start | bytes 393220
  17.9 5.5 %collective-permute-start.2 = (bf16[96,512]{1,0:T(8,128)(2,1)S(1)}, bf16[96,512]{1,0:T(8,128)(2,1)S(1)}, u32[]{:S(2)}, u32[]{:S(2)}) collective-permute-start(bf16[96,512]{1,0:T(8,128)(2,1)S(1)} %get-tuple-element.16), channel_id=1, source_target_pairs={{0,1},{1,2},{2,3},{3,4},{4,5},{5,6},{6,7},{8,9},{9,10},{10,11},{11... | collective-permute-start | bytes 294920 | tf_op jit(solution)/shard_map/ppermute | solution.py:223
  21.3 7.5 %collective-permute-start.3 = (bf16[96,512]{1,0:T(8,128)(2,1)S(1)}, bf16[96,512]{1,0:T(8,128)(2,1)S(1)}, u32[]{:S(2)}, u32[]{:S(2)}) collective-permute-start(bf16[96,512]{1,0:T(8,128)(2,1)S(1)} %get-tuple-element.17), channel_id=1, source_target_pairs={{1,0},{2,1},{3,2},{4,3},{5,4},{6,5},{7,6},{9,8},{10,9},{11,10},{12... | collective-permute-start | bytes 294920 | tf_op jit(solution)/shard_map/ppermute | solution.py:223
  28.8 1.2 %copy-start.8 = (bf16[2,512,512]{2,1,0:T(8,128)(2,1)S(1)}, bf16[2,512,512]{2,1,0:T(8,128)(2,1)}, u32[]{:S(2)}) copy-start(bf16[2,512,512]{2,1,0:T(8,128)(2,1)} %w_nbr.1) | copy-start | bytes 3145732
  30.0 1.2 %copy-start.9 = (bf16[2,512,512]{2,1,0:T(8,128)(2,1)S(1)}, bf16[2,512,512]{2,1,0:T(8,128)(2,1)}, u32[]{:S(2)}) copy-start(bf16[2,512,512]{2,1,0:T(8,128)(2,1)} %w_out.1) | copy-start | bytes 3145732
  36.5 15.0 %all-to-all-start = ((bf16[8,64,128]{2,1,0:T(8,128)(2,1)}), bf16[8,64,128]{2,1,0:T(8,128)(2,1)S(1)}, u32[]{:S(2)}, u32[]{:S(2)}) async-start(bf16[8,64,128]{2,1,0:T(8,128)(2,1)} %bitcast.19), calls=%async_computation | async-start | bytes 262144 | tf_op jit(solution)/shard_map/all_to_all | solution.py:305

commit v3 on v2

v3 whole, which is shorter than its diff:
```python
import functools

import jax
import jax.numpy as jnp
from jax import lax
from jax.experimental import pallas as pl
from jax.experimental.pallas import tpu as pltpu
from jax.sharding import PartitionSpec as P

EAST = 32
NORTH = 16
OWN = EAST * NORTH
LONG = EAST + 4
PAD = 48
CODED = 40
FAR = 56
SIDE = 96
LANES = 128
CODE = 1024
OUT = OWN + 2 * NORTH + 2 * PAD
ALL = OUT + 2 * NORTH + 2 * PAD
EPS = 1e-05


def place(row, column):
    inner = jnp.where(
        (row >= 0) & (row < EAST),
        row * NORTH + column,
        jnp.where(
            row == -1,
            OWN + column,
            jnp.where(
                row == EAST,
                OWN + NORTH + column,
                jnp.where(row == -2, OUT + column, OUT + NORTH + column),
            ),
        ),
    )
    side = jnp.where(
        column == -1,
        OWN + 2 * NORTH,
        jnp.where(
            column == NORTH,
            OWN + 2 * NORTH + PAD,
            jnp.where(column == -2, OUT + 2 * NORTH, OUT + 2 * NORTH + PAD),
        ),
    )
    return jnp.where((column >= 0) & (column < NORTH), inner, side + row + 2)


def neighbours(codes, row, column, spot, sizes):
    third = (codes >= 3).astype(jnp.int32) + (codes >= 6).astype(jnp.int32)
    to_row = row + third - 1
    to_column = column + (codes - 3 * third) - 1
    east = spot[0] * EAST + to_row
    north = spot[1] * NORTH + to_column
    real = (east >= 0) & (east < sizes[0]) & (north >= 0) & (north < sizes[1])
    real = real & (row >= -1) & (row <= EAST)
    return jnp.where(real, place(to_row, to_column), -1)


def counted(index, at, width, degree):
    lanes = lax.broadcasted_iota(jnp.int32, (index.shape[0], width), 1) + at
    total = jnp.zeros(lanes.shape, jnp.float32)
    for slot in range(degree):
        total = total + jnp.where(lanes == index[:, slot : slot + 1], 1.0, 0.0)
    return total.astype(jnp.bfloat16)


def norm(x):
    away = x - jnp.mean(x, axis=-1, keepdims=True)
    var = jnp.mean(away * away, axis=-1, keepdims=True)
    return away * lax.rsqrt(var + EPS)


def dot(a, b):
    return jnp.dot(a, b, preferred_element_type=jnp.float32)


def here(axis):
    return lax.axis_index(axis).astype(jnp.int32)


def rows_out(degree, top, bottom, codes, far_out, near_out):
    lane = lax.broadcasted_iota(jnp.int32, (NORTH, LANES), 1)
    lines = []
    for row in (0, EAST - 1):
        named = jnp.zeros((NORTH, LANES), jnp.int32)
        for slot in range(degree):
            named = jnp.where(lane == slot, codes[slot, :, row : row + 1], named)
        lines.append(named.astype(jnp.float32).astype(jnp.bfloat16))
    odd = here("sx") % 2 == 1
    for out, is_top in ((far_out, jnp.logical_not(odd)), (near_out, odd)):
        out[: 2 * NORTH] = jnp.where(is_top, top[...], bottom[...])
        out[2 * NORTH :] = jnp.zeros((NORTH, out.shape[1]), jnp.bfloat16)
        out[2 * NORTH :, :LANES] = jnp.where(is_top, lines[0], lines[1])


def sorted_by(axis, far, near):
    odd = here(axis) % 2 == 1
    far, near = (far[...].astype(jnp.float32), near[...].astype(jnp.float32))
    return jnp.where(odd, near, far), jnp.where(odd, far, near)


def collect(degree, x, coded, sides, named):
    sides[...] = jnp.zeros(sides.shape, jnp.float32)
    named[...] = jnp.zeros(named.shape, jnp.float32)
    lines = 8
    rows = lines * NORTH
    for part in range(EAST // lines):
        span = slice(part * rows, (part + 1) * rows)
        grid = x[span].astype(jnp.float32).reshape(lines, NORTH, x.shape[1])
        held = coded[span].reshape(lines, NORTH, degree)
        at = 2 + part * lines
        for side, (near, far) in enumerate(((0, 1), (NORTH - 1, NORTH - 2))):
            sides[side, at : at + lines] = grid[:, near]
            sides[side, FAR + at : FAR + at + lines] = grid[:, far]
            named[side, at : at + lines, :degree] = (held[:, near] >> 10).astype(jnp.float32)
    for side in range(2):
        for part in range(PAD // 16):
            sides[side, CODED:FAR, part * LANES : (part + 1) * LANES] = named[
                side, part * 16 : (part + 1) * 16
            ]


def prepare(
    degree, x, coded, noise, w_scale, w_shift, w_self, sent,
    first, links, gains, own_sum, own_part,
):
    for layer in range(w_scale.shape[0]):
        for at, w in enumerate((w_scale, w_shift)):
            gains[2 * layer + at : 2 * layer + at + 1] = (1.0 - at) + jnp.dot(
                noise[...], w[layer], precision=lax.Precision.HIGHEST,
                preferred_element_type=jnp.float32,
            )
    links[...] = jnp.zeros(links.shape, jnp.bfloat16)
    rows = OWN // 4
    for part in range(4):
        span = slice(part * rows, (part + 1) * rows)
        state = x[span].astype(jnp.float32)
        first[span] = (norm(state) * gains[0:1] + gains[1:2]).astype(jnp.bfloat16)
    for row in range(EAST):
        span = slice(row * NORTH, (row + 1) * NORTH)
        index = (coded[span] & (CODE - 1)) - 1
        tiles = {max(row - 1, 0) * NORTH // LANES, min(row + 1, EAST - 1) * NORTH // LANES}
        for tile in sorted(tiles) + [OWN // LANES]:
            links[span, tile * LANES : (tile + 1) * LANES] = counted(
                index, tile * LANES, LANES, degree
            )
    for part in range(2):
        span = slice(part * OWN // 2, (part + 1) * OWN // 2)
        own_part[span] = dot(first[span], w_self[0])
        own_sum[span] = dot(links[span, :OWN], first[...])


def columns_out(sides, far_row, near_row, far_out, near_out, lines):
    top, bottom = sorted_by("sx", far_row, near_row)
    for side, (near, far) in enumerate(((0, 1), (NORTH - 1, NORTH - 2))):
        lines[side] = sides[side]
        for at, column in ((0, near), (FAR, far)):
            for step, source, row in (
                (0, top, 0), (1, top, 1), (EAST + 2, bottom, 0), (EAST + 3, bottom, 1)
            ):
                picked = row * NORTH + column
                lines[side, at + step : at + step + 1] = source[picked : picked + 1]
        picked = 2 * NORTH + near
        lines[side, CODED + 1 : CODED + 2, :LANES] = top[picked : picked + 1, :LANES]
        part, line = divmod(EAST + 2, 16)
        lines[side, CODED + line : CODED + line + 1, part * LANES : (part + 1) * LANES] = bottom[
            picked : picked + 1, :LANES
        ]
    odd = here("sy") % 2
    far_out[...] = lines[odd].astype(jnp.bfloat16)
    near_out[...] = lines[1 - odd].astype(jnp.bfloat16)


def advance(
    sizes, degree, x, links, gains, own_sum, own_part, far_row, near_row, far_column, near_column,
    w_self, w_nbr, w_out, w_dec, first, preds, sent, rim_first, second, total, part, rim, ring,
):
    place_here = (here("sx"), here("sy"))
    sixth = 1.0 / degree

    def active(v, layer):
        return (norm(v) * gains[2 * layer : 2 * layer + 1] + gains[2 * layer + 1 : 2 * layer + 2]).astype(
            jnp.bfloat16
        )

    top, bottom = sorted_by("sx", far_row, near_row)
    west, east = sorted_by("sy", far_column, near_column)
    gap = jnp.zeros((PAD - SIDE + FAR, west.shape[1]), jnp.float32)
    rims = (
        (top[NORTH : 2 * NORTH], bottom[:NORTH], west[:PAD], east[:PAD]),
        (top[:NORTH], bottom[NORTH : 2 * NORTH], west[FAR:], gap, east[FAR:], gap),
    )
    at = 0
    for ring_parts in rims:
        for nodes in ring_parts:
            rim[at : at + nodes.shape[0]] = nodes
            at += nodes.shape[0]

    at = 0
    for arrived, row0, column0 in ((top, -1, 0), (bottom, EAST, 0), (west, -2, -1), (east, -2, NORTH)):
        if column0 == 0:
            held = arrived[2 * NORTH : 3 * NORTH, :LANES]
        else:
            held = jnp.concatenate(
                [arrived[CODED:FAR, i * LANES : (i + 1) * LANES] for i in range(PAD // 16)], axis=0
            )
        held = held[:, :degree].astype(jnp.int32)
        step = lax.broadcasted_iota(jnp.int32, held.shape, 0)
        if column0 == 0:
            row, column = (jnp.full(held.shape, row0, jnp.int32), step)
        else:
            row, column = (row0 + step, jnp.full(held.shape, column0, jnp.int32))
        index = neighbours(held, row, column, place_here, sizes)
        ring[at : at + held.shape[0]] = counted(index, 0, ALL, degree)
        at += held.shape[0]

    def rest(total, part, layer):
        hidden = jax.nn.silu(part + dot(total, w_nbr[layer])).astype(jnp.bfloat16)
        return dot(hidden, w_out[layer])

    rim_first[...] = active(rim[...], 0)
    near = slice(0, OUT - OWN)
    own = slice(0, OWN)
    total[own] = ((own_sum[...] + dot(links[:, OWN:], rim_first[near])) * sixth).astype(jnp.bfloat16)
    total[OWN:] = (
        (dot(ring[:, :OWN], first[...]) + dot(ring[:, OWN:], rim_first[...])) * sixth
    ).astype(jnp.bfloat16)
    part[own] = own_part[...]
    part[OWN:] = dot(rim_first[near], w_self[0])
    v = rest(total[...], part[...], 0)
    part[own] = x[...].astype(jnp.float32) + v[own]
    part[OWN:] = rim[near] + v[OWN:]
    second[...] = active(part[...], 1)
    total[own] = (dot(links[...], second[...]) * sixth).astype(jnp.bfloat16)
    v = part[own] + rest(total[own], dot(second[own], w_self[1]), 1)
    value = dot(norm(v).astype(jnp.bfloat16), w_dec[...]).astype(jnp.bfloat16)
    preds[...] = value
    sent[...] = value


def score_share(mine, truth, copies):
    members, share, _ = mine.shape
    denom = 2.0 * members * (members - 1)
    held = [mine[one].astype(jnp.float32) for one in range(members)]
    goal = truth[pl.ds(pl.multiple_of(here("member") * share, share), share)].astype(jnp.float32)
    skill = jnp.zeros(goal.shape, jnp.float32)
    spread = jnp.zeros(goal.shape, jnp.float32)
    for one in range(members):
        skill = skill + jnp.abs(held[one] - goal)
        for two in range(one):
            spread = spread + jnp.abs(held[one] - held[two])
    score = (skill * (1.0 / members) - spread * (2.0 / denom)).astype(jnp.bfloat16)
    for one in range(members):
        copies[one] = score


def swap(far, near, axis):
    peers = lax.axis_size(axis)
    pairs = [[(i, i + 1), (i + 1, i)] for i in range(peers - 1)]
    return (
        lax.ppermute(far, axis, sum(pairs[1::2], [])),
        lax.ppermute(near, axis, sum(pairs[0::2], [])),
    )


def local(states, noises, codes, target, w_self, w_nbr, w_out, w_scale, w_shift, w_dec):
    width = states.shape[-1]
    degree = codes.shape[-1]
    variables = w_dec.shape[-1]
    layers = w_self.shape[0]
    x = states.reshape(OWN, width)
    sizes = (lax.axis_size("sx") * EAST, lax.axis_size("sy") * NORTH)
    vmem = pl.BlockSpec(memory_space=pltpu.VMEM)

    def like(shape, dtype=jnp.bfloat16):
        return jax.ShapeDtypeStruct(shape, dtype)

    def limits(mib):
        return pltpu.CompilerParams(vmem_limit_bytes=mib << 20)

    def cost(flops, size):
        return pl.CostEstimate(flops=flops, bytes_accessed=size, transcendentals=0)

    slots = codes.transpose(2, 1, 0)
    far_row, near_row = swap(
        *pl.pallas_call(
            functools.partial(rows_out, degree),
            grid=(1,),
            out_shape=(like((3 * NORTH, width)),) * 2,
            in_specs=[
                pl.BlockSpec((2 * NORTH, width), lambda i: (0, 0)),
                pl.BlockSpec((2 * NORTH, width), lambda i: (OWN // (2 * NORTH) - 1, 0)),
                pl.BlockSpec(slots.shape, lambda i: (0, 0, 0)),
            ],
            out_specs=(pl.BlockSpec((3 * NORTH, width), lambda i: (0, 0)),) * 2,
            compiler_params=limits(60),
            name="rows_out",
        )(x, x, slots),
        "sx",
    )

    index = neighbours(
        slots,
        lax.broadcasted_iota(jnp.int32, slots.shape, 2),
        lax.broadcasted_iota(jnp.int32, slots.shape, 1),
        (here("sx"), here("sy")),
        sizes,
    )
    coded = (index + 1 + CODE * slots).transpose(2, 1, 0).reshape(OWN, degree)
    sides = pl.pallas_call(
        functools.partial(collect, degree),
        out_shape=like((2, SIDE, width), jnp.float32),
        in_specs=[vmem] * 2,
        out_specs=vmem,
        scratch_shapes=[pltpu.VMEM((2, PAD, LANES), jnp.float32)],
        compiler_params=limits(8),
        cost_estimate=cost(1 << 20, 1 << 24),
        name="collect",
    )(x, coded)

    sent = pl.pallas_call(
        columns_out,
        out_shape=(like((SIDE, width)),) * 2,
        in_specs=[vmem] * 3,
        out_specs=(vmem,) * 2,
        scratch_shapes=[pltpu.VMEM((2, SIDE, width), jnp.float32)],
        compiler_params=limits(8),
        name="columns_out",
    )(sides, far_row, near_row)
    far_column, near_column = swap(*sent, "sy")

    first, links, gains, own_sum, own_part = pl.pallas_call(
        functools.partial(prepare, degree),
        out_shape=(
            like((OWN, width)),
            like((OWN, OUT)),
            like((2 * layers, width), jnp.float32),
            like((OWN, width), jnp.float32),
            like((OWN, width), jnp.float32),
        ),
        in_specs=[vmem] * 6 + [pl.BlockSpec(memory_space=pl.ANY)],
        out_specs=(vmem,) * 5,
        compiler_params=limits(16),
        cost_estimate=cost(1 << 24, 1 << 25),
        name="prepare",
    )(x, coded, noises, w_scale, w_shift, w_self, sent[1])

    preds, shares = pl.pallas_call(
        functools.partial(advance, sizes, degree),
        out_shape=(like((OWN, variables)),) * 2,
        in_specs=[vmem] * 14,
        out_specs=(vmem,) * 2,
        scratch_shapes=[
            pltpu.VMEM((ALL - OWN, width), jnp.bfloat16),
            pltpu.VMEM((OUT, width), jnp.bfloat16),
            pltpu.VMEM((OUT, width), jnp.bfloat16),
            pltpu.VMEM((OUT, width), jnp.float32),
            pltpu.VMEM((ALL - OWN, width), jnp.float32),
            pltpu.VMEM((OUT - OWN, ALL), jnp.bfloat16),
        ],
        compiler_params=limits(16),
        cost_estimate=cost(1 << 31, 1 << 23),
        name="advance",
    )(
        x, links, gains, own_sum, own_part, far_row, near_row, far_column, near_column,
        w_self, w_nbr, w_out, w_dec, first,
    )

    members = lax.axis_size("member")
    share = OWN // members
    mine = lax.all_to_all(shares.reshape(members, share, variables), "member", 0, 0)
    copies = pl.pallas_call(
        score_share,
        out_shape=like(mine.shape),
        in_specs=[vmem] * 2,
        out_specs=vmem,
        compiler_params=limits(8),
        name="score_share",
    )(mine, target.reshape(OWN, variables))
    scores = lax.all_to_all(copies, "member", 0, 0).astype(jnp.float32)
    return (preds.reshape(1, EAST, NORTH, variables), scores.reshape(target.shape))


def solution(mesh):
    placed = (
        P("member", "sx", "sy", None),
        P("member", None),
        P("sx", "sy", None),
        P("sx", "sy", None),
        P(),
        P(),
        P(),
        P(),
        P(),
        P(),
    )
    return jax.shard_map(
        local,
        mesh=mesh,
        in_specs=placed,
        out_specs=(P("member", "sx", "sy", None), P("sx", "sy", None)),
        check_vma=False,
    )
```

time: 64.4 us -> 57.8 us (0.90)
  the two profiles are of different devices: /device:TPU:135 before, /device:TPU:134 now
where the time goes in v3:
time: 57.8 us; the launch traced here: 57.5 us
  blocking collectives  27.6 us (48%)
  starting transfers between devices  16.1 us (28%)
  Pallas kernels  8.08 us (14%)
  waiting for transfers between devices  3.76 us (7%)
  between operations  0.84 us (1%)
  other arithmetic  0.82 us (1%)
    all_to_all x1, blocking collectives, local(): lax.all_to_all(shares.reshape(members, share, variables), 'member', 0, 0)  16.1 us
    all_to_all x1, blocking collectives, local(): scores = lax.all_to_all(copies, 'member', 0, 0).astype(jnp.float32)  11.5 us
    ppermute x2, starting transfers between devices, swap(): lax.ppermute(near, axis, sum(pairs[0::2], []))  10.1 us
    ppermute x2, starting transfers between devices, swap(): lax.ppermute(far, axis, sum(pairs[1::2], []))  6 us
    pallas_call x1, Pallas kernels, local(): pl.pallas_call(functools.partial(advance, sizes, degree), out_shape=(like...  4.59 us
    ppermute x2, waiting for transfers between devices, swap(): lax.ppermute(far, axis, sum(pairs[1::2], []))  3.33 us
    pallas_call x1, Pallas kernels, local(): pl.pallas_call(functools.partial(rows_out, degree), grid=(1,), out_shape=...  1.63 us
    pallas_call x1, Pallas kernels, local(): pl.pallas_call(functools.partial(prepare, degree), out_shape=(like((OWN,...  1.43 us
  transfers between devices with their start and end apart: 4, of which 2 were waited for; matrix products, arithmetic and copies ran while one was open for 1% of the time, Pallas kernels for 3%

profile of v3, /device:TPU:134, one launch (start us, length us, event | category | flops | bytes accessed | tf_op | source)
XLA Modules:
  0.0 57.5 jit_solution(11078398653644567784)
XLA Ops:
  0.6 0.0 copy-start.9
  0.6 0.0 copy-start
  0.6 1.6 %rows_out.1 = (bf16[48,512]{1,0:T(8,128)(2,1)}, bf16[48,512]{1,0:T(8,128)(2,1)}) custom-call(bf16[512,512]{1,0:T(8,128)(2,1)} %bitcast.8, bf16[512,512]{1,0:T(8,128)(2,1)} %bitcast.9, s32[6,16,32]{2,1,0:T(8,128)} %bitcast.18), custom_call_target="tpu_custom_call" | custom-call | tf_op jit(solution)/shard_map/rows_out/pallas_call | solution.py:289
  2.3 1.9 %collective-permute-start = (bf16[48,512]{1,0:T(8,128)(2,1)}, bf16[48,512]{1,0:T(8,128)(2,1)S(1)}, u32[]{:S(2)}, u32[]{:S(2)}) collective-permute-start(bf16[48,512]{1,0:T(8,128)(2,1)} %get-tuple-element.13), channel_id=1, source_target_pairs={{8,16},{16,8},{24,32},{32,24},{40,48},{48,40},{9,17},{17,9},{25,33... | collective-permute-start | bytes 147464 | tf_op jit(solution)/shard_map/ppermute | solution.py:264
  4.2 7.4 %collective-permute-start.1 = (bf16[48,512]{1,0:T(8,128)(2,1)}, bf16[48,512]{1,0:T(8,128)(2,1)S(1)}, u32[]{:S(2)}, u32[]{:S(2)}) collective-permute-start(bf16[48,512]{1,0:T(8,128)(2,1)} %get-tuple-element.14), channel_id=1, source_target_pairs={{0,8},{8,0},{16,24},{24,16},{32,40},{40,32},{48,56},{56,48},{1,9},... | collective-permute-start | bytes 147464 | tf_op jit(solution)/shard_map/ppermute | solution.py:265
  11.6 0.0 copy-start.1
  11.6 0.0 copy-done.9
  11.7 0.1 multiply_add_fusion
  11.8 0.2 copy.12
  12.0 0.0 copy-done
  12.0 0.2 collect.1.sides
  12.2 0.0 copy-start.2
  12.2 0.0 copy-start.3
  12.2 0.0 collective-permute-done.far_row
  12.2 0.4 collective-permute-done.1.near_row
  12.7 0.0 copy-start.8
  12.7 0.1 columns_out.1
  12.8 0.0 copy-start.5
  12.8 2.7 %collective-permute-start.3 = (bf16[96,512]{1,0:T(8,128)(2,1)S(1)}, bf16[96,512]{1,0:T(8,128)(2,1)S(1)}, u32[]{:S(2)}, u32[]{:S(2)}) collective-permute-start(bf16[96,512]{1,0:T(8,128)(2,1)S(1)} %get-tuple-element.15.sent), channel_id=1, source_target_pairs={{0,1},{1,0},{2,3},{3,2},{4,5},{5,4},{6,7},{7,6},{8,9},{9,8},{10,11... | collective-permute-start | bytes 294920 | tf_op jit(solution)/shard_map/ppermute | solution.py:265
  15.5 0.0 copy-start.6
  15.5 0.0 copy-start.7
  15.5 4.1 %collective-permute-start.2 = (bf16[96,512]{1,0:T(8,128)(2,1)S(1)}, bf16[96,512]{1,0:T(8,128)(2,1)S(1)}, u32[]{:S(2)}, u32[]{:S(2)}) collective-permute-start(bf16[96,512]{1,0:T(8,128)(2,1)S(1)} %get-tuple-element.20), channel_id=1, source_target_pairs={{1,2},{2,1},{3,4},{4,3},{5,6},{6,5},{9,10},{10,9},{11,12},{12,11},... | collective-permute-start | bytes 294920 | tf_op jit(solution)/shard_map/ppermute | solution.py:264
  19.6 0.0 copy-done.1
  19.6 0.0 copy-done.2
  19.7 0.0 copy-done.3
  19.7 0.0 copy-done.5
  19.7 1.4 %prepare.1 = (bf16[512,512]{1,0:T(8,128)(2,1)S(1)}, bf16[512,640]{1,0:T(8,128)(2,1)S(1)}, f32[4,512]{1,0:T(4,128)S(1)}, f32[512,512]{1,0:T(8,128)S(1)}, f32[512,512]{1,0:T(8,128)S(1)}) custom-call(bf16[512,512]{1,0:T(8,128)(2,1)S(1)} %bitcast.11, s32[512,6]{1,0:T(8,128)S(1)} %bitcast.14, f32[1,32]{1,0:T(1,128)S(1)} %copy-done.5, ...), custom_call_target="tpu_custom_call" | custom-call | flops 16777216 | bytes 33554432 | tf_op jit(solution)/shard_map/prepare/pallas_call | solution.py:335
  21.1 0.0 collective-permute-done.3.near_column
  21.1 3.3 %collective-permute-done.2.far_column = bf16[96,512]{1,0:T(8,128)(2,1)S(1)} collective-permute-done((bf16[96,512]{1,0:T(8,128)(2,1)S(1)}, bf16[96,512]{1,0:T(8,128)(2,1)S(1)}, u32[]{:S(2)}, u32[]{:S(2)}) %collective-permute-start.2) | collective-permute-done | bytes 98336 | tf_op jit(solution)/shard_map/ppermute | solution.py:264
  24.4 0.0 copy-done.8
  24.4 0.0 copy-done.6
  24.4 0.0 copy-done.7
  24.4 4.6 %advance.1 = (bf16[512,128]{1,0:T(8,128)(2,1)}, bf16[512,128]{1,0:T(8,128)(2,1)S(1)}) custom-call(bf16[512,512]{1,0:T(8,128)(2,1)S(1)} %bitcast.12, bf16[512,640]{1,0:T(8,128)(2,1)S(1)} %get-tuple-element.16.links, f32[4,512]{1,0:T(4,128)S(1)} %get-tuple-element.17.gains, f32[512,512]{1,0:T(8,128)S(1)} %get-tuple-element.18.own_sum, ...), custom_call_target="tpu_custom_call" | custom-call | flops 2147483648 | bytes 8388608 | tf_op jit(solution)/shard_map/advance/pallas_call | solution.py:351
  29.0 0.0 copy-start.4
  29.0 16.1 %all_to_all.10.mine = bf16[8,64,128]{2,1,0:T(8,128)(2,1)S(1)} all-to-all(bf16[8,64,128]{2,1,0:T(8,128)(2,1)S(1)} %bitcast.16), channel_id=1, replica_groups=mesh['member'=8,'sx'=8,'sy'=8] {'member'}, dimensions={0} | all-to-all | bytes 262144 | tf_op jit(solution)/shard_map/all_to_all | solution.py:374
  45.1 0.0 copy-done.4
  45.1 0.1 score_share.1
  45.3 11.5 %all_to_all.11 = bf16[8,64,128]{2,1,0:T(8,128)(2,1)S(1)} all-to-all(bf16[8,64,128]{2,1,0:T(8,128)(2,1)S(1)} %score_share.1), channel_id=1, replica_groups=mesh['member'=8,'sx'=8,'sy'=8] {'member'}, dimensions={0} | all-to-all | bytes 262144 | tf_op jit(solution)/shard_map/all_to_all | solution.py:383
  56.7 0.7 %convert.1 = f32[32,16,128]{2,1,0:T(8,128)} convert(bf16[32,16,128]{2,1,0:T(8,128)(2,1)S(1)} %bitcast.17) | non-fusion elementwise | flops 65536 | bytes 393216 | tf_op jit(solution)/shard_map/reshape | solution.py:384
  (1 shorter events, 0.0 us)
Async XLA Ops:
  0.6 11.0 %copy-start.9 = (s32[32,16,6]{0,1,2:T(8,128)S(1)}, s32[32,16,6]{0,1,2:T(8,128)}, u32[]{:S(2)}) copy-start(s32[32,16,6]{0,1,2:T(8,128)} %param.12) | copy-start | bytes 36868
  0.6 11.3 %copy-start = (bf16[1,32,16,512]{3,2,1,0:T(8,128)(2,1)S(1)}, bf16[1,32,16,512]{3,2,1,0:T(8,128)(2,1)}, u32[]{:S(2)}) copy-start(bf16[1,32,16,512]{3,2,1,0:T(8,128)(2,1)} %param.10) | copy-start | bytes 1572868
  2.3 10.0 %collective-permute-start = (bf16[48,512]{1,0:T(8,128)(2,1)}, bf16[48,512]{1,0:T(8,128)(2,1)S(1)}, u32[]{:S(2)}, u32[]{:S(2)}) collective-permute-start(bf16[48,512]{1,0:T(8,128)(2,1)} %get-tuple-element.13), channel_id=1, source_target_pairs={{8,16},{16,8},{24,32},{32,24},{40,48},{48,40},{9,17},{17,9},{25,33... | collective-permute-start | bytes 147464 | tf_op jit(solution)/shard_map/ppermute | solution.py:264
  4.2 8.5 %collective-permute-start.1 = (bf16[48,512]{1,0:T(8,128)(2,1)}, bf16[48,512]{1,0:T(8,128)(2,1)S(1)}, u32[]{:S(2)}, u32[]{:S(2)}) collective-permute-start(bf16[48,512]{1,0:T(8,128)(2,1)} %get-tuple-element.14), channel_id=1, source_target_pairs={{0,8},{8,0},{16,24},{24,16},{32,40},{40,32},{48,56},{56,48},{1,9},... | collective-permute-start | bytes 147464 | tf_op jit(solution)/shard_map/ppermute | solution.py:265
  11.6 8.0 %copy-start.1 = (bf16[2,512,512]{2,1,0:T(8,128)(2,1)S(1)}, bf16[2,512,512]{2,1,0:T(8,128)(2,1)}, u32[]{:S(2)}) copy-start(bf16[2,512,512]{2,1,0:T(8,128)(2,1)} %w_self.3) | copy-start | bytes 3145732
  12.2 7.4 %copy-start.2 = (f32[2,32,512]{2,1,0:T(8,128)S(1)}, f32[2,32,512]{2,1,0:T(8,128)}, u32[]{:S(2)}) copy-start(f32[2,32,512]{2,1,0:T(8,128)} %w_scale.1) | copy-start | bytes 393220
  12.2 7.4 %copy-start.3 = (f32[2,32,512]{2,1,0:T(8,128)S(1)}, f32[2,32,512]{2,1,0:T(8,128)}, u32[]{:S(2)}) copy-start(f32[2,32,512]{2,1,0:T(8,128)} %w_shift.1) | copy-start | bytes 393220
  12.7 11.8 %copy-start.8 = (bf16[512,128]{1,0:T(8,128)(2,1)S(1)}, bf16[512,128]{1,0:T(8,128)(2,1)}, u32[]{:S(2)}) copy-start(bf16[512,128]{1,0:T(8,128)(2,1)} %w_dec.1) | copy-start | bytes 393220
  12.8 6.9 %copy-start.5 = (f32[1,32]{1,0:T(1,128)S(1)}, f32[1,32]{1,0:T(1,128)}, u32[]{:S(2)}) copy-start(f32[1,32]{1,0:T(1,128)} %noise.1) | copy-start | bytes 388
  12.8 8.3 %collective-permute-start.3 = (bf16[96,512]{1,0:T(8,128)(2,1)S(1)}, bf16[96,512]{1,0:T(8,128)(2,1)S(1)}, u32[]{:S(2)}, u32[]{:S(2)}) collective-permute-start(bf16[96,512]{1,0:T(8,128)(2,1)S(1)} %get-tuple-element.15.sent), channel_id=1, source_target_pairs={{0,1},{1,0},{2,3},{3,2},{4,5},{5,4},{6,7},{7,6},{8,9},{9,8},{10,11... | collective-permute-start | bytes 294920 | tf_op jit(solution)/shard_map/ppermute | solution.py:265
  15.5 8.9 %copy-start.6 = (bf16[2,512,512]{2,1,0:T(8,128)(2,1)S(1)}, bf16[2,512,512]{2,1,0:T(8,128)(2,1)}, u32[]{:S(2)}) copy-start(bf16[2,512,512]{2,1,0:T(8,128)(2,1)} %w_nbr.1) | copy-start | bytes 3145732
  15.5 8.9 %copy-start.7 = (bf16[2,512,512]{2,1,0:T(8,128)(2,1)S(1)}, bf16[2,512,512]{2,1,0:T(8,128)(2,1)}, u32[]{:S(2)}) copy-start(bf16[2,512,512]{2,1,0:T(8,128)(2,1)} %w_out.1) | copy-start | bytes 3145732
  15.5 8.9 %collective-permute-start.2 = (bf16[96,512]{1,0:T(8,128)(2,1)S(1)}, bf16[96,512]{1,0:T(8,128)(2,1)S(1)}, u32[]{:S(2)}, u32[]{:S(2)}) collective-permute-start(bf16[96,512]{1,0:T(8,128)(2,1)S(1)} %get-tuple-element.20), channel_id=1, source_target_pairs={{1,2},{2,1},{3,4},{4,3},{5,6},{6,5},{9,10},{10,9},{11,12},{12,11},... | collective-permute-start | bytes 294920 | tf_op jit(solution)/shard_map/ppermute | solution.py:264
  29.0 16.1 %copy-start.4 = (bf16[32,16,128]{2,1,0:T(8,128)(2,1)S(1)}, bf16[32,16,128]{2,1,0:T(8,128)(2,1)}, u32[]{:S(2)}) copy-start(bf16[32,16,128]{2,1,0:T(8,128)(2,1)} %param.13) | copy-start | bytes 393220

commit v4 on v3

--- a/solution.py
+++ b/solution.py
@@ -123,9 +123,32 @@
             ]
 
 
+def active(v, gains, layer):
+    return norm(v) * gains[2 * layer : 2 * layer + 1] + gains[2 * layer + 1 : 2 * layer + 2]
+
+
+def rest(total, part, w_nbr, w_out, layer):
+    hidden = jax.nn.silu(part + dot(total, w_nbr[layer])).astype(jnp.bfloat16)
+    return dot(hidden, w_out[layer])
+
+
+def ends(v):
+    grid = v.reshape(EAST, NORTH, v.shape[-1])
+    return jnp.concatenate([grid[:, 0], grid[:, NORTH - 1]], axis=0)
+
+
+def split(out, v):
+    for tile in range(out.shape[0]):
+        out[tile] = v[:, tile * LANES : (tile + 1) * LANES]
+
+
+def joined(tiles):
+    return jnp.concatenate([tiles[tile] for tile in range(tiles.shape[0])], axis=1)
+
+
 def prepare(
-    degree, x, coded, noise, w_scale, w_shift, w_self, sent,
-    first, links, gains, own_sum, own_part,
+    degree, x, coded, noise, w_scale, w_shift, w_self, w_nbr, w_out, far_row, near_row, sent,
+    first, links, gains, end_links, end_sum, end_part, x1, a1, own_sum, own_part, rim,
 ):
     for layer in range(w_scale.shape[0]):
         for at, w in enumerate((w_scale, w_shift)):
@@ -134,11 +157,7 @@
                 preferred_element_type=jnp.float32,
             )
     links[...] = jnp.zeros(links.shape, jnp.bfloat16)
-    rows = OWN // 4
-    for part in range(4):
-        span = slice(part * rows, (part + 1) * rows)
-        state = x[span].astype(jnp.float32)
-        first[span] = (norm(state) * gains[0:1] + gains[1:2]).astype(jnp.bfloat16)
+    first[...] = active(x[...].astype(jnp.float32), gains, 0).astype(jnp.bfloat16)
     for row in range(EAST):
         span = slice(row * NORTH, (row + 1) * NORTH)
         index = (coded[span] & (CODE - 1)) - 1
@@ -147,13 +166,25 @@
             links[span, tile * LANES : (tile + 1) * LANES] = counted(
                 index, tile * LANES, LANES, degree
             )
-    for part in range(2):
-        span = slice(part * OWN // 2, (part + 1) * OWN // 2)
-        own_part[span] = dot(first[span], w_self[0])
-        own_sum[span] = dot(links[span, :OWN], first[...])
-
-
-def columns_out(sides, far_row, near_row, far_out, near_out, lines):
+    end_links[...] = counted(ends((coded[...] & (CODE - 1)) - 1), OWN, OUT - OWN, degree)
+
+    top, bottom = sorted_by("sx", far_row, near_row)
+    rim[: 2 * NORTH] = active(
+        jnp.concatenate([top[NORTH : 2 * NORTH], bottom[:NORTH]], axis=0), gains, 0
+    ).astype(jnp.bfloat16)
+    rim[2 * NORTH :] = jnp.zeros((rim.shape[0] - 2 * NORTH, rim.shape[1]), jnp.bfloat16)
+    own_part[...] = dot(first[...], w_self[0])
+    own_sum[...] = dot(links[:, :OWN], first[...])
+    end_part[...] = ends(own_part[...])
+    end_sum[...] = ends(own_sum[...])
+    total = own_sum[...] + dot(links[:, OWN:], rim[...])
+    total = (total * (1.0 / degree)).astype(jnp.bfloat16)
+    v = x[...].astype(jnp.float32) + rest(total, own_part[...], w_nbr, w_out, 0)
+    split(x1, v)
+    split(a1, active(v, gains, 1))
+
+
+def columns_out(w_out, sides, far_row, near_row, far_out, near_out, lines):
     top, bottom = sorted_by("sx", far_row, near_row)
     for side, (near, far) in enumerate(((0, 1), (NORTH - 1, NORTH - 2))):
         lines[side] = sides[side]
@@ -175,16 +206,12 @@
 
 
 def advance(
-    sizes, degree, x, links, gains, own_sum, own_part, far_row, near_row, far_column, near_column,
-    w_self, w_nbr, w_out, w_dec, first, preds, sent, rim_first, second, total, part, rim, ring,
+    sizes, degree, first, links, gains, end_links, end_sum, end_part, old_x1, old_a1, sides,
+    far_row, near_row, far_column, near_column, w_self, w_nbr, w_out, w_dec,
+    preds, sent, x1, a1, rim_first, second, total, part, rim, ring,
 ):
     place_here = (here("sx"), here("sy"))
     sixth = 1.0 / degree
-
-    def active(v, layer):
-        return (norm(v) * gains[2 * layer : 2 * layer + 1] + gains[2 * layer + 1 : 2 * layer + 2]).astype(
-            jnp.bfloat16
-        )
 
     top, bottom = sorted_by("sx", far_row, near_row)
     west, east = sorted_by("sy", far_column, near_column)
@@ -217,25 +244,31 @@
         ring[at : at + held.shape[0]] = counted(index, 0, ALL, degree)
         at += held.shape[0]
 
-    def rest(total, part, layer):
-        hidden = jax.nn.silu(part + dot(total, w_nbr[layer])).astype(jnp.bfloat16)
-        return dot(hidden, w_out[layer])
-
-    rim_first[...] = active(rim[...], 0)
+    rim_first[...] = active(rim[...], gains, 0).astype(jnp.bfloat16)
     near = slice(0, OUT - OWN)
-    own = slice(0, OWN)
-    total[own] = ((own_sum[...] + dot(links[:, OWN:], rim_first[near])) * sixth).astype(jnp.bfloat16)
-    total[OWN:] = (
+    ended = slice(0, 2 * EAST)
+    total[ended] = ((end_sum[...] + dot(end_links[...], rim_first[near])) * sixth).astype(jnp.bfloat16)
+    total[2 * EAST :] = (
         (dot(ring[:, :OWN], first[...]) + dot(ring[:, OWN:], rim_first[...])) * sixth
     ).astype(jnp.bfloat16)
-    part[own] = own_part[...]
-    part[OWN:] = dot(rim_first[near], w_self[0])
-    v = rest(total[...], part[...], 0)
-    part[own] = x[...].astype(jnp.float32) + v[own]
-    part[OWN:] = rim[near] + v[OWN:]
-    second[...] = active(part[...], 1)
-    total[own] = (dot(links[...], second[...]) * sixth).astype(jnp.bfloat16)
-    v = part[own] + rest(total[own], dot(second[own], w_self[1]), 1)
+    part[ended] = end_part[...]
+    part[2 * EAST :] = dot(rim_first[near], w_self[0])
+    v = rest(total[...], part[...], w_nbr, w_out, 0)
+    own = slice(0, OWN)
+    column = slice(2, 2 + EAST)
+    v_ends = v[ended] + jnp.concatenate([sides[0, column], sides[1, column]], axis=0)
+    second[OWN:] = active(v[2 * EAST :] + rim[near], gains, 1).astype(jnp.bfloat16)
+    a_ends = active(v_ends, gains, 1)
+
+    for out, new in ((x1, v_ends), (a1, a_ends)):
+        for tile in range(out.shape[0]):
+            for side, place_in in enumerate((0, NORTH - 1)):
+                out[tile, pl.ds(place_in, EAST, stride=NORTH)] = new[
+                    side * EAST : (side + 1) * EAST, tile * LANES : (tile + 1) * LANES
+                ]
+    second[own] = joined(a1).astype(jnp.bfloat16)
+    sums = (dot(links[...], second[...]) * sixth).astype(jnp.bfloat16)
+    v = joined(x1) + rest(sums, dot(second[own], w_self[1]), w_nbr, w_out, 1)
     value = dot(norm(v).astype(jnp.bfloat16), w_dec[...]).astype(jnp.bfloat16)
     preds[...] = value
     sent[...] = value
@@ -296,7 +329,7 @@
                 pl.BlockSpec(slots.shape, lambda i: (0, 0, 0)),
             ],
             out_specs=(pl.BlockSpec((3 * NORTH, width), lambda i: (0, 0)),) * 2,
-            compiler_params=limits(60),
+            compiler_params=pltpu.CompilerParams(vmem_limit_bytes=55104 << 10),
             name="rows_out",
         )(x, x, slots),
         "sx",
@@ -317,47 +350,60 @@
         out_specs=vmem,
         scratch_shapes=[pltpu.VMEM((2, PAD, LANES), jnp.float32)],
         compiler_params=limits(8),
-        cost_estimate=cost(1 << 20, 1 << 24),
+        cost_estimate=cost(1 << 20, 1 << 25),
         name="collect",
     )(x, coded)
 
     sent = pl.pallas_call(
         columns_out,
         out_shape=(like((SIDE, width)),) * 2,
-        in_specs=[vmem] * 3,
+        in_specs=[pl.BlockSpec(memory_space=pl.ANY)] + [vmem] * 3,
         out_specs=(vmem,) * 2,
         scratch_shapes=[pltpu.VMEM((2, SIDE, width), jnp.float32)],
         compiler_params=limits(8),
+        cost_estimate=cost(1 << 20, 1 << 25),
         name="columns_out",
-    )(sides, far_row, near_row)
+    )(w_out, sides, far_row, near_row)
     far_column, near_column = swap(*sent, "sy")
 
-    first, links, gains, own_sum, own_part = pl.pallas_call(
+    halves = like((2 * EAST, width), jnp.float32)
+    whole = like((width // LANES, OWN, LANES), jnp.float32)
+    first, links, gains, end_links, end_sum, end_part, x1, a1 = pl.pallas_call(
         functools.partial(prepare, degree),
         out_shape=(
             like((OWN, width)),
             like((OWN, OUT)),
             like((2 * layers, width), jnp.float32),
-            like((OWN, width), jnp.float32),
-            like((OWN, width), jnp.float32),
+            like((2 * EAST, OUT - OWN)),
+            halves,
+            halves,
+            whole,
+            whole,
         ),
-        in_specs=[vmem] * 6 + [pl.BlockSpec(memory_space=pl.ANY)],
-        out_specs=(vmem,) * 5,
+        in_specs=[vmem] * 10 + [pl.BlockSpec(memory_space=pl.ANY)],
+        out_specs=(vmem,) * 8,
+        scratch_shapes=[
+            pltpu.VMEM((OWN, width), jnp.float32),
+            pltpu.VMEM((OWN, width), jnp.float32),
+            pltpu.VMEM((OUT - OWN, width), jnp.bfloat16),
+        ],
         compiler_params=limits(16),
         cost_estimate=cost(1 << 24, 1 << 25),
         name="prepare",
-    )(x, coded, noises, w_scale, w_shift, w_self, sent[1])
-
-    preds, shares = pl.pallas_call(
+    )(x, coded, noises, w_scale, w_shift, w_self, w_nbr, w_out, far_row, near_row, sent[1])
+
+    busy = 2 * EAST + OUT - OWN
+    preds, shares, _, _ = pl.pallas_call(
         functools.partial(advance, sizes, degree),
-        out_shape=(like((OWN, variables)),) * 2,
-        in_specs=[vmem] * 14,
-        out_specs=(vmem,) * 2,
+        out_shape=(like((OWN, variables)),) * 2 + (whole,) * 2,
+        in_specs=[vmem] * 17,
+        out_specs=(vmem,) * 4,
+        input_output_aliases={6: 2, 7: 3},
         scratch_shapes=[
             pltpu.VMEM((ALL - OWN, width), jnp.bfloat16),
             pltpu.VMEM((OUT, width), jnp.bfloat16),
-            pltpu.VMEM((OUT, width), jnp.bfloat16),
-            pltpu.VMEM((OUT, width), jnp.float32),
+            pltpu.VMEM((busy, width), jnp.bfloat16),
+            pltpu.VMEM((busy, width), jnp.float32),
             pltpu.VMEM((ALL - OWN, width), jnp.float32),
             pltpu.VMEM((OUT - OWN, ALL), jnp.bfloat16),
         ],
@@ -365,8 +411,8 @@
         cost_estimate=cost(1 << 31, 1 << 23),
         name="advance",
     )(
-        x, links, gains, own_sum, own_part, far_row, near_row, far_column, near_column,
-        w_self, w_nbr, w_out, w_dec, first,
+        first, links, gains, end_links, end_sum, end_part, x1, a1, sides,
+        far_row, near_row, far_column, near_column, w_self, w_nbr, w_out, w_dec,
     )
 
     members = lax.axis_size("member")

time: 57.8 us -> 55.5 us (0.960)
  the two profiles are of different devices: /device:TPU:134 before, /device:TPU:192 now
where the time goes in v4:
time: 55.5 us; the launch traced here: 55.2 us
  blocking collectives  27.6 us (50%)
  starting transfers between devices  15.6 us (28%)
  Pallas kernels  8.17 us (15%)
  waiting for transfers between devices  1.95 us (4%)
  between operations  0.85 us (2%)
  other arithmetic  0.82 us (1%)
    all_to_all x1, blocking collectives, local(): lax.all_to_all(shares.reshape(members, share, variables), 'member', 0, 0)  16.1 us
    all_to_all x1, blocking collectives, local(): scores = lax.all_to_all(copies, 'member', 0, 0).astype(jnp.float32)  11.5 us
    ppermute x2, starting transfers between devices, swap(): lax.ppermute(near, axis, sum(pairs[0::2], []))  8.78 us
    ppermute x2, starting transfers between devices, swap(): lax.ppermute(far, axis, sum(pairs[1::2], []))  6.84 us
    pallas_call x1, Pallas kernels, local(): pl.pallas_call(functools.partial(advance, sizes, degree), out_shape=(like...  4.12 us
    pallas_call x1, Pallas kernels, local(): pl.pallas_call(functools.partial(prepare, degree), out_shape=(like((OWN,...  2.62 us
    ppermute x2, waiting for transfers between devices, swap(): lax.ppermute(near, axis, sum(pairs[0::2], []))  1.94 us
  transfers between devices with their start and end apart: 4, of which 2 were waited for; matrix products, arithmetic and copies ran while one was open for 1% of the time, Pallas kernels for 5%

profile of v4, /device:TPU:192, one launch (start us, length us, event | category | flops | bytes accessed | tf_op | source)
XLA Modules:
  0.0 55.2 jit_solution(13320301520663061439)
XLA Ops:
  0.6 0.0 copy-start.9
  0.6 0.0 copy-start
  0.7 0.0 copy-start.4
  0.7 0.0 copy-start.5
  0.7 1.0 %rows_out.1 = (bf16[48,512]{1,0:T(8,128)(2,1)S(1)}, bf16[48,512]{1,0:T(8,128)(2,1)S(1)}) custom-call(bf16[512,512]{1,0:T(8,128)(2,1)} %bitcast.8, bf16[512,512]{1,0:T(8,128)(2,1)} %bitcast.9, s32[6,16,32]{2,1,0:T(8,128)} %bitcast.17), custom_call_target="tpu_custom_call" | custom-call | tf_op jit(solution)/shard_map/rows_out/pallas_call | solution.py:322
  1.7 0.0 copy-start.1
  1.7 2.1 %collective-permute-start = (bf16[48,512]{1,0:T(8,128)(2,1)S(1)}, bf16[48,512]{1,0:T(8,128)(2,1)S(1)}, u32[]{:S(2)}, u32[]{:S(2)}) collective-permute-start(bf16[48,512]{1,0:T(8,128)(2,1)S(1)} %get-tuple-element.16), channel_id=1, source_target_pairs={{8,16},{16,8},{24,32},{32,24},{40,48},{48,40},{9,17},{17,9},{25,33... | collective-permute-start | bytes 147464 | tf_op jit(solution)/shard_map/ppermute | solution.py:297
  3.8 6.5 %collective-permute-start.1 = (bf16[48,512]{1,0:T(8,128)(2,1)S(1)}, bf16[48,512]{1,0:T(8,128)(2,1)S(1)}, u32[]{:S(2)}, u32[]{:S(2)}) collective-permute-start(bf16[48,512]{1,0:T(8,128)(2,1)S(1)} %get-tuple-element.17), channel_id=1, source_target_pairs={{0,8},{8,0},{16,24},{24,16},{32,40},{40,32},{48,56},{56,48},{1,9},... | collective-permute-start | bytes 147464 | tf_op jit(solution)/shard_map/ppermute | solution.py:298
  10.3 0.0 copy-done.9
  10.3 0.1 multiply_add_fusion
  10.4 0.2 copy.14
  10.6 0.0 copy-done
  10.6 0.0 copy-start.3
  10.6 0.2 collect.1.sides
  10.9 0.0 copy-start.2
  10.9 0.0 collective-permute-done.far_row
  10.9 0.2 collective-permute-done.1.near_row
  11.1 0.0 copy-done.1
  11.1 0.1 columns_out.1
  11.2 0.0 copy-start.7
  11.2 4.8 %collective-permute-start.2 = (bf16[96,512]{1,0:T(8,128)(2,1)S(1)}, bf16[96,512]{1,0:T(8,128)(2,1)S(1)}, u32[]{:S(2)}, u32[]{:S(2)}) collective-permute-start(bf16[96,512]{1,0:T(8,128)(2,1)S(1)} %get-tuple-element.27), channel_id=1, source_target_pairs={{1,2},{2,1},{3,4},{4,3},{5,6},{6,5},{9,10},{10,9},{11,12},{12,11},... | collective-permute-start | bytes 294920 | tf_op jit(solution)/shard_map/ppermute | solution.py:297
  16.0 0.0 copy-start.8
  16.0 2.3 %collective-permute-start.3 = (bf16[96,512]{1,0:T(8,128)(2,1)S(1)}, bf16[96,512]{1,0:T(8,128)(2,1)S(1)}, u32[]{:S(2)}, u32[]{:S(2)}) collective-permute-start(bf16[96,512]{1,0:T(8,128)(2,1)S(1)} %get-tuple-element.18.sent), channel_id=1, source_target_pairs={{0,1},{1,0},{2,3},{3,2},{4,5},{5,4},{6,7},{7,6},{8,9},{9,8},{10,11... | collective-permute-start | bytes 294920 | tf_op jit(solution)/shard_map/ppermute | solution.py:298
  18.3 0.0 copy-done.4
  18.3 0.0 copy-done.5
  18.3 0.0 copy-done.3
  18.3 0.0 copy-done.2
  18.3 0.0 copy-done.7
  18.3 2.6 %prepare.1 = (bf16[512,512]{1,0:T(8,128)(2,1)S(1)}, bf16[512,640]{1,0:T(8,128)(2,1)S(1)}, f32[4,512]{1,0:T(4,128)S(1)}, bf16[64,128]{1,0:T(8,128)(2,1)S(1)}, f32...) custom-call(bf16[512,512]{1,0:T(8,128)(2,1)S(1)} %bitcast.11, ...), custom_call_target="tpu_custom_call" | custom-call | flops 16777216 | bytes 33554432 | tf_op jit(solution)/shard_map/prepare/pallas_call | solution.py:371
  21.0 0.0 collective-permute-done.2.far_column
  21.0 1.7 %collective-permute-done.3.near_column = bf16[96,512]{1,0:T(8,128)(2,1)S(1)} collective-permute-done((bf16[96,512]{1,0:T(8,128)(2,1)S(1)}, bf16[96,512]{1,0:T(8,128)(2,1)S(1)}, u32[]{:S(2)}, u32[]{:S(2)}) %collective-permute-start.3) | collective-permute-done | bytes 98336 | tf_op jit(solution)/shard_map/ppermute | solution.py:298
  22.7 0.0 copy-done.8
  22.7 4.1 %advance.1 = (bf16[512,128]{1,0:T(8,128)(2,1)}, bf16[512,128]{1,0:T(8,128)(2,1)S(1)}, f32[4,512,128]{2,1,0:T(8,128)S(1)}, f32[4,512,128]{2,1,0:T(8,128)S(1)}) custom-call(bf16[512,512]{1,0:T(8,128)(2,1)S(1)} %get-tuple-element.19.first, bf16[512,640]{1,0:T(8,128)(2,1)S(1)} %get-tuple-element.20.links, ...), custom_call_target="tpu_custom_call", output_to_operand_aliasing={{2}: (6, {}), {3}: (7, {})} | custom-call | flops 2147483648 | bytes 8388608 | tf_op jit(solution)/shard_map/advance/pallas_call | solution.py:396
  26.8 0.0 copy-start.6
  26.8 16.1 %all_to_all.10.mine = bf16[8,64,128]{2,1,0:T(8,128)(2,1)S(1)} all-to-all(bf16[8,64,128]{2,1,0:T(8,128)(2,1)S(1)} %bitcast.15), channel_id=1, replica_groups=mesh['member'=8,'sx'=8,'sy'=8] {'member'}, dimensions={0} | all-to-all | bytes 262144 | tf_op jit(solution)/shard_map/all_to_all | solution.py:420
  42.9 0.0 copy-done.6
  42.9 0.1 score_share.1
  43.0 11.5 %all_to_all.11 = bf16[8,64,128]{2,1,0:T(8,128)(2,1)S(1)} all-to-all(bf16[8,64,128]{2,1,0:T(8,128)(2,1)S(1)} %score_share.1), channel_id=1, replica_groups=mesh['member'=8,'sx'=8,'sy'=8] {'member'}, dimensions={0} | all-to-all | bytes 262144 | tf_op jit(solution)/shard_map/all_to_all | solution.py:429
  54.5 0.7 %convert.1 = f32[32,16,128]{2,1,0:T(8,128)} convert(bf16[32,16,128]{2,1,0:T(8,128)(2,1)S(1)} %bitcast.16) | non-fusion elementwise | flops 65536 | bytes 393216 | tf_op jit(solution)/shard_map/reshape | solution.py:430
  (1 shorter events, 0.0 us)
Async XLA Ops:
  0.6 9.7 %copy-start.9 = (s32[32,16,6]{0,1,2:T(8,128)S(1)}, s32[32,16,6]{0,1,2:T(8,128)}, u32[]{:S(2)}) copy-start(s32[32,16,6]{0,1,2:T(8,128)} %param.12) | copy-start | bytes 36868
  0.6 10.0 %copy-start = (bf16[1,32,16,512]{3,2,1,0:T(8,128)(2,1)S(1)}, bf16[1,32,16,512]{3,2,1,0:T(8,128)(2,1)}, u32[]{:S(2)}) copy-start(bf16[1,32,16,512]{3,2,1,0:T(8,128)(2,1)} %param.10) | copy-start | bytes 1572868
  0.7 17.6 %copy-start.4 = (f32[2,32,512]{2,1,0:T(8,128)S(1)}, f32[2,32,512]{2,1,0:T(8,128)}, u32[]{:S(2)}) copy-start(f32[2,32,512]{2,1,0:T(8,128)} %w_scale.1) | copy-start | bytes 393220
  0.7 17.6 %copy-start.5 = (f32[2,32,512]{2,1,0:T(8,128)S(1)}, f32[2,32,512]{2,1,0:T(8,128)}, u32[]{:S(2)}) copy-start(f32[2,32,512]{2,1,0:T(8,128)} %w_shift.1) | copy-start | bytes 393220
  1.7 9.4 %copy-start.1 = (bf16[2,512,512]{2,1,0:T(8,128)(2,1)S(1)}, bf16[2,512,512]{2,1,0:T(8,128)(2,1)}, u32[]{:S(2)}) copy-start(bf16[2,512,512]{2,1,0:T(8,128)(2,1)} %w_out.5) | copy-start | bytes 3145732
  1.7 9.2 %collective-permute-start = (bf16[48,512]{1,0:T(8,128)(2,1)S(1)}, bf16[48,512]{1,0:T(8,128)(2,1)S(1)}, u32[]{:S(2)}, u32[]{:S(2)}) collective-permute-start(bf16[48,512]{1,0:T(8,128)(2,1)S(1)} %get-tuple-element.16), channel_id=1, source_target_pairs={{8,16},{16,8},{24,32},{32,24},{40,48},{48,40},{9,17},{17,9},{25,33... | collective-permute-start | bytes 147464 | tf_op jit(solution)/shard_map/ppermute | solution.py:297
  3.8 7.4 %collective-permute-start.1 = (bf16[48,512]{1,0:T(8,128)(2,1)S(1)}, bf16[48,512]{1,0:T(8,128)(2,1)S(1)}, u32[]{:S(2)}, u32[]{:S(2)}) collective-permute-start(bf16[48,512]{1,0:T(8,128)(2,1)S(1)} %get-tuple-element.17), channel_id=1, source_target_pairs={{0,8},{8,0},{16,24},{24,16},{32,40},{40,32},{48,56},{56,48},{1,9},... | collective-permute-start | bytes 147464 | tf_op jit(solution)/shard_map/ppermute | solution.py:298
  10.6 7.7 %copy-start.3 = (bf16[2,512,512]{2,1,0:T(8,128)(2,1)S(1)}, bf16[2,512,512]{2,1,0:T(8,128)(2,1)}, u32[]{:S(2)}) copy-start(bf16[2,512,512]{2,1,0:T(8,128)(2,1)} %w_nbr.3) | copy-start | bytes 3145732
  10.9 7.5 %copy-start.2 = (bf16[2,512,512]{2,1,0:T(8,128)(2,1)S(1)}, bf16[2,512,512]{2,1,0:T(8,128)(2,1)}, u32[]{:S(2)}) copy-start(bf16[2,512,512]{2,1,0:T(8,128)(2,1)} %w_self.3) | copy-start | bytes 3145732
  11.2 7.1 %copy-start.7 = (f32[1,32]{1,0:T(1,128)S(1)}, f32[1,32]{1,0:T(1,128)}, u32[]{:S(2)}) copy-start(f32[1,32]{1,0:T(1,128)} %noise.1) | copy-start | bytes 388
  11.2 9.8 %collective-permute-start.2 = (bf16[96,512]{1,0:T(8,128)(2,1)S(1)}, bf16[96,512]{1,0:T(8,128)(2,1)S(1)}, u32[]{:S(2)}, u32[]{:S(2)}) collective-permute-start(bf16[96,512]{1,0:T(8,128)(2,1)S(1)} %get-tuple-element.27), channel_id=1, source_target_pairs={{1,2},{2,1},{3,4},{4,3},{5,6},{6,5},{9,10},{10,9},{11,12},{12,11},... | collective-permute-start | bytes 294920 | tf_op jit(solution)/shard_map/ppermute | solution.py:297
  16.0 6.7 %copy-start.8 = (bf16[512,128]{1,0:T(8,128)(2,1)S(1)}, bf16[512,128]{1,0:T(8,128)(2,1)}, u32[]{:S(2)}) copy-start(bf16[512,128]{1,0:T(8,128)(2,1)} %w_dec.1) | copy-start | bytes 393220
  16.0 6.7 %collective-permute-start.3 = (bf16[96,512]{1,0:T(8,128)(2,1)S(1)}, bf16[96,512]{1,0:T(8,128)(2,1)S(1)}, u32[]{:S(2)}, u32[]{:S(2)}) collective-permute-start(bf16[96,512]{1,0:T(8,128)(2,1)S(1)} %get-tuple-element.18.sent), channel_id=1, source_target_pairs={{0,1},{1,0},{2,3},{3,2},{4,5},{5,4},{6,7},{7,6},{8,9},{9,8},{10,11... | collective-permute-start | bytes 294920 | tf_op jit(solution)/shard_map/ppermute | solution.py:298
  26.8 16.1 %copy-start.6 = (bf16[32,16,128]{2,1,0:T(8,128)(2,1)S(1)}, bf16[32,16,128]{2,1,0:T(8,128)(2,1)}, u32[]{:S(2)}) copy-start(bf16[32,16,128]{2,1,0:T(8,128)(2,1)} %param.13) | copy-start | bytes 393220

commit v5 on v4

--- a/solution.py
+++ b/solution.py
@@ -59,12 +59,16 @@
     return jnp.where(real, place(to_row, to_column), -1)
 
 
-def counted(index, at, width, degree):
-    lanes = lax.broadcasted_iota(jnp.int32, (index.shape[0], width), 1) + at
+def counted(slots, at, width):
+    lanes = lax.broadcasted_iota(jnp.int32, (slots[0].shape[0], width), 1) + at
     total = jnp.zeros(lanes.shape, jnp.float32)
-    for slot in range(degree):
-        total = total + jnp.where(lanes == index[:, slot : slot + 1], 1.0, 0.0)
+    for slot in slots:
+        total = total + jnp.where(lanes == slot, 1.0, 0.0)
     return total.astype(jnp.bfloat16)
+
+
+def apart(index, degree):
+    return [index[:, slot : slot + 1] for slot in range(degree)]
 
 
 def norm(x):
@@ -102,6 +106,13 @@
     return jnp.where(odd, near, far), jnp.where(odd, far, near)
 
 
+def by_row(slots, column, turned):
+    turned[...] = jnp.zeros(turned.shape, jnp.float32)
+    for slot in range(slots.shape[0]):
+        turned[slot : slot + 1, :EAST] = slots[slot, column : column + 1].astype(jnp.float32)
+    return turned[...].T[:EAST]
+
+
 def collect(degree, x, coded, sides, named):
     sides[...] = jnp.zeros(sides.shape, jnp.float32)
     named[...] = jnp.zeros(named.shape, jnp.float32)
@@ -115,7 +126,7 @@
         for side, (near, far) in enumerate(((0, 1), (NORTH - 1, NORTH - 2))):
             sides[side, at : at + lines] = grid[:, near]
             sides[side, FAR + at : FAR + at + lines] = grid[:, far]
-            named[side, at : at + lines, :degree] = (held[:, near] >> 10).astype(jnp.float32)
+            named[side, at : at + lines, :degree] = (held[:, near] & (CODE - 1)).astype(jnp.float32)
     for side in range(2):
         for part in range(PAD // 16):
             sides[side, CODED:FAR, part * LANES : (part + 1) * LANES] = named[
@@ -146,10 +157,29 @@
     return jnp.concatenate([tiles[tile] for tile in range(tiles.shape[0])], axis=1)
 
 
+def own_neighbours(arrived, row0, column0, sizes, degree):
+    if column0 == 0:
+        held = arrived[2 * NORTH : 3 * NORTH, :LANES]
+    else:
+        held = jnp.concatenate(
+            [arrived[CODED:FAR, i * LANES : (i + 1) * LANES] for i in range(PAD // 16)], axis=0
+        )
+    held = held[:, :degree].astype(jnp.int32)
+    step = lax.broadcasted_iota(jnp.int32, held.shape, 0)
+    if column0 == 0:
+        row, column = (jnp.full(held.shape, row0, jnp.int32), step)
+    else:
+        row, column = (row0 + step, jnp.full(held.shape, column0, jnp.int32))
+    index = neighbours(held, row, column, (here("sx"), here("sy")), sizes)
+    return counted(apart(index, degree), 0, ALL)
+
+
 def prepare(
-    degree, x, coded, noise, w_scale, w_shift, w_self, w_nbr, w_out, far_row, near_row, sent,
-    first, links, gains, end_links, end_sum, end_part, x1, a1, own_sum, own_part, rim,
+    sizes, x, slots, noise, w_scale, w_shift, w_self, w_nbr, w_out, far_row, near_row, sent,
+    first, gains, late_links, end_links, end_sum, end_part, x1, sum1, part1,
+    rim_rows, ring_rows, rim_x, links, own_sum, own_part, rim, index, turned,
 ):
+    degree = slots.shape[0]
     for layer in range(w_scale.shape[0]):
         for at, w in enumerate((w_scale, w_shift)):
             gains[2 * layer + at : 2 * layer + at + 1] = (1.0 - at) + jnp.dot(
@@ -158,30 +188,58 @@
             )
     links[...] = jnp.zeros(links.shape, jnp.bfloat16)
     first[...] = active(x[...].astype(jnp.float32), gains, 0).astype(jnp.bfloat16)
+    own_part[...] = dot(first[...], w_self[0])
+
+    found = neighbours(
+        slots[...],
+        lax.broadcasted_iota(jnp.int32, slots.shape, 2),
+        lax.broadcasted_iota(jnp.int32, slots.shape, 1),
+        (here("sx"), here("sy")),
+        sizes,
+    )
+    index[0] = found
+    line, step = (found // NORTH, found % NORTH)
+    end = jnp.where(step == 0, line, jnp.where(step == NORTH - 1, EAST + line, -1))
+    index[1] = jnp.where((found >= 0) & (found < OWN), end, -1)
     for row in range(EAST):
         span = slice(row * NORTH, (row + 1) * NORTH)
-        index = (coded[span] & (CODE - 1)) - 1
+        named, ended = (
+            [index[which, slot, :, row : row + 1] for slot in range(degree)] for which in (0, 1)
+        )
         tiles = {max(row - 1, 0) * NORTH // LANES, min(row + 1, EAST - 1) * NORTH // LANES}
         for tile in sorted(tiles) + [OWN // LANES]:
-            links[span, tile * LANES : (tile + 1) * LANES] = counted(
-                index, tile * LANES, LANES, degree
-            )
-    end_links[...] = counted(ends((coded[...] & (CODE - 1)) - 1), OWN, OUT - OWN, degree)
-
-    top, bottom = sorted_by("sx", far_row, near_row)
-    rim[: 2 * NORTH] = active(
-        jnp.concatenate([top[NORTH : 2 * NORTH], bottom[:NORTH]], axis=0), gains, 0
-    ).astype(jnp.bfloat16)
-    rim[2 * NORTH :] = jnp.zeros((rim.shape[0] - 2 * NORTH, rim.shape[1]), jnp.bfloat16)
-    own_part[...] = dot(first[...], w_self[0])
+            links[span, tile * LANES : (tile + 1) * LANES] = counted(named, tile * LANES, LANES)
+        late_links[span, LANES:] = counted(ended, 0, LANES)
+    late_links[:, :LANES] = links[:, OWN:]
+    for side, column in enumerate((0, NORTH - 1)):
+        ends_found = by_row(index.at[0], column, turned.at[side]).astype(jnp.int32)
+        end_links[side * EAST : (side + 1) * EAST] = counted(
+            apart(ends_found, degree), OWN, OUT - OWN
+        )
+
     own_sum[...] = dot(links[:, :OWN], first[...])
     end_part[...] = ends(own_part[...])
     end_sum[...] = ends(own_sum[...])
+    top, bottom = sorted_by("sx", far_row, near_row)
+    nearer = jnp.concatenate([top[NORTH : 2 * NORTH], bottom[:NORTH]], axis=0)
+    rim_x[...] = nearer
+    rim_rows[: 2 * NORTH] = active(nearer, gains, 0).astype(jnp.bfloat16)
+    rim_rows[2 * NORTH :] = active(
+        jnp.concatenate([top[:NORTH], bottom[NORTH : 2 * NORTH]], axis=0), gains, 0
+    ).astype(jnp.bfloat16)
+    rim[: 2 * NORTH] = rim_rows[: 2 * NORTH]
+    rim[2 * NORTH :] = jnp.zeros((rim.shape[0] - 2 * NORTH, rim.shape[1]), jnp.bfloat16)
     total = own_sum[...] + dot(links[:, OWN:], rim[...])
     total = (total * (1.0 / degree)).astype(jnp.bfloat16)
     v = x[...].astype(jnp.float32) + rest(total, own_part[...], w_nbr, w_out, 0)
     split(x1, v)
-    split(a1, active(v, gains, 1))
+    step = lax.broadcasted_iota(jnp.int32, (OWN, 1), 0) % NORTH
+    inner = (step > 0) & (step < NORTH - 1)
+    a1 = jnp.where(inner, active(v, gains, 1), 0.0).astype(jnp.bfloat16)
+    sum1[...] = dot(links[:, :OWN], a1)
+    split(part1, dot(a1, w_self[1]))
+    ring_rows[:NORTH] = own_neighbours(top, -1, 0, sizes, degree)
+    ring_rows[NORTH:] = own_neighbours(bottom, EAST, 0, sizes, degree)
 
 
 def columns_out(w_out, sides, far_row, near_row, far_out, near_out, lines):
@@ -206,46 +264,25 @@
 
 
 def advance(
-    sizes, degree, first, links, gains, end_links, end_sum, end_part, old_x1, old_a1, sides,
-    far_row, near_row, far_column, near_column, w_self, w_nbr, w_out, w_dec,
-    preds, sent, x1, a1, rim_first, second, total, part, rim, ring,
+    sizes, degree, first, gains, late_links, end_links, end_sum, end_part, old_x1, sum1, old_part1,
+    rim_rows, ring_rows, rim_x, sides, far_column, near_column, w_self, w_nbr, w_out, w_dec,
+    preds, sent, x1, part1, rim_first, late, total, part, ring,
 ):
-    place_here = (here("sx"), here("sy"))
     sixth = 1.0 / degree
-
-    top, bottom = sorted_by("sx", far_row, near_row)
     west, east = sorted_by("sy", far_column, near_column)
+    nearer = jnp.concatenate([west[:PAD], east[:PAD]], axis=0)
     gap = jnp.zeros((PAD - SIDE + FAR, west.shape[1]), jnp.float32)
-    rims = (
-        (top[NORTH : 2 * NORTH], bottom[:NORTH], west[:PAD], east[:PAD]),
-        (top[:NORTH], bottom[NORTH : 2 * NORTH], west[FAR:], gap, east[FAR:], gap),
-    )
-    at = 0
-    for ring_parts in rims:
-        for nodes in ring_parts:
-            rim[at : at + nodes.shape[0]] = nodes
-            at += nodes.shape[0]
-
-    at = 0
-    for arrived, row0, column0 in ((top, -1, 0), (bottom, EAST, 0), (west, -2, -1), (east, -2, NORTH)):
-        if column0 == 0:
-            held = arrived[2 * NORTH : 3 * NORTH, :LANES]
-        else:
-            held = jnp.concatenate(
-                [arrived[CODED:FAR, i * LANES : (i + 1) * LANES] for i in range(PAD // 16)], axis=0
-            )
-        held = held[:, :degree].astype(jnp.int32)
-        step = lax.broadcasted_iota(jnp.int32, held.shape, 0)
-        if column0 == 0:
-            row, column = (jnp.full(held.shape, row0, jnp.int32), step)
-        else:
-            row, column = (row0 + step, jnp.full(held.shape, column0, jnp.int32))
-        index = neighbours(held, row, column, place_here, sizes)
-        ring[at : at + held.shape[0]] = counted(index, 0, ALL, degree)
-        at += held.shape[0]
-
-    rim_first[...] = active(rim[...], gains, 0).astype(jnp.bfloat16)
+    farther = jnp.concatenate([west[FAR:], gap, east[FAR:], gap], axis=0)
     near = slice(0, OUT - OWN)
+    rows = 2 * NORTH
+    rim_first[:rows] = rim_rows[:rows]
+    rim_first[rows : OUT - OWN] = active(nearer, gains, 0).astype(jnp.bfloat16)
+    rim_first[OUT - OWN : OUT - OWN + rows] = rim_rows[rows:]
+    rim_first[OUT - OWN + rows :] = active(farther, gains, 0).astype(jnp.bfloat16)
+    ring[:rows] = ring_rows[...]
+    ring[rows : rows + PAD] = own_neighbours(west, -2, -1, sizes, degree)
+    ring[rows + PAD :] = own_neighbours(east, -2, NORTH, sizes, degree)
+
     ended = slice(0, 2 * EAST)
     total[ended] = ((end_sum[...] + dot(end_links[...], rim_first[near])) * sixth).astype(jnp.bfloat16)
     total[2 * EAST :] = (
@@ -254,21 +291,22 @@
     part[ended] = end_part[...]
     part[2 * EAST :] = dot(rim_first[near], w_self[0])
     v = rest(total[...], part[...], w_nbr, w_out, 0)
-    own = slice(0, OWN)
     column = slice(2, 2 + EAST)
     v_ends = v[ended] + jnp.concatenate([sides[0, column], sides[1, column]], axis=0)
-    second[OWN:] = active(v[2 * EAST :] + rim[near], gains, 1).astype(jnp.bfloat16)
-    a_ends = active(v_ends, gains, 1)
-
-    for out, new in ((x1, v_ends), (a1, a_ends)):
+    v_ring = v[2 * EAST :] + jnp.concatenate([rim_x[...], nearer], axis=0)
+    a_ends = active(v_ends, gains, 1).astype(jnp.bfloat16)
+    late[near] = active(v_ring, gains, 1).astype(jnp.bfloat16)
+    late[OUT - OWN : OUT - OWN + 2 * EAST] = a_ends
+    late[OUT - OWN + 2 * EAST :] = jnp.zeros((LANES - 2 * EAST, late.shape[1]), jnp.bfloat16)
+
+    for out, new in ((x1, v_ends), (part1, dot(a_ends, w_self[1]))):
         for tile in range(out.shape[0]):
             for side, place_in in enumerate((0, NORTH - 1)):
                 out[tile, pl.ds(place_in, EAST, stride=NORTH)] = new[
                     side * EAST : (side + 1) * EAST, tile * LANES : (tile + 1) * LANES
                 ]
-    second[own] = joined(a1).astype(jnp.bfloat16)
-    sums = (dot(links[...], second[...]) * sixth).astype(jnp.bfloat16)
-    v = joined(x1) + rest(sums, dot(second[own], w_self[1]), w_nbr, w_out, 1)
+    sums = ((sum1[...] + dot(late_links[...], late[...])) * sixth).astype(jnp.bfloat16)
+    v = joined(x1) + rest(sums, joined(part1), w_nbr, w_out, 1)
     value = dot(norm(v).astype(jnp.bfloat16), w_dec[...]).astype(jnp.bfloat16)
     preds[...] = value
     sent[...] = value
@@ -335,14 +373,7 @@
         "sx",
     )
 
-    index = neighbours(
-        slots,
-        lax.broadcasted_iota(jnp.int32, slots.shape, 2),
-        lax.broadcasted_iota(jnp.int32, slots.shape, 1),
-        (here("sx"), here("sy")),
-        sizes,
-    )
-    coded = (index + 1 + CODE * slots).transpose(2, 1, 0).reshape(OWN, degree)
+    coded = (slots + CODE * here("sx")).transpose(2, 1, 0).reshape(OWN, degree)
     sides = pl.pallas_call(
         functools.partial(collect, degree),
         out_shape=like((2, SIDE, width), jnp.float32),
@@ -368,51 +399,61 @@
 
     halves = like((2 * EAST, width), jnp.float32)
     whole = like((width // LANES, OWN, LANES), jnp.float32)
-    first, links, gains, end_links, end_sum, end_part, x1, a1 = pl.pallas_call(
-        functools.partial(prepare, degree),
+    square = pltpu.VMEM((OWN, width), jnp.float32)
+    (
+        first, gains, late_links, end_links, end_sum, end_part, x1, sum1, part1,
+        rim_rows, ring_rows, rim_x,
+    ) = pl.pallas_call(
+        functools.partial(prepare, sizes),
         out_shape=(
             like((OWN, width)),
-            like((OWN, OUT)),
             like((2 * layers, width), jnp.float32),
+            like((OWN, 2 * LANES)),
             like((2 * EAST, OUT - OWN)),
             halves,
             halves,
             whole,
+            like((OWN, width), jnp.float32),
             whole,
+            like((4 * NORTH, width)),
+            like((2 * NORTH, ALL)),
+            like((2 * NORTH, width), jnp.float32),
         ),
         in_specs=[vmem] * 10 + [pl.BlockSpec(memory_space=pl.ANY)],
-        out_specs=(vmem,) * 8,
+        out_specs=(vmem,) * 12,
         scratch_shapes=[
-            pltpu.VMEM((OWN, width), jnp.float32),
-            pltpu.VMEM((OWN, width), jnp.float32),
+            pltpu.VMEM((OWN, OUT), jnp.bfloat16),
+            square,
+            square,
             pltpu.VMEM((OUT - OWN, width), jnp.bfloat16),
+            pltpu.VMEM((2,) + slots.shape, jnp.int32),
+            pltpu.VMEM((2, 8, LANES), jnp.float32),
         ],
         compiler_params=limits(16),
         cost_estimate=cost(1 << 24, 1 << 25),
         name="prepare",
-    )(x, coded, noises, w_scale, w_shift, w_self, w_nbr, w_out, far_row, near_row, sent[1])
+    )(x, slots, noises, w_scale, w_shift, w_self, w_nbr, w_out, far_row, near_row, sent[1])
 
     busy = 2 * EAST + OUT - OWN
     preds, shares, _, _ = pl.pallas_call(
         functools.partial(advance, sizes, degree),
         out_shape=(like((OWN, variables)),) * 2 + (whole,) * 2,
-        in_specs=[vmem] * 17,
+        in_specs=[vmem] * 19,
         out_specs=(vmem,) * 4,
-        input_output_aliases={6: 2, 7: 3},
+        input_output_aliases={6: 2, 8: 3},
         scratch_shapes=[
             pltpu.VMEM((ALL - OWN, width), jnp.bfloat16),
-            pltpu.VMEM((OUT, width), jnp.bfloat16),
+            pltpu.VMEM((2 * LANES, width), jnp.bfloat16),
             pltpu.VMEM((busy, width), jnp.bfloat16),
             pltpu.VMEM((busy, width), jnp.float32),
-            pltpu.VMEM((ALL - OWN, width), jnp.float32),
             pltpu.VMEM((OUT - OWN, ALL), jnp.bfloat16),
         ],
         compiler_params=limits(16),
         cost_estimate=cost(1 << 31, 1 << 23),
         name="advance",
     )(
-        first, links, gains, end_links, end_sum, end_part, x1, a1, sides,
-        far_row, near_row, far_column, near_column, w_self, w_nbr, w_out, w_dec,
+        first, gains, late_links, end_links, end_sum, end_part, x1, sum1, part1,
+        rim_rows, ring_rows, rim_x, sides, far_column, near_column, w_self, w_nbr, w_out, w_dec,
     )
 
     members = lax.axis_size("member")

time: 55.5 us -> 54.9 us (0.989)
    pallas_call x1, Pallas kernels: 2.62 us -> 3.3 us  [local(): pl.pallas_call(functools.partial(prepare, sizes), out_shape=(like((OWN, w...]
    pallas_call x1, Pallas kernels: 4.12 us -> 3.52 us  [local(): pl.pallas_call(functools.partial(advance, sizes, degree), out_shape=(like...]
  transfers between devices with their start and end apart: 4 -> 4, of which waited for: 2 -> 2; matrix products, arithmetic and copies ran while one was open for 1% -> 0% of each run, Pallas kernels for 5% -> 6%
where the time goes in v5:
time: 54.9 us; the launch traced here: 54.6 us
  blocking collectives  27.6 us (50%)
  starting transfers between devices  15.5 us (28%)
  Pallas kernels  8.25 us (15%)
  waiting for transfers between devices  1.5 us (3%)
  between operations  0.84 us (2%)
  other arithmetic  0.73 us (1%)
    all_to_all x1, blocking collectives, local(): lax.all_to_all(shares.reshape(members, share, variables), 'member', 0, 0)  16.1 us
    all_to_all x1, blocking collectives, local(): scores = lax.all_to_all(copies, 'member', 0, 0).astype(jnp.float32)  11.5 us
    ppermute x2, starting transfers between devices, swap(): lax.ppermute(near, axis, sum(pairs[0::2], []))  8.78 us
    ppermute x2, starting transfers between devices, swap(): lax.ppermute(far, axis, sum(pairs[1::2], []))  6.71 us
    pallas_call x1, Pallas kernels, local(): pl.pallas_call(functools.partial(advance, sizes, degree), out_shape=(like...  3.52 us
    pallas_call x1, Pallas kernels, local(): pl.pallas_call(functools.partial(prepare, sizes), out_shape=(like((OWN, w...  3.3 us
    ppermute x2, waiting for transfers between devices, swap(): lax.ppermute(near, axis, sum(pairs[0::2], []))  1.5 us
  transfers between devices with their start and end apart: 4, of which 2 were waited for; matrix products, arithmetic and copies ran while one was open for 0% of the time, Pallas kernels for 6%

profile of v5, /device:TPU:192, one launch (start us, length us, event | category | flops | bytes accessed | tf_op | source)
XLA Modules:
  0.0 54.6 jit_solution(15841918637608839372)
XLA Ops:
  0.6 0.0 copy-start.4
  0.6 0.0 copy-start.1
  0.7 0.0 copy-start.6
  0.7 0.0 copy-start.7
  0.7 1.0 %rows_out.1 = (bf16[48,512]{1,0:T(8,128)(2,1)S(1)}, bf16[48,512]{1,0:T(8,128)(2,1)S(1)}) custom-call(bf16[512,512]{1,0:T(8,128)(2,1)} %bitcast.8, bf16[512,512]{1,0:T(8,128)(2,1)} %bitcast.9, s32[6,16,32]{2,1,0:T(8,128)} %bitcast.13), custom_call_target="tpu_custom_call" | custom-call | tf_op jit(solution)/shard_map/rows_out/pallas_call | solution.py:360
  1.7 0.0 copy-start
  1.7 2.1 %collective-permute-start = (bf16[48,512]{1,0:T(8,128)(2,1)S(1)}, bf16[48,512]{1,0:T(8,128)(2,1)S(1)}, u32[]{:S(2)}, u32[]{:S(2)}) collective-permute-start(bf16[48,512]{1,0:T(8,128)(2,1)S(1)} %get-tuple-element.20), channel_id=1, source_target_pairs={{8,16},{16,8},{24,32},{32,24},{40,48},{48,40},{9,17},{17,9},{25,33... | collective-permute-start | bytes 147464 | tf_op jit(solution)/shard_map/ppermute | solution.py:335
  3.8 6.5 %collective-permute-start.1 = (bf16[48,512]{1,0:T(8,128)(2,1)S(1)}, bf16[48,512]{1,0:T(8,128)(2,1)S(1)}, u32[]{:S(2)}, u32[]{:S(2)}) collective-permute-start(bf16[48,512]{1,0:T(8,128)(2,1)S(1)} %get-tuple-element.21), channel_id=1, source_target_pairs={{0,8},{8,0},{16,24},{24,16},{32,40},{40,32},{48,56},{56,48},{1,9},... | collective-permute-start | bytes 147464 | tf_op jit(solution)/shard_map/ppermute | solution.py:336
  10.3 0.0 copy-done.4
  10.3 0.2 copy.14
  10.5 0.0 copy-done.1
  10.5 0.0 copy-start.3
  10.5 0.2 collect.1.sides
  10.8 0.0 copy-start.2
  10.8 0.0 collective-permute-done.far_row
  10.8 0.3 collective-permute-done.1.near_row
  11.1 0.0 copy-done
  11.1 0.1 columns_out.1
  11.2 0.0 copy-start.9
  11.2 4.7 %collective-permute-start.2 = (bf16[96,512]{1,0:T(8,128)(2,1)S(1)}, bf16[96,512]{1,0:T(8,128)(2,1)S(1)}, u32[]{:S(2)}, u32[]{:S(2)}) collective-permute-start(bf16[96,512]{1,0:T(8,128)(2,1)S(1)} %get-tuple-element.35), channel_id=1, source_target_pairs={{1,2},{2,1},{3,4},{4,3},{5,6},{6,5},{9,10},{10,9},{11,12},{12,11},... | collective-permute-start | bytes 294920 | tf_op jit(solution)/shard_map/ppermute | solution.py:335
  15.9 0.0 copy-start.5
  15.9 2.3 %collective-permute-start.3 = (bf16[96,512]{1,0:T(8,128)(2,1)S(1)}, bf16[96,512]{1,0:T(8,128)(2,1)S(1)}, u32[]{:S(2)}, u32[]{:S(2)}) collective-permute-start(bf16[96,512]{1,0:T(8,128)(2,1)S(1)} %get-tuple-element.22.sent), channel_id=1, source_target_pairs={{0,1},{1,0},{2,3},{3,2},{4,5},{5,4},{6,7},{7,6},{8,9},{9,8},{10,11... | collective-permute-start | bytes 294920 | tf_op jit(solution)/shard_map/ppermute | solution.py:336
  18.2 0.0 copy-done.6
  18.2 0.0 copy-done.7
  18.2 0.0 copy-done.3
  18.2 0.0 copy-done.2
  18.2 0.0 copy-done.9
  18.2 3.3 %prepare.1 = (bf16[512,512]{1,0:T(8,128)(2,1)S(1)}, f32[4,512]{1,0:T(4,128)S(1)}, bf16[512,256]{1,0:T(8,128)(2,1)S(1)}, bf16[64,128]{1,0:T(8,128)(2,1)S(1)}, f32...) custom-call(bf16[512,512]{1,0:T(8,128)(2,1)S(1)} %bitcast.11, ...), custom_call_target="tpu_custom_call" | custom-call | flops 16777216 | bytes 33554432 | tf_op jit(solution)/shard_map/prepare/pallas_call | solution.py:406
  21.5 0.0 collective-permute-done.2.far_column
  21.5 1.2 %collective-permute-done.3.near_column = bf16[96,512]{1,0:T(8,128)(2,1)S(1)} collective-permute-done((bf16[96,512]{1,0:T(8,128)(2,1)S(1)}, bf16[96,512]{1,0:T(8,128)(2,1)S(1)}, u32[]{:S(2)}, u32[]{:S(2)}) %collective-permute-start.3) | collective-permute-done | bytes 98336 | tf_op jit(solution)/shard_map/ppermute | solution.py:336
  22.7 0.0 copy-done.5
  22.7 3.5 %advance.1 = (bf16[512,128]{1,0:T(8,128)(2,1)}, bf16[512,128]{1,0:T(8,128)(2,1)S(1)}, f32[4,512,128]{2,1,0:T(8,128)S(1)}, f32[4,512,128]{2,1,0:T(8,128)S(1)}) custom-call(bf16[512,512]{1,0:T(8,128)(2,1)S(1)} %get-tuple-element.23.first, f32[4,512]{1,0:T(4,128)S(1)} %get-tuple-element.24.gains, ...), custom_call_target="tpu_custom_call", output_to_operand_aliasing={{2}: (6, {}), {3}: (8, {})} | custom-call | flops 2147483648 | bytes 8388608 | tf_op jit(solution)/shard_map/advance/pallas_call | solution.py:438
  26.2 0.0 copy-start.8
  26.2 16.1 %all_to_all.10.mine = bf16[8,64,128]{2,1,0:T(8,128)(2,1)S(1)} all-to-all(bf16[8,64,128]{2,1,0:T(8,128)(2,1)S(1)} %bitcast.16), channel_id=1, replica_groups=mesh['member'=8,'sx'=8,'sy'=8] {'member'}, dimensions={0} | all-to-all | bytes 262144 | tf_op jit(solution)/shard_map/all_to_all | solution.py:461
  42.3 0.0 copy-done.8
  42.3 0.1 score_share.1
  42.4 11.5 %all_to_all.11 = bf16[8,64,128]{2,1,0:T(8,128)(2,1)S(1)} all-to-all(bf16[8,64,128]{2,1,0:T(8,128)(2,1)S(1)} %score_share.1), channel_id=1, replica_groups=mesh['member'=8,'sx'=8,'sy'=8] {'member'}, dimensions={0} | all-to-all | bytes 262144 | tf_op jit(solution)/shard_map/all_to_all | solution.py:470
  53.9 0.7 %convert.1 = f32[32,16,128]{2,1,0:T(8,128)} convert(bf16[32,16,128]{2,1,0:T(8,128)(2,1)S(1)} %bitcast.17) | non-fusion elementwise | flops 65536 | bytes 393216 | tf_op jit(solution)/shard_map/reshape | solution.py:471
  (1 shorter events, 0.0 us)
Async XLA Ops:
  0.6 9.6 %copy-start.4 = (s32[32,16,6]{0,1,2:T(8,128)S(1)}, s32[32,16,6]{0,1,2:T(8,128)}, u32[]{:S(2)}) copy-start(s32[32,16,6]{0,1,2:T(8,128)} %param.12) | copy-start | bytes 36868
  0.6 9.9 %copy-start.1 = (bf16[1,32,16,512]{3,2,1,0:T(8,128)(2,1)S(1)}, bf16[1,32,16,512]{3,2,1,0:T(8,128)(2,1)}, u32[]{:S(2)}) copy-start(bf16[1,32,16,512]{3,2,1,0:T(8,128)(2,1)} %param.10) | copy-start | bytes 1572868
  0.7 17.5 %copy-start.6 = (f32[2,32,512]{2,1,0:T(8,128)S(1)}, f32[2,32,512]{2,1,0:T(8,128)}, u32[]{:S(2)}) copy-start(f32[2,32,512]{2,1,0:T(8,128)} %w_scale.1) | copy-start | bytes 393220
  0.7 17.5 %copy-start.7 = (f32[2,32,512]{2,1,0:T(8,128)S(1)}, f32[2,32,512]{2,1,0:T(8,128)}, u32[]{:S(2)}) copy-start(f32[2,32,512]{2,1,0:T(8,128)} %w_shift.1) | copy-start | bytes 393220
  1.7 9.4 %copy-start = (bf16[2,512,512]{2,1,0:T(8,128)(2,1)S(1)}, bf16[2,512,512]{2,1,0:T(8,128)(2,1)}, u32[]{:S(2)}) copy-start(bf16[2,512,512]{2,1,0:T(8,128)(2,1)} %w_out.5) | copy-start | bytes 3145732
  1.7 9.1 %collective-permute-start = (bf16[48,512]{1,0:T(8,128)(2,1)S(1)}, bf16[48,512]{1,0:T(8,128)(2,1)S(1)}, u32[]{:S(2)}, u32[]{:S(2)}) collective-permute-start(bf16[48,512]{1,0:T(8,128)(2,1)S(1)} %get-tuple-element.20), channel_id=1, source_target_pairs={{8,16},{16,8},{24,32},{32,24},{40,48},{48,40},{9,17},{17,9},{25,33... | collective-permute-start | bytes 147464 | tf_op jit(solution)/shard_map/ppermute | solution.py:335
  3.8 7.4 %collective-permute-start.1 = (bf16[48,512]{1,0:T(8,128)(2,1)S(1)}, bf16[48,512]{1,0:T(8,128)(2,1)S(1)}, u32[]{:S(2)}, u32[]{:S(2)}) collective-permute-start(bf16[48,512]{1,0:T(8,128)(2,1)S(1)} %get-tuple-element.21), channel_id=1, source_target_pairs={{0,8},{8,0},{16,24},{24,16},{32,40},{40,32},{48,56},{56,48},{1,9},... | collective-permute-start | bytes 147464 | tf_op jit(solution)/shard_map/ppermute | solution.py:336
  10.5 7.7 %copy-start.3 = (bf16[2,512,512]{2,1,0:T(8,128)(2,1)S(1)}, bf16[2,512,512]{2,1,0:T(8,128)(2,1)}, u32[]{:S(2)}) copy-start(bf16[2,512,512]{2,1,0:T(8,128)(2,1)} %w_nbr.3) | copy-start | bytes 3145732
  10.8 7.4 %copy-start.2 = (bf16[2,512,512]{2,1,0:T(8,128)(2,1)S(1)}, bf16[2,512,512]{2,1,0:T(8,128)(2,1)}, u32[]{:S(2)}) copy-start(bf16[2,512,512]{2,1,0:T(8,128)(2,1)} %w_self.3) | copy-start | bytes 3145732
  11.2 7.0 %copy-start.9 = (f32[1,32]{1,0:T(1,128)S(1)}, f32[1,32]{1,0:T(1,128)}, u32[]{:S(2)}) copy-start(f32[1,32]{1,0:T(1,128)} %noise.1) | copy-start | bytes 388
  11.2 10.3 %collective-permute-start.2 = (bf16[96,512]{1,0:T(8,128)(2,1)S(1)}, bf16[96,512]{1,0:T(8,128)(2,1)S(1)}, u32[]{:S(2)}, u32[]{:S(2)}) collective-permute-start(bf16[96,512]{1,0:T(8,128)(2,1)S(1)} %get-tuple-element.35), channel_id=1, source_target_pairs={{1,2},{2,1},{3,4},{4,3},{5,6},{6,5},{9,10},{10,9},{11,12},{12,11},... | collective-permute-start | bytes 294920 | tf_op jit(solution)/shard_map/ppermute | solution.py:335
  15.9 6.8 %copy-start.5 = (bf16[512,128]{1,0:T(8,128)(2,1)S(1)}, bf16[512,128]{1,0:T(8,128)(2,1)}, u32[]{:S(2)}) copy-start(bf16[512,128]{1,0:T(8,128)(2,1)} %w_dec.1) | copy-start | bytes 393220
  15.9 6.8 %collective-permute-start.3 = (bf16[96,512]{1,0:T(8,128)(2,1)S(1)}, bf16[96,512]{1,0:T(8,128)(2,1)S(1)}, u32[]{:S(2)}, u32[]{:S(2)}) collective-permute-start(bf16[96,512]{1,0:T(8,128)(2,1)S(1)} %get-tuple-element.22.sent), channel_id=1, source_target_pairs={{0,1},{1,0},{2,3},{3,2},{4,5},{5,4},{6,7},{7,6},{8,9},{9,8},{10,11... | collective-permute-start | bytes 294920 | tf_op jit(solution)/shard_map/ppermute | solution.py:336
  26.2 16.1 %copy-start.8 = (bf16[32,16,128]{2,1,0:T(8,128)(2,1)S(1)}, bf16[32,16,128]{2,1,0:T(8,128)(2,1)}, u32[]{:S(2)}) copy-start(bf16[32,16,128]{2,1,0:T(8,128)(2,1)} %param.13) | copy-start | bytes 393220

commit v6 on v5

--- a/solution.py
+++ b/solution.py
@@ -98,6 +98,11 @@
         out[: 2 * NORTH] = jnp.where(is_top, top[...], bottom[...])
         out[2 * NORTH :] = jnp.zeros((NORTH, out.shape[1]), jnp.bfloat16)
         out[2 * NORTH :, :LANES] = jnp.where(is_top, lines[0], lines[1])
+
+
+def hand_on(message, *others):
+    out = others[-1]
+    out[...] = message[...]
 
 
 def sorted_by(axis, far, near):
@@ -148,13 +153,46 @@
     return jnp.concatenate([grid[:, 0], grid[:, NORTH - 1]], axis=0)
 
 
-def split(out, v):
-    for tile in range(out.shape[0]):
-        out[tile] = v[:, tile * LANES : (tile + 1) * LANES]
-
-
-def joined(tiles):
-    return jnp.concatenate([tiles[tile] for tile in range(tiles.shape[0])], axis=1)
+FOUR = (0, NORTH - 1, 1, NORTH - 2)
+
+
+def begin(
+    sizes, x, slots, noise, w_scale, w_shift, first, gains, links, four_links, own_sum,
+    index, turned,
+):
+    degree = slots.shape[0]
+    for layer in range(w_scale.shape[0]):
+        for at, w in enumerate((w_scale, w_shift)):
+            gains[2 * layer + at : 2 * layer + at + 1] = (1.0 - at) + jnp.dot(
+                noise[...], w[layer], precision=lax.Precision.HIGHEST,
+                preferred_element_type=jnp.float32,
+            )
+    links[...] = jnp.zeros(links.shape, jnp.bfloat16)
+    first[...] = active(x[...].astype(jnp.float32), gains, 0).astype(jnp.bfloat16)
+    found = neighbours(
+        slots[...],
+        lax.broadcasted_iota(jnp.int32, slots.shape, 2),
+        lax.broadcasted_iota(jnp.int32, slots.shape, 1),
+        (here("sx"), here("sy")),
+        sizes,
+    )
+    index[0] = found
+    line, step = (found // NORTH, found % NORTH)
+    end = jnp.where(step == 0, line, jnp.where(step == NORTH - 1, EAST + line, -1))
+    index[1] = jnp.where((found >= 0) & (found < OWN), end, -1)
+    for row in range(EAST):
+        span = slice(row * NORTH, (row + 1) * NORTH)
+        named = [index[0, slot, :, row : row + 1] for slot in range(degree)]
+        tiles = {max(row - 1, 0) * NORTH // LANES, min(row + 1, EAST - 1) * NORTH // LANES}
+        for tile in sorted(tiles) + [OWN // LANES]:
+            links[span, tile * LANES : (tile + 1) * LANES] = counted(named, tile * LANES, LANES)
+    for part, column in enumerate(FOUR):
+        for which, at in enumerate((OWN, 0)):
+            turn = by_row(index.at[which], column, turned.at[2 * part + which])
+            four_links[part * EAST : (part + 1) * EAST, which * LANES : (which + 1) * LANES] = (
+                counted(apart(turn.astype(jnp.int32), degree), at, LANES)
+            )
+    own_sum[...] = dot(links[:, :OWN], first[...])
 
 
 def own_neighbours(arrived, row0, column0, sizes, degree):
@@ -174,75 +212,60 @@
     return counted(apart(index, degree), 0, ALL)
 
 
+def columns(v, which):
+    grid = v.reshape(EAST, NORTH, v.shape[-1])
+    return jnp.concatenate([grid[:, column] for column in which], axis=0)
+
+
 def prepare(
-    sizes, x, slots, noise, w_scale, w_shift, w_self, w_nbr, w_out, far_row, near_row, sent,
-    first, gains, late_links, end_links, end_sum, end_part, x1, sum1, part1,
-    rim_rows, ring_rows, rim_x, links, own_sum, own_part, rim, index, turned,
+    sizes, degree, x, first, gains, links, own_sum, w_self, w_nbr, w_out, w_dec,
+    far_row, near_row, sent,
+    end_sum, end_part, four_sum, two_part, two_x, mid, rim_rows, ring_rows, rim_x,
+    total, part, rim, state,
 ):
-    degree = slots.shape[0]
-    for layer in range(w_scale.shape[0]):
-        for at, w in enumerate((w_scale, w_shift)):
-            gains[2 * layer + at : 2 * layer + at + 1] = (1.0 - at) + jnp.dot(
-                noise[...], w[layer], precision=lax.Precision.HIGHEST,
-                preferred_element_type=jnp.float32,
-            )
-    links[...] = jnp.zeros(links.shape, jnp.bfloat16)
-    first[...] = active(x[...].astype(jnp.float32), gains, 0).astype(jnp.bfloat16)
-    own_part[...] = dot(first[...], w_self[0])
-
-    found = neighbours(
-        slots[...],
-        lax.broadcasted_iota(jnp.int32, slots.shape, 2),
-        lax.broadcasted_iota(jnp.int32, slots.shape, 1),
-        (here("sx"), here("sy")),
-        sizes,
-    )
-    index[0] = found
-    line, step = (found // NORTH, found % NORTH)
-    end = jnp.where(step == 0, line, jnp.where(step == NORTH - 1, EAST + line, -1))
-    index[1] = jnp.where((found >= 0) & (found < OWN), end, -1)
-    for row in range(EAST):
-        span = slice(row * NORTH, (row + 1) * NORTH)
-        named, ended = (
-            [index[which, slot, :, row : row + 1] for slot in range(degree)] for which in (0, 1)
-        )
-        tiles = {max(row - 1, 0) * NORTH // LANES, min(row + 1, EAST - 1) * NORTH // LANES}
-        for tile in sorted(tiles) + [OWN // LANES]:
-            links[span, tile * LANES : (tile + 1) * LANES] = counted(named, tile * LANES, LANES)
-        late_links[span, LANES:] = counted(ended, 0, LANES)
-    late_links[:, :LANES] = links[:, OWN:]
-    for side, column in enumerate((0, NORTH - 1)):
-        ends_found = by_row(index.at[0], column, turned.at[side]).astype(jnp.int32)
-        end_links[side * EAST : (side + 1) * EAST] = counted(
-            apart(ends_found, degree), OWN, OUT - OWN
-        )
-
-    own_sum[...] = dot(links[:, :OWN], first[...])
-    end_part[...] = ends(own_part[...])
-    end_sum[...] = ends(own_sum[...])
+    sixth = 1.0 / degree
+    own = slice(0, OWN)
     top, bottom = sorted_by("sx", far_row, near_row)
     nearer = jnp.concatenate([top[NORTH : 2 * NORTH], bottom[:NORTH]], axis=0)
+    rows = 2 * NORTH
     rim_x[...] = nearer
-    rim_rows[: 2 * NORTH] = active(nearer, gains, 0).astype(jnp.bfloat16)
-    rim_rows[2 * NORTH :] = active(
+    rim_rows[:rows] = active(nearer, gains, 0).astype(jnp.bfloat16)
+    rim_rows[rows:] = active(
         jnp.concatenate([top[:NORTH], bottom[NORTH : 2 * NORTH]], axis=0), gains, 0
     ).astype(jnp.bfloat16)
-    rim[: 2 * NORTH] = rim_rows[: 2 * NORTH]
-    rim[2 * NORTH :] = jnp.zeros((rim.shape[0] - 2 * NORTH, rim.shape[1]), jnp.bfloat16)
-    total = own_sum[...] + dot(links[:, OWN:], rim[...])
-    total = (total * (1.0 / degree)).astype(jnp.bfloat16)
-    v = x[...].astype(jnp.float32) + rest(total, own_part[...], w_nbr, w_out, 0)
-    split(x1, v)
+    rim[...] = jnp.zeros(rim.shape, jnp.bfloat16)
+    rim[:rows] = rim_rows[:rows]
+    rim[OUT - OWN : OUT - OWN + rows] = rim_rows[rows:]
+    ring_rows[:NORTH] = own_neighbours(top, -1, 0, sizes, degree)
+    ring_rows[NORTH:] = own_neighbours(bottom, EAST, 0, sizes, degree)
+
+    part[own] = dot(first[...], w_self[0])
+    end_part[...] = ends(part[own])
+    end_sum[...] = ends(own_sum[...])
+    part[OWN:] = dot(rim_rows[:rows], w_self[0])
+    total[own] = (
+        (own_sum[...] + dot(links[:, OWN:], rim[: OUT - OWN])) * sixth
+    ).astype(jnp.bfloat16)
+    total[OWN:] = (
+        (dot(ring_rows[:, :OWN], first[...]) + dot(ring_rows[:, OWN:], rim[...])) * sixth
+    ).astype(jnp.bfloat16)
+    v = rest(total[...], part[...], w_nbr, w_out, 0)
+    state[...] = x[...].astype(jnp.float32) + v[own]
+    two_x[...] = columns(state[...], FOUR[2:])
+    rim[:rows] = active(nearer + v[OWN:], gains, 1).astype(jnp.bfloat16)
     step = lax.broadcasted_iota(jnp.int32, (OWN, 1), 0) % NORTH
     inner = (step > 0) & (step < NORTH - 1)
-    a1 = jnp.where(inner, active(v, gains, 1), 0.0).astype(jnp.bfloat16)
-    sum1[...] = dot(links[:, :OWN], a1)
-    split(part1, dot(a1, w_self[1]))
-    ring_rows[:NORTH] = own_neighbours(top, -1, 0, sizes, degree)
-    ring_rows[NORTH:] = own_neighbours(bottom, EAST, 0, sizes, degree)
-
-
-def columns_out(w_out, sides, far_row, near_row, far_out, near_out, lines):
+    a1 = jnp.where(inner, active(state[...], gains, 1), 0.0).astype(jnp.bfloat16)
+    sums = dot(links[:, :OWN], a1)
+    four_sum[...] = columns(sums, FOUR)
+    part[own] = dot(a1, w_self[1])
+    two_part[...] = columns(part[own], FOUR[2:])
+    sums = ((sums + dot(links[:, OWN:], rim[: OUT - OWN])) * sixth).astype(jnp.bfloat16)
+    v = state[...] + rest(sums, part[own], w_nbr, w_out, 1)
+    mid[...] = dot(norm(v).astype(jnp.bfloat16), w_dec[...])
+
+
+def columns_out(w_out, gains, sides, far_row, near_row, far_out, near_out, lines):
     top, bottom = sorted_by("sx", far_row, near_row)
     for side, (near, far) in enumerate(((0, 1), (NORTH - 1, NORTH - 2))):
         lines[side] = sides[side]
@@ -264,9 +287,9 @@
 
 
 def advance(
-    sizes, degree, first, gains, late_links, end_links, end_sum, end_part, old_x1, sum1, old_part1,
+    sizes, degree, first, gains, four_links, end_sum, end_part, four_sum, two_part, two_x, old_mid,
     rim_rows, ring_rows, rim_x, sides, far_column, near_column, w_self, w_nbr, w_out, w_dec,
-    preds, sent, x1, part1, rim_first, late, total, part, ring,
+    preds, sent, mid, rim_first, late, total, part, ring,
 ):
     sixth = 1.0 / degree
     west, east = sorted_by("sy", far_column, near_column)
@@ -284,7 +307,7 @@
     ring[rows + PAD :] = own_neighbours(east, -2, NORTH, sizes, degree)
 
     ended = slice(0, 2 * EAST)
-    total[ended] = ((end_sum[...] + dot(end_links[...], rim_first[near])) * sixth).astype(jnp.bfloat16)
+    total[ended] = ((end_sum[...] + dot(four_links[ended, :LANES], rim_first[near])) * sixth).astype(jnp.bfloat16)
     total[2 * EAST :] = (
         (dot(ring[:, :OWN], first[...]) + dot(ring[:, OWN:], rim_first[...])) * sixth
     ).astype(jnp.bfloat16)
@@ -299,15 +322,13 @@
     late[OUT - OWN : OUT - OWN + 2 * EAST] = a_ends
     late[OUT - OWN + 2 * EAST :] = jnp.zeros((LANES - 2 * EAST, late.shape[1]), jnp.bfloat16)
 
-    for out, new in ((x1, v_ends), (part1, dot(a_ends, w_self[1]))):
-        for tile in range(out.shape[0]):
-            for side, place_in in enumerate((0, NORTH - 1)):
-                out[tile, pl.ds(place_in, EAST, stride=NORTH)] = new[
-                    side * EAST : (side + 1) * EAST, tile * LANES : (tile + 1) * LANES
-                ]
-    sums = ((sum1[...] + dot(late_links[...], late[...])) * sixth).astype(jnp.bfloat16)
-    v = joined(x1) + rest(sums, joined(part1), w_nbr, w_out, 1)
-    value = dot(norm(v).astype(jnp.bfloat16), w_dec[...]).astype(jnp.bfloat16)
+    sums = ((four_sum[...] + dot(four_links[...], late[...])) * sixth).astype(jnp.bfloat16)
+    own_part = jnp.concatenate([dot(a_ends, w_self[1]), two_part[...]], axis=0)
+    v = jnp.concatenate([v_ends, two_x[...]], axis=0) + rest(sums, own_part, w_nbr, w_out, 1)
+    value = dot(norm(v).astype(jnp.bfloat16), w_dec[...])
+    for at, place_in in enumerate(FOUR):
+        mid[pl.ds(place_in, EAST, stride=NORTH)] = value[at * EAST : (at + 1) * EAST]
+    value = mid[...].astype(jnp.bfloat16)
     preds[...] = value
     sent[...] = value
 
@@ -331,10 +352,8 @@
 def swap(far, near, axis):
     peers = lax.axis_size(axis)
     pairs = [[(i, i + 1), (i + 1, i)] for i in range(peers - 1)]
-    return (
-        lax.ppermute(far, axis, sum(pairs[1::2], [])),
-        lax.ppermute(near, axis, sum(pairs[0::2], [])),
-    )
+    from_near = lax.ppermute(near, axis, sum(pairs[0::2], []))
+    return lax.ppermute(far, axis, sum(pairs[1::2], [])), from_near
 
 
 def local(states, noises, codes, target, w_self, w_nbr, w_out, w_scale, w_shift, w_dec):
@@ -356,8 +375,8 @@
         return pl.CostEstimate(flops=flops, bytes_accessed=size, transcendentals=0)
 
     slots = codes.transpose(2, 1, 0)
-    far_row, near_row = swap(
-        *pl.pallas_call(
+    far_out, near_out = (
+        pl.pallas_call(
             functools.partial(rows_out, degree),
             grid=(1,),
             out_shape=(like((3 * NORTH, width)),) * 2,
@@ -369,9 +388,17 @@
             out_specs=(pl.BlockSpec((3 * NORTH, width), lambda i: (0, 0)),) * 2,
             compiler_params=pltpu.CompilerParams(vmem_limit_bytes=55104 << 10),
             name="rows_out",
-        )(x, x, slots),
-        "sx",
-    )
+        )(x, x, slots)
+    )
+    far_out = pl.pallas_call(
+        hand_on,
+        out_shape=like(far_out.shape),
+        in_specs=[vmem] + [pl.BlockSpec(memory_space=pl.ANY)] * 4,
+        out_specs=vmem,
+        compiler_params=limits(8),
+        name="hand_on",
+    )(far_out, near_out, noises, w_scale, w_shift)
+    far_row, near_row = swap(far_out, near_out, "sx")
 
     coded = (slots + CODE * here("sx")).transpose(2, 1, 0).reshape(OWN, degree)
     sides = pl.pallas_call(
@@ -385,62 +412,77 @@
         name="collect",
     )(x, coded)
 
+    wide = like((OWN, width), jnp.float32)
+    halves = like((2 * EAST, width), jnp.float32)
+    first, gains, links, four_links, own_sum = pl.pallas_call(
+        functools.partial(begin, sizes),
+        out_shape=(
+            like((OWN, width)),
+            like((2 * layers, width), jnp.float32),
+            like((OWN, OUT)),
+            like((4 * EAST, 2 * LANES)),
+            wide,
+        ),
+        in_specs=[vmem] * 5,
+        out_specs=(vmem,) * 5,
+        scratch_shapes=[
+            pltpu.VMEM((2,) + slots.shape, jnp.int32),
+            pltpu.VMEM((8, 8, LANES), jnp.float32),
+        ],
+        compiler_params=limits(8),
+        cost_estimate=cost(1 << 24, 1 << 24),
+        name="begin",
+    )(x, slots, noises, w_scale, w_shift)
+
     sent = pl.pallas_call(
         columns_out,
         out_shape=(like((SIDE, width)),) * 2,
-        in_specs=[pl.BlockSpec(memory_space=pl.ANY)] + [vmem] * 3,
+        in_specs=[pl.BlockSpec(memory_space=pl.ANY)] * 2 + [vmem] * 3,
         out_specs=(vmem,) * 2,
         scratch_shapes=[pltpu.VMEM((2, SIDE, width), jnp.float32)],
         compiler_params=limits(8),
         cost_estimate=cost(1 << 20, 1 << 25),
         name="columns_out",
-    )(w_out, sides, far_row, near_row)
+    )(w_out, gains, sides, far_row, near_row)
     far_column, near_column = swap(*sent, "sy")
 
-    halves = like((2 * EAST, width), jnp.float32)
-    whole = like((width // LANES, OWN, LANES), jnp.float32)
-    square = pltpu.VMEM((OWN, width), jnp.float32)
     (
-        first, gains, late_links, end_links, end_sum, end_part, x1, sum1, part1,
-        rim_rows, ring_rows, rim_x,
+        end_sum, end_part, four_sum, two_part, two_x, mid, rim_rows, ring_rows, rim_x,
     ) = pl.pallas_call(
-        functools.partial(prepare, sizes),
+        functools.partial(prepare, sizes, degree),
         out_shape=(
-            like((OWN, width)),
-            like((2 * layers, width), jnp.float32),
-            like((OWN, 2 * LANES)),
-            like((2 * EAST, OUT - OWN)),
             halves,
             halves,
-            whole,
-            like((OWN, width), jnp.float32),
-            whole,
+            like((4 * EAST, width), jnp.float32),
+            halves,
+            halves,
+            like((OWN, variables), jnp.float32),
             like((4 * NORTH, width)),
             like((2 * NORTH, ALL)),
             like((2 * NORTH, width), jnp.float32),
         ),
-        in_specs=[vmem] * 10 + [pl.BlockSpec(memory_space=pl.ANY)],
-        out_specs=(vmem,) * 12,
+        in_specs=[vmem] * 11 + [pl.BlockSpec(memory_space=pl.ANY)],
+        out_specs=(vmem,) * 9,
         scratch_shapes=[
-            pltpu.VMEM((OWN, OUT), jnp.bfloat16),
-            square,
-            square,
-            pltpu.VMEM((OUT - OWN, width), jnp.bfloat16),
-            pltpu.VMEM((2,) + slots.shape, jnp.int32),
-            pltpu.VMEM((2, 8, LANES), jnp.float32),
+            pltpu.VMEM((OWN + 2 * NORTH, width), jnp.bfloat16),
+            pltpu.VMEM((OWN + 2 * NORTH, width), jnp.float32),
+            pltpu.VMEM((ALL - OWN, width), jnp.bfloat16),
+            pltpu.VMEM((OWN, width), jnp.float32),
         ],
         compiler_params=limits(16),
         cost_estimate=cost(1 << 24, 1 << 25),
         name="prepare",
-    )(x, slots, noises, w_scale, w_shift, w_self, w_nbr, w_out, far_row, near_row, sent[1])
+    )(
+        x, first, gains, links, own_sum, w_self, w_nbr, w_out, w_dec, far_row, near_row, sent[1]
+    )
 
     busy = 2 * EAST + OUT - OWN
-    preds, shares, _, _ = pl.pallas_call(
+    preds, shares, _ = pl.pallas_call(
         functools.partial(advance, sizes, degree),
-        out_shape=(like((OWN, variables)),) * 2 + (whole,) * 2,
+        out_shape=(like((OWN, variables)),) * 2 + (like(mid.shape, jnp.float32),),
         in_specs=[vmem] * 19,
-        out_specs=(vmem,) * 4,
-        input_output_aliases={6: 2, 8: 3},
+        out_specs=(vmem,) * 3,
+        input_output_aliases={8: 2},
         scratch_shapes=[
             pltpu.VMEM((ALL - OWN, width), jnp.bfloat16),
             pltpu.VMEM((2 * LANES, width), jnp.bfloat16),
@@ -452,7 +494,7 @@
         cost_estimate=cost(1 << 31, 1 << 23),
         name="advance",
     )(
-        first, gains, late_links, end_links, end_sum, end_part, x1, sum1, part1,
+        first, gains, four_links, end_sum, end_part, four_sum, two_part, two_x, mid,
         rim_rows, ring_rows, rim_x, sides, far_column, near_column, w_self, w_nbr, w_out, w_dec,
     )
 

time: 54.9 us -> 54.6 us (level)
  the two profiles are of different devices: /device:TPU:192 before, /device:TPU:132 now
where the time goes in v6:
time: 54.6 us; the launch traced here: 54.3 us
  blocking collectives  29.3 us (54%)
  starting transfers between devices  11.3 us (21%)
  Pallas kernels  9.46 us (17%)
  waiting for transfers between devices  2.39 us (4%)
  between operations  0.87 us (2%)
  other arithmetic  0.73 us (1%)
    all_to_all x1, blocking collectives, local(): lax.all_to_all(shares.reshape(members, share, variables), 'member', 0, 0)  17.3 us
    all_to_all x1, blocking collectives, local(): scores = lax.all_to_all(copies, 'member', 0, 0).astype(jnp.float32)  12 us
    ppermute x2, starting transfers between devices, swap(): from_near = lax.ppermute(near, axis, sum(pairs[0::2], []))  6.91 us
    ppermute x2, starting transfers between devices, swap(): return (lax.ppermute(far, axis, sum(pairs[1::2], [])), from_near)  4.36 us
    pallas_call x1, Pallas kernels, local(): pl.pallas_call(functools.partial(prepare, sizes, degree), out_shape=(halv...  3.76 us
    pallas_call x1, Pallas kernels, local(): pl.pallas_call(functools.partial(advance, sizes, degree), out_shape=(like...  2.77 us
    ppermute x2, waiting for transfers between devices, swap(): return (lax.ppermute(far, axis, sum(pairs[1::2], [])), from_near)  2.38 us
    pallas_call x1, Pallas kernels, local(): pl.pallas_call(functools.partial(begin, sizes), out_shape=(like((OWN, wid...  1.48 us
  transfers between devices with their start and end apart: 4, of which 1 were waited for; matrix products, arithmetic and copies ran while one was open for 0% of the time, Pallas kernels for 10%

profile of v6, /device:TPU:132, one launch (start us, length us, event | category | flops | bytes accessed | tf_op | source)
XLA Modules:
  0.0 54.3 jit_solution(9352051638633432932)
XLA Ops:
  0.6 0.0 copy-start.4
  0.6 0.0 copy-start.5
  0.7 0.0 copy-start.9
  0.7 0.0 copy-start.6
  0.7 1.0 %rows_out.1 = (bf16[48,512]{1,0:T(8,128)(2,1)S(1)}, bf16[48,512]{1,0:T(8,128)(2,1)S(1)}) custom-call(bf16[512,512]{1,0:T(8,128)(2,1)} %bitcast.8, bf16[512,512]{1,0:T(8,128)(2,1)} %bitcast.9, s32[6,16,32]{2,1,0:T(8,128)} %bitcast.14), custom_call_target="tpu_custom_call" | custom-call | tf_op jit(solution)/shard_map/rows_out/pallas_call | solution.py:379
  1.7 0.0 copy-start
  1.7 2.1 %collective-permute-start.1 = (bf16[48,512]{1,0:T(8,128)(2,1)S(1)}, bf16[48,512]{1,0:T(8,128)(2,1)S(1)}, u32[]{:S(2)}, u32[]{:S(2)}) collective-permute-start(bf16[48,512]{1,0:T(8,128)(2,1)S(1)} %get-tuple-element.28.others_0_), channel_id=1, source_target_pairs={{0,8},{8,0},{16,24},{24,16},{32,40},{40,32},{48,56},{56,48},{1,9},... | collective-permute-start | bytes 147464 | tf_op jit(solution)/shard_map/ppermute | solution.py:355
  3.7 0.0 copy-done.4
  3.8 0.0 copy-done.5
  3.8 0.0 copy-done.9
  3.8 1.9 %collective-permute-start = (bf16[48,512]{1,0:T(8,128)(2,1)S(1)}, bf16[48,512]{1,0:T(8,128)(2,1)S(1)}, u32[]{:S(2)}, u32[]{:S(2)}) collective-permute-start(bf16[48,512]{1,0:T(8,128)(2,1)S(1)} %hand_on.1), channel_id=1, source_target_pairs={{8,16},{16,8},{24,32},{32,24},{40,48},{48,40},{9,17},{17,9},{25,33... | collective-permute-start | bytes 147464 | tf_op jit(solution)/shard_map/ppermute | solution.py:356
  5.7 0.0 copy-done.6
  5.7 0.2 copy.13
  6.0 0.0 copy-start.1
  6.0 0.0 copy-done
  6.0 0.2 collect.1.sides
  6.2 0.0 copy-start.2
  6.2 0.0 copy-start.3
  6.2 1.5 %begin.1 = (bf16[512,512]{1,0:T(8,128)(2,1)S(1)}, f32[4,512]{1,0:T(4,128)S(1)}, bf16[512,640]{1,0:T(8,128)(2,1)S(1)}, bf16[128,256]{1,0:T(8,128)(2,1)S(1)}, f32[512,512]{1,0:T(8,128)S(1)}) custom-call(bf16[512,512]{1,0:T(8,128)(2,1)S(1)} %bitcast.11, s32[6,16,32]{2,1,0:T(8,128)S(1)} %bitcast.15, f32[1,32]{1,0:T(1,128)S(1)} %copy-done.9, ...), custom_call_target="tpu_custom_call" | custom-call | flops 16777216 | bytes 16777216 | tf_op jit(solution)/shard_map/begin/pallas_call | solution.py:417
  7.7 2.4 %collective-permute-done.far_row = bf16[48,512]{1,0:T(8,128)(2,1)S(1)} collective-permute-done((bf16[48,512]{1,0:T(8,128)(2,1)S(1)}, bf16[48,512]{1,0:T(8,128)(2,1)S(1)}, u32[]{:S(2)}, u32[]{:S(2)}) %collective-permute-start) | collective-permute-done | bytes 49184 | tf_op jit(solution)/shard_map/ppermute | solution.py:356
  10.1 0.0 collective-permute-done.1.near_row
  10.1 0.0 copy-done.1
  10.1 0.0 copy-start.7
  10.1 0.1 columns_out.1
  10.2 2.4 %collective-permute-start.2 = (bf16[96,512]{1,0:T(8,128)(2,1)S(1)}, bf16[96,512]{1,0:T(8,128)(2,1)S(1)}, u32[]{:S(2)}, u32[]{:S(2)}) collective-permute-start(bf16[96,512]{1,0:T(8,128)(2,1)S(1)} %get-tuple-element.39), channel_id=1, source_target_pairs={{1,2},{2,1},{3,4},{4,3},{5,6},{6,5},{9,10},{10,9},{11,12},{12,11},... | collective-permute-start | bytes 294920 | tf_op jit(solution)/shard_map/ppermute | solution.py:356
  12.6 4.9 %collective-permute-start.3 = (bf16[96,512]{1,0:T(8,128)(2,1)S(1)}, bf16[96,512]{1,0:T(8,128)(2,1)S(1)}, u32[]{:S(2)}, u32[]{:S(2)}) collective-permute-start(bf16[96,512]{1,0:T(8,128)(2,1)S(1)} %get-tuple-element.29.sent), channel_id=1, source_target_pairs={{0,1},{1,0},{2,3},{3,2},{4,5},{5,4},{6,7},{7,6},{8,9},{9,8},{10,11... | collective-permute-start | bytes 294920 | tf_op jit(solution)/shard_map/ppermute | solution.py:355
  17.5 0.0 copy-done.2
  17.5 0.0 copy-done.3
  17.5 0.0 copy-done.7
  17.5 3.8 %prepare.1 = (f32[64,512]{1,0:T(8,128)S(1)}, f32[64,512]{1,0:T(8,128)S(1)}, f32[128,512]{1,0:T(8,128)S(1)}, f32[64,512]{1,0:T(8,128)S(1)}, f32[64,512]{1,0:T(8,1...) custom-call(bf16[512,512]{1,0:T(8,128)(2,1)S(1)} %bitcast.12, ...), custom_call_target="tpu_custom_call" | custom-call | flops 16777216 | bytes 33554432 | tf_op jit(solution)/shard_map/prepare/pallas_call | solution.py:451
  21.3 0.0 collective-permute-done.2.far_column
  21.3 0.0 collective-permute-done.3.near_column
  21.3 2.8 %advance.1 = (bf16[512,128]{1,0:T(8,128)(2,1)}, bf16[512,128]{1,0:T(8,128)(2,1)S(1)}, f32[512,128]{1,0:T(8,128)S(1)}) custom-call(bf16[512,512]{1,0:T(8,128)(2,1)S(1)} %get-tuple-element.22.first, f32[4,512]{1,0:T(4,128)S(1)} %get-tuple-element.23.gains, bf16[128,256]{1,0:T(8,128)(2,1)S(1)} %get-tuple-element.24.four_links, ...), custom_call_target="tpu_custom_call", output_to_operand_aliasing={{2}: (8, {})} | custom-call | flops 2147483648 | bytes 8388608 | tf_op jit(solution)/shard_map/advance/pallas_call | solution.py:480
  24.1 0.0 copy-start.8
  24.1 17.3 %all_to_all.10.mine = bf16[8,64,128]{2,1,0:T(8,128)(2,1)S(1)} all-to-all(bf16[8,64,128]{2,1,0:T(8,128)(2,1)S(1)} %bitcast.17), channel_id=1, replica_groups=mesh['member'=8,'sx'=8,'sy'=8] {'member'}, dimensions={0} | all-to-all | bytes 262144 | tf_op jit(solution)/shard_map/all_to_all | solution.py:503
  41.4 0.0 copy-done.8
  41.4 0.1 score_share.1
  41.5 12.0 %all_to_all.11 = bf16[8,64,128]{2,1,0:T(8,128)(2,1)S(1)} all-to-all(bf16[8,64,128]{2,1,0:T(8,128)(2,1)S(1)} %score_share.1), channel_id=1, replica_groups=mesh['member'=8,'sx'=8,'sy'=8] {'member'}, dimensions={0} | all-to-all | bytes 262144 | tf_op jit(solution)/shard_map/all_to_all | solution.py:512
  53.5 0.7 %convert.1 = f32[32,16,128]{2,1,0:T(8,128)} convert(bf16[32,16,128]{2,1,0:T(8,128)(2,1)S(1)} %bitcast.18) | non-fusion elementwise | flops 65536 | bytes 393216 | tf_op jit(solution)/shard_map/reshape | solution.py:513
  (2 shorter events, 0.0 us)
Async XLA Ops:
  0.6 3.1 %copy-start.4 = (f32[2,32,512]{2,1,0:T(8,128)S(1)}, f32[2,32,512]{2,1,0:T(8,128)}, u32[]{:S(2)}) copy-start(f32[2,32,512]{2,1,0:T(8,128)} %others_2_.1) | copy-start | bytes 393220
  0.6 3.1 %copy-start.5 = (f32[2,32,512]{2,1,0:T(8,128)S(1)}, f32[2,32,512]{2,1,0:T(8,128)}, u32[]{:S(2)}) copy-start(f32[2,32,512]{2,1,0:T(8,128)} %others_3_.1) | copy-start | bytes 393220
  0.7 3.1 %copy-start.9 = (f32[1,32]{1,0:T(1,128)S(1)}, f32[1,32]{1,0:T(1,128)}, u32[]{:S(2)}) copy-start(f32[1,32]{1,0:T(1,128)} %others_1_.1) | copy-start | bytes 388
  0.7 5.1 %copy-start.6 = (s32[32,16,6]{0,1,2:T(8,128)S(1)}, s32[32,16,6]{0,1,2:T(8,128)}, u32[]{:S(2)}) copy-start(s32[32,16,6]{0,1,2:T(8,128)} %param.12) | copy-start | bytes 36868
  1.7 4.3 %copy-start = (bf16[1,32,16,512]{3,2,1,0:T(8,128)(2,1)S(1)}, bf16[1,32,16,512]{3,2,1,0:T(8,128)(2,1)}, u32[]{:S(2)}) copy-start(bf16[1,32,16,512]{3,2,1,0:T(8,128)(2,1)} %param.10) | copy-start | bytes 1572868
  1.7 8.4 %collective-permute-start.1 = (bf16[48,512]{1,0:T(8,128)(2,1)S(1)}, bf16[48,512]{1,0:T(8,128)(2,1)S(1)}, u32[]{:S(2)}, u32[]{:S(2)}) collective-permute-start(bf16[48,512]{1,0:T(8,128)(2,1)S(1)} %get-tuple-element.28.others_0_), channel_id=1, source_target_pairs={{0,8},{8,0},{16,24},{24,16},{32,40},{40,32},{48,56},{56,48},{1,9},... | collective-permute-start | bytes 147464 | tf_op jit(solution)/shard_map/ppermute | solution.py:355
  3.8 6.3 %collective-permute-start = (bf16[48,512]{1,0:T(8,128)(2,1)S(1)}, bf16[48,512]{1,0:T(8,128)(2,1)S(1)}, u32[]{:S(2)}, u32[]{:S(2)}) collective-permute-start(bf16[48,512]{1,0:T(8,128)(2,1)S(1)} %hand_on.1), channel_id=1, source_target_pairs={{8,16},{16,8},{24,32},{32,24},{40,48},{48,40},{9,17},{17,9},{25,33... | collective-permute-start | bytes 147464 | tf_op jit(solution)/shard_map/ppermute | solution.py:356
  6.0 4.1 %copy-start.1 = (bf16[2,512,512]{2,1,0:T(8,128)(2,1)S(1)}, bf16[2,512,512]{2,1,0:T(8,128)(2,1)}, u32[]{:S(2)}) copy-start(bf16[2,512,512]{2,1,0:T(8,128)(2,1)} %w_out.5) | copy-start | bytes 3145732
  6.2 11.3 %copy-start.2 = (bf16[2,512,512]{2,1,0:T(8,128)(2,1)S(1)}, bf16[2,512,512]{2,1,0:T(8,128)(2,1)}, u32[]{:S(2)}) copy-start(bf16[2,512,512]{2,1,0:T(8,128)(2,1)} %w_self.3) | copy-start | bytes 3145732
  6.2 11.3 %copy-start.3 = (bf16[2,512,512]{2,1,0:T(8,128)(2,1)S(1)}, bf16[2,512,512]{2,1,0:T(8,128)(2,1)}, u32[]{:S(2)}) copy-start(bf16[2,512,512]{2,1,0:T(8,128)(2,1)} %w_nbr.3) | copy-start | bytes 3145732
  10.1 7.4 %copy-start.7 = (bf16[512,128]{1,0:T(8,128)(2,1)S(1)}, bf16[512,128]{1,0:T(8,128)(2,1)}, u32[]{:S(2)}) copy-start(bf16[512,128]{1,0:T(8,128)(2,1)} %w_dec.3) | copy-start | bytes 393220
  10.2 11.1 %collective-permute-start.2 = (bf16[96,512]{1,0:T(8,128)(2,1)S(1)}, bf16[96,512]{1,0:T(8,128)(2,1)S(1)}, u32[]{:S(2)}, u32[]{:S(2)}) collective-permute-start(bf16[96,512]{1,0:T(8,128)(2,1)S(1)} %get-tuple-element.39), channel_id=1, source_target_pairs={{1,2},{2,1},{3,4},{4,3},{5,6},{6,5},{9,10},{10,9},{11,12},{12,11},... | collective-permute-start | bytes 294920 | tf_op jit(solution)/shard_map/ppermute | solution.py:356
  12.6 8.7 %collective-permute-start.3 = (bf16[96,512]{1,0:T(8,128)(2,1)S(1)}, bf16[96,512]{1,0:T(8,128)(2,1)S(1)}, u32[]{:S(2)}, u32[]{:S(2)}) collective-permute-start(bf16[96,512]{1,0:T(8,128)(2,1)S(1)} %get-tuple-element.29.sent), channel_id=1, source_target_pairs={{0,1},{1,0},{2,3},{3,2},{4,5},{5,4},{6,7},{7,6},{8,9},{9,8},{10,11... | collective-permute-start | bytes 294920 | tf_op jit(solution)/shard_map/ppermute | solution.py:355
  24.1 17.3 %copy-start.8 = (bf16[32,16,128]{2,1,0:T(8,128)(2,1)S(1)}, bf16[32,16,128]{2,1,0:T(8,128)(2,1)}, u32[]{:S(2)}) copy-start(bf16[32,16,128]{2,1,0:T(8,128)(2,1)} %param.13) | copy-start | bytes 393220

commit v7 on v6

--- a/solution.py
+++ b/solution.py
@@ -249,20 +249,34 @@
     total[OWN:] = (
         (dot(ring_rows[:, :OWN], first[...]) + dot(ring_rows[:, OWN:], rim[...])) * sixth
     ).astype(jnp.bfloat16)
-    v = rest(total[...], part[...], w_nbr, w_out, 0)
-    state[...] = x[...].astype(jnp.float32) + v[own]
+    step = lax.broadcasted_iota(jnp.int32, (OWN // 2, 1), 0) % NORTH
+    inner = (step > 0) & (step < NORTH - 1)
+    spans = [slice(0, OWN // 2), slice(OWN // 2, OWN + rows)]
+    ready = [part[span] + dot(total[span], w_nbr[0]) for span in spans]
+    done = [dot(jax.nn.silu(v).astype(jnp.bfloat16), w_out[0]) for v in ready]
+    rim[:rows] = active(nearer + done[1][OWN // 2 :], gains, 1).astype(jnp.bfloat16)
+    held = []
+    for at, v in zip((0, OWN // 2), done):
+        span = slice(at, at + OWN // 2)
+        state[span] = x[span].astype(jnp.float32) + v[: OWN // 2]
+        held.append(jnp.where(inner, active(state[span], gains, 1), 0.0).astype(jnp.bfloat16))
+    a1 = jnp.concatenate(held, axis=0)
     two_x[...] = columns(state[...], FOUR[2:])
-    rim[:rows] = active(nearer + v[OWN:], gains, 1).astype(jnp.bfloat16)
-    step = lax.broadcasted_iota(jnp.int32, (OWN, 1), 0) % NORTH
-    inner = (step > 0) & (step < NORTH - 1)
-    a1 = jnp.where(inner, active(state[...], gains, 1), 0.0).astype(jnp.bfloat16)
     sums = dot(links[:, :OWN], a1)
     four_sum[...] = columns(sums, FOUR)
     part[own] = dot(a1, w_self[1])
     two_part[...] = columns(part[own], FOUR[2:])
-    sums = ((sums + dot(links[:, OWN:], rim[: OUT - OWN])) * sixth).astype(jnp.bfloat16)
-    v = state[...] + rest(sums, part[own], w_nbr, w_out, 1)
-    mid[...] = dot(norm(v).astype(jnp.bfloat16), w_dec[...])
+    halves = [slice(0, OWN // 2), slice(OWN // 2, OWN)]
+    ready = []
+    for span in halves:
+        mixed = (sums[span] + dot(links[span, OWN:], rim[: OUT - OWN])) * sixth
+        ready.append(part[span] + dot(mixed.astype(jnp.bfloat16), w_nbr[1]))
+    done = []
+    for span, v in zip(halves, ready):
+        hidden = jax.nn.silu(v).astype(jnp.bfloat16)
+        done.append(state[span] + dot(hidden, w_out[1]))
+    for span, v in zip(halves, done):
+        mid[span] = dot(norm(v).astype(jnp.bfloat16), w_dec[...])
 
 
 def columns_out(w_out, gains, sides, far_row, near_row, far_out, near_out, lines):

time: 54.6 us -> 54.3 us (level)
  no operation moved by 1% of the time
where the time goes in v7:
time: 54.3 us; the launch traced here: 54 us
  blocking collectives  29.2 us (54%)
  starting transfers between devices  11.3 us (21%)
  Pallas kernels  9.31 us (17%)
  waiting for transfers between devices  2.39 us (4%)
  between operations  0.87 us (2%)
  other arithmetic  0.73 us (1%)
    all_to_all x1, blocking collectives, local(): lax.all_to_all(shares.reshape(members, share, variables), 'member', 0, 0)  17.2 us
    all_to_all x1, blocking collectives, local(): scores = lax.all_to_all(copies, 'member', 0, 0).astype(jnp.float32)  12 us
    ppermute x2, starting transfers between devices, swap(): from_near = lax.ppermute(near, axis, sum(pairs[0::2], []))  6.91 us
    ppermute x2, starting transfers between devices, swap(): return (lax.ppermute(far, axis, sum(pairs[1::2], [])), from_near)  4.36 us
    pallas_call x1, Pallas kernels, local(): pl.pallas_call(functools.partial(prepare, sizes, degree), out_shape=(halv...  3.61 us
    pallas_call x1, Pallas kernels, local(): pl.pallas_call(functools.partial(advance, sizes, degree), out_shape=(like...  2.77 us
    ppermute x2, waiting for transfers between devices, swap(): return (lax.ppermute(far, axis, sum(pairs[1::2], [])), from_near)  2.38 us
    pallas_call x1, Pallas kernels, local(): pl.pallas_call(functools.partial(begin, sizes), out_shape=(like((OWN, wid...  1.48 us
  transfers between devices with their start and end apart: 4, of which 1 were waited for; matrix products, arithmetic and copies ran while one was open for 0% of the time, Pallas kernels for 10%

profile of v7, /device:TPU:132, one launch (start us, length us, event | category | flops | bytes accessed | tf_op | source)
XLA Modules:
  0.0 54.0 jit_solution(16306901448576296823)
XLA Ops:
  0.6 0.0 copy-start.4
  0.6 0.0 copy-start.5
  0.7 0.0 copy-start.9
  0.7 0.0 copy-start.6
  0.7 1.0 %rows_out.1 = (bf16[48,512]{1,0:T(8,128)(2,1)S(1)}, bf16[48,512]{1,0:T(8,128)(2,1)S(1)}) custom-call(bf16[512,512]{1,0:T(8,128)(2,1)} %bitcast.8, bf16[512,512]{1,0:T(8,128)(2,1)} %bitcast.9, s32[6,16,32]{2,1,0:T(8,128)} %bitcast.14), custom_call_target="tpu_custom_call" | custom-call | tf_op jit(solution)/shard_map/rows_out/pallas_call | solution.py:393
  1.7 0.0 copy-start
  1.7 2.1 %collective-permute-start.1 = (bf16[48,512]{1,0:T(8,128)(2,1)S(1)}, bf16[48,512]{1,0:T(8,128)(2,1)S(1)}, u32[]{:S(2)}, u32[]{:S(2)}) collective-permute-start(bf16[48,512]{1,0:T(8,128)(2,1)S(1)} %get-tuple-element.28.others_0_), channel_id=1, source_target_pairs={{0,8},{8,0},{16,24},{24,16},{32,40},{40,32},{48,56},{56,48},{1,9},... | collective-permute-start | bytes 147464 | tf_op jit(solution)/shard_map/ppermute | solution.py:369
  3.7 0.0 copy-done.4
  3.8 0.0 copy-done.5
  3.8 0.0 copy-done.9
  3.8 1.9 %collective-permute-start = (bf16[48,512]{1,0:T(8,128)(2,1)S(1)}, bf16[48,512]{1,0:T(8,128)(2,1)S(1)}, u32[]{:S(2)}, u32[]{:S(2)}) collective-permute-start(bf16[48,512]{1,0:T(8,128)(2,1)S(1)} %hand_on.1), channel_id=1, source_target_pairs={{8,16},{16,8},{24,32},{32,24},{40,48},{48,40},{9,17},{17,9},{25,33... | collective-permute-start | bytes 147464 | tf_op jit(solution)/shard_map/ppermute | solution.py:370
  5.7 0.0 copy-done.6
  5.7 0.2 copy.13
  6.0 0.0 copy-start.1
  6.0 0.0 copy-done
  6.0 0.2 collect.1.sides
  6.2 0.0 copy-start.2
  6.2 0.0 copy-start.3
  6.2 1.5 %begin.1 = (bf16[512,512]{1,0:T(8,128)(2,1)S(1)}, f32[4,512]{1,0:T(4,128)S(1)}, bf16[512,640]{1,0:T(8,128)(2,1)S(1)}, bf16[128,256]{1,0:T(8,128)(2,1)S(1)}, f32[512,512]{1,0:T(8,128)S(1)}) custom-call(bf16[512,512]{1,0:T(8,128)(2,1)S(1)} %bitcast.11, s32[6,16,32]{2,1,0:T(8,128)S(1)} %bitcast.15, f32[1,32]{1,0:T(1,128)S(1)} %copy-done.9, ...), custom_call_target="tpu_custom_call" | custom-call | flops 16777216 | bytes 16777216 | tf_op jit(solution)/shard_map/begin/pallas_call | solution.py:431
  7.7 2.4 %collective-permute-done.far_row = bf16[48,512]{1,0:T(8,128)(2,1)S(1)} collective-permute-done((bf16[48,512]{1,0:T(8,128)(2,1)S(1)}, bf16[48,512]{1,0:T(8,128)(2,1)S(1)}, u32[]{:S(2)}, u32[]{:S(2)}) %collective-permute-start) | collective-permute-done | bytes 49184 | tf_op jit(solution)/shard_map/ppermute | solution.py:370
  10.1 0.0 collective-permute-done.1.near_row
  10.1 0.0 copy-done.1
  10.1 0.0 copy-start.7
  10.1 0.1 columns_out.1
  10.2 2.4 %collective-permute-start.2 = (bf16[96,512]{1,0:T(8,128)(2,1)S(1)}, bf16[96,512]{1,0:T(8,128)(2,1)S(1)}, u32[]{:S(2)}, u32[]{:S(2)}) collective-permute-start(bf16[96,512]{1,0:T(8,128)(2,1)S(1)} %get-tuple-element.39), channel_id=1, source_target_pairs={{1,2},{2,1},{3,4},{4,3},{5,6},{6,5},{9,10},{10,9},{11,12},{12,11},... | collective-permute-start | bytes 294920 | tf_op jit(solution)/shard_map/ppermute | solution.py:370
  12.6 4.9 %collective-permute-start.3 = (bf16[96,512]{1,0:T(8,128)(2,1)S(1)}, bf16[96,512]{1,0:T(8,128)(2,1)S(1)}, u32[]{:S(2)}, u32[]{:S(2)}) collective-permute-start(bf16[96,512]{1,0:T(8,128)(2,1)S(1)} %get-tuple-element.29.sent), channel_id=1, source_target_pairs={{0,1},{1,0},{2,3},{3,2},{4,5},{5,4},{6,7},{7,6},{8,9},{9,8},{10,11... | collective-permute-start | bytes 294920 | tf_op jit(solution)/shard_map/ppermute | solution.py:369
  17.5 0.0 copy-done.2
  17.5 0.0 copy-done.3
  17.5 0.0 copy-done.7
  17.5 3.6 %prepare.1 = (f32[64,512]{1,0:T(8,128)S(1)}, f32[64,512]{1,0:T(8,128)S(1)}, f32[128,512]{1,0:T(8,128)S(1)}, f32[64,512]{1,0:T(8,128)S(1)}, f32[64,512]{1,0:T(8,1...) custom-call(bf16[512,512]{1,0:T(8,128)(2,1)S(1)} %bitcast.12, ...), custom_call_target="tpu_custom_call" | custom-call | flops 16777216 | bytes 33554432 | tf_op jit(solution)/shard_map/prepare/pallas_call | solution.py:465
  21.2 0.0 collective-permute-done.2.far_column
  21.2 0.0 collective-permute-done.3.near_column
  21.2 2.8 %advance.1 = (bf16[512,128]{1,0:T(8,128)(2,1)}, bf16[512,128]{1,0:T(8,128)(2,1)S(1)}, f32[512,128]{1,0:T(8,128)S(1)}) custom-call(bf16[512,512]{1,0:T(8,128)(2,1)S(1)} %get-tuple-element.22.first, f32[4,512]{1,0:T(4,128)S(1)} %get-tuple-element.23.gains, bf16[128,256]{1,0:T(8,128)(2,1)S(1)} %get-tuple-element.24.four_links, ...), custom_call_target="tpu_custom_call", output_to_operand_aliasing={{2}: (8, {})} | custom-call | flops 2147483648 | bytes 8388608 | tf_op jit(solution)/shard_map/advance/pallas_call | solution.py:494
  23.9 0.0 copy-start.8
  23.9 17.2 %all_to_all.10.mine = bf16[8,64,128]{2,1,0:T(8,128)(2,1)S(1)} all-to-all(bf16[8,64,128]{2,1,0:T(8,128)(2,1)S(1)} %bitcast.17), channel_id=1, replica_groups=mesh['member'=8,'sx'=8,'sy'=8] {'member'}, dimensions={0} | all-to-all | bytes 262144 | tf_op jit(solution)/shard_map/all_to_all | solution.py:517
  41.1 0.0 copy-done.8
  41.1 0.1 score_share.1
  41.2 12.0 %all_to_all.11 = bf16[8,64,128]{2,1,0:T(8,128)(2,1)S(1)} all-to-all(bf16[8,64,128]{2,1,0:T(8,128)(2,1)S(1)} %score_share.1), channel_id=1, replica_groups=mesh['member'=8,'sx'=8,'sy'=8] {'member'}, dimensions={0} | all-to-all | bytes 262144 | tf_op jit(solution)/shard_map/all_to_all | solution.py:526
  53.3 0.7 %convert.1 = f32[32,16,128]{2,1,0:T(8,128)} convert(bf16[32,16,128]{2,1,0:T(8,128)(2,1)S(1)} %bitcast.18) | non-fusion elementwise | flops 65536 | bytes 393216 | tf_op jit(solution)/shard_map/reshape | solution.py:527
  (2 shorter events, 0.0 us)
Async XLA Ops:
  0.6 3.1 %copy-start.4 = (f32[2,32,512]{2,1,0:T(8,128)S(1)}, f32[2,32,512]{2,1,0:T(8,128)}, u32[]{:S(2)}) copy-start(f32[2,32,512]{2,1,0:T(8,128)} %others_2_.1) | copy-start | bytes 393220
  0.6 3.1 %copy-start.5 = (f32[2,32,512]{2,1,0:T(8,128)S(1)}, f32[2,32,512]{2,1,0:T(8,128)}, u32[]{:S(2)}) copy-start(f32[2,32,512]{2,1,0:T(8,128)} %others_3_.1) | copy-start | bytes 393220
  0.7 3.1 %copy-start.9 = (f32[1,32]{1,0:T(1,128)S(1)}, f32[1,32]{1,0:T(1,128)}, u32[]{:S(2)}) copy-start(f32[1,32]{1,0:T(1,128)} %others_1_.1) | copy-start | bytes 388
  0.7 5.1 %copy-start.6 = (s32[32,16,6]{0,1,2:T(8,128)S(1)}, s32[32,16,6]{0,1,2:T(8,128)}, u32[]{:S(2)}) copy-start(s32[32,16,6]{0,1,2:T(8,128)} %param.12) | copy-start | bytes 36868
  1.7 4.3 %copy-start = (bf16[1,32,16,512]{3,2,1,0:T(8,128)(2,1)S(1)}, bf16[1,32,16,512]{3,2,1,0:T(8,128)(2,1)}, u32[]{:S(2)}) copy-start(bf16[1,32,16,512]{3,2,1,0:T(8,128)(2,1)} %param.10) | copy-start | bytes 1572868
  1.7 8.4 %collective-permute-start.1 = (bf16[48,512]{1,0:T(8,128)(2,1)S(1)}, bf16[48,512]{1,0:T(8,128)(2,1)S(1)}, u32[]{:S(2)}, u32[]{:S(2)}) collective-permute-start(bf16[48,512]{1,0:T(8,128)(2,1)S(1)} %get-tuple-element.28.others_0_), channel_id=1, source_target_pairs={{0,8},{8,0},{16,24},{24,16},{32,40},{40,32},{48,56},{56,48},{1,9},... | collective-permute-start | bytes 147464 | tf_op jit(solution)/shard_map/ppermute | solution.py:369
  3.8 6.3 %collective-permute-start = (bf16[48,512]{1,0:T(8,128)(2,1)S(1)}, bf16[48,512]{1,0:T(8,128)(2,1)S(1)}, u32[]{:S(2)}, u32[]{:S(2)}) collective-permute-start(bf16[48,512]{1,0:T(8,128)(2,1)S(1)} %hand_on.1), channel_id=1, source_target_pairs={{8,16},{16,8},{24,32},{32,24},{40,48},{48,40},{9,17},{17,9},{25,33... | collective-permute-start | bytes 147464 | tf_op jit(solution)/shard_map/ppermute | solution.py:370
  6.0 4.1 %copy-start.1 = (bf16[2,512,512]{2,1,0:T(8,128)(2,1)S(1)}, bf16[2,512,512]{2,1,0:T(8,128)(2,1)}, u32[]{:S(2)}) copy-start(bf16[2,512,512]{2,1,0:T(8,128)(2,1)} %w_out.5) | copy-start | bytes 3145732
  6.2 11.3 %copy-start.2 = (bf16[2,512,512]{2,1,0:T(8,128)(2,1)S(1)}, bf16[2,512,512]{2,1,0:T(8,128)(2,1)}, u32[]{:S(2)}) copy-start(bf16[2,512,512]{2,1,0:T(8,128)(2,1)} %w_self.3) | copy-start | bytes 3145732
  6.2 11.3 %copy-start.3 = (bf16[2,512,512]{2,1,0:T(8,128)(2,1)S(1)}, bf16[2,512,512]{2,1,0:T(8,128)(2,1)}, u32[]{:S(2)}) copy-start(bf16[2,512,512]{2,1,0:T(8,128)(2,1)} %w_nbr.3) | copy-start | bytes 3145732
  10.1 7.4 %copy-start.7 = (bf16[512,128]{1,0:T(8,128)(2,1)S(1)}, bf16[512,128]{1,0:T(8,128)(2,1)}, u32[]{:S(2)}) copy-start(bf16[512,128]{1,0:T(8,128)(2,1)} %w_dec.3) | copy-start | bytes 393220
  10.2 11.0 %collective-permute-start.2 = (bf16[96,512]{1,0:T(8,128)(2,1)S(1)}, bf16[96,512]{1,0:T(8,128)(2,1)S(1)}, u32[]{:S(2)}, u32[]{:S(2)}) collective-permute-start(bf16[96,512]{1,0:T(8,128)(2,1)S(1)} %get-tuple-element.39), channel_id=1, source_target_pairs={{1,2},{2,1},{3,4},{4,3},{5,6},{6,5},{9,10},{10,9},{11,12},{12,11},... | collective-permute-start | bytes 294920 | tf_op jit(solution)/shard_map/ppermute | solution.py:370
  12.6 8.5 %collective-permute-start.3 = (bf16[96,512]{1,0:T(8,128)(2,1)S(1)}, bf16[96,512]{1,0:T(8,128)(2,1)S(1)}, u32[]{:S(2)}, u32[]{:S(2)}) collective-permute-start(bf16[96,512]{1,0:T(8,128)(2,1)S(1)} %get-tuple-element.29.sent), channel_id=1, source_target_pairs={{0,1},{1,0},{2,3},{3,2},{4,5},{5,4},{6,7},{7,6},{8,9},{9,8},{10,11... | collective-permute-start | bytes 294920 | tf_op jit(solution)/shard_map/ppermute | solution.py:369
  23.9 17.2 %copy-start.8 = (bf16[32,16,128]{2,1,0:T(8,128)(2,1)S(1)}, bf16[32,16,128]{2,1,0:T(8,128)(2,1)}, u32[]{:S(2)}) copy-start(bf16[32,16,128]{2,1,0:T(8,128)(2,1)} %param.13) | copy-start | bytes 393220

commit v8 on v7

--- a/solution.py
+++ b/solution.py
@@ -247,7 +247,12 @@
         (own_sum[...] + dot(links[:, OWN:], rim[: OUT - OWN])) * sixth
     ).astype(jnp.bfloat16)
     total[OWN:] = (
-        (dot(ring_rows[:, :OWN], first[...]) + dot(ring_rows[:, OWN:], rim[...])) * sixth
+        (
+            dot(ring_rows[:, :LANES], first[:LANES])
+            + dot(ring_rows[:, OWN - LANES : OWN], first[OWN - LANES :])
+            + dot(ring_rows[:, OWN:], rim[...])
+        )
+        * sixth
     ).astype(jnp.bfloat16)
     step = lax.broadcasted_iota(jnp.int32, (OWN // 2, 1), 0) % NORTH
     inner = (step > 0) & (step < NORTH - 1)

time: 54.3 us -> 54.4 us (level)
  no operation moved by 1% of the time
where the time goes in v8:
time: 54.4 us; the launch traced here: 54 us
  blocking collectives  29.3 us (54%)
  starting transfers between devices  11.3 us (21%)
  Pallas kernels  9.26 us (17%)
  waiting for transfers between devices  2.39 us (4%)
  between operations  0.87 us (2%)
  other arithmetic  0.73 us (1%)
    all_to_all x1, blocking collectives, local(): lax.all_to_all(shares.reshape(members, share, variables), 'member', 0, 0)  17.3 us
    all_to_all x1, blocking collectives, local(): scores = lax.all_to_all(copies, 'member', 0, 0).astype(jnp.float32)  12 us
    ppermute x2, starting transfers between devices, swap(): from_near = lax.ppermute(near, axis, sum(pairs[0::2], []))  6.91 us
    ppermute x2, starting transfers between devices, swap(): return (lax.ppermute(far, axis, sum(pairs[1::2], [])), from_near)  4.36 us
    pallas_call x1, Pallas kernels, local(): pl.pallas_call(functools.partial(prepare, sizes, degree), out_shape=(halv...  3.59 us
    pallas_call x1, Pallas kernels, local(): pl.pallas_call(functools.partial(advance, sizes, degree), out_shape=(like...  2.76 us
    ppermute x2, waiting for transfers between devices, swap(): return (lax.ppermute(far, axis, sum(pairs[1::2], [])), from_near)  2.38 us
    pallas_call x1, Pallas kernels, local(): pl.pallas_call(functools.partial(begin, sizes), out_shape=(like((OWN, wid...  1.48 us
  transfers between devices with their start and end apart: 4, of which 1 were waited for; matrix products, arithmetic and copies ran while one was open for 0% of the time, Pallas kernels for 10%

profile of v8, /device:TPU:132, one launch (start us, length us, event | category | flops | bytes accessed | tf_op | source)
XLA Modules:
  0.0 54.0 jit_solution(3173188751609429080)
XLA Ops:
  0.6 0.0 copy-start.4
  0.6 0.0 copy-start.5
  0.7 0.0 copy-start.9
  0.7 0.0 copy-start.6
  0.7 1.0 %rows_out.1 = (bf16[48,512]{1,0:T(8,128)(2,1)S(1)}, bf16[48,512]{1,0:T(8,128)(2,1)S(1)}) custom-call(bf16[512,512]{1,0:T(8,128)(2,1)} %bitcast.8, bf16[512,512]{1,0:T(8,128)(2,1)} %bitcast.9, s32[6,16,32]{2,1,0:T(8,128)} %bitcast.14), custom_call_target="tpu_custom_call" | custom-call | tf_op jit(solution)/shard_map/rows_out/pallas_call | solution.py:398
  1.7 0.0 copy-start
  1.7 2.1 %collective-permute-start.1 = (bf16[48,512]{1,0:T(8,128)(2,1)S(1)}, bf16[48,512]{1,0:T(8,128)(2,1)S(1)}, u32[]{:S(2)}, u32[]{:S(2)}) collective-permute-start(bf16[48,512]{1,0:T(8,128)(2,1)S(1)} %get-tuple-element.28.others_0_), channel_id=1, source_target_pairs={{0,8},{8,0},{16,24},{24,16},{32,40},{40,32},{48,56},{56,48},{1,9},... | collective-permute-start | bytes 147464 | tf_op jit(solution)/shard_map/ppermute | solution.py:374
  3.7 0.0 copy-done.4
  3.8 0.0 copy-done.5
  3.8 0.0 copy-done.9
  3.8 1.9 %collective-permute-start = (bf16[48,512]{1,0:T(8,128)(2,1)S(1)}, bf16[48,512]{1,0:T(8,128)(2,1)S(1)}, u32[]{:S(2)}, u32[]{:S(2)}) collective-permute-start(bf16[48,512]{1,0:T(8,128)(2,1)S(1)} %hand_on.1), channel_id=1, source_target_pairs={{8,16},{16,8},{24,32},{32,24},{40,48},{48,40},{9,17},{17,9},{25,33... | collective-permute-start | bytes 147464 | tf_op jit(solution)/shard_map/ppermute | solution.py:375
  5.7 0.0 copy-done.6
  5.7 0.2 copy.13
  6.0 0.0 copy-start.1
  6.0 0.0 copy-done
  6.0 0.2 collect.1.sides
  6.2 0.0 copy-start.2
  6.2 0.0 copy-start.3
  6.2 1.5 %begin.1 = (bf16[512,512]{1,0:T(8,128)(2,1)S(1)}, f32[4,512]{1,0:T(4,128)S(1)}, bf16[512,640]{1,0:T(8,128)(2,1)S(1)}, bf16[128,256]{1,0:T(8,128)(2,1)S(1)}, f32[512,512]{1,0:T(8,128)S(1)}) custom-call(bf16[512,512]{1,0:T(8,128)(2,1)S(1)} %bitcast.11, s32[6,16,32]{2,1,0:T(8,128)S(1)} %bitcast.15, f32[1,32]{1,0:T(1,128)S(1)} %copy-done.9, ...), custom_call_target="tpu_custom_call" | custom-call | flops 16777216 | bytes 16777216 | tf_op jit(solution)/shard_map/begin/pallas_call | solution.py:436
  7.7 2.4 %collective-permute-done.far_row = bf16[48,512]{1,0:T(8,128)(2,1)S(1)} collective-permute-done((bf16[48,512]{1,0:T(8,128)(2,1)S(1)}, bf16[48,512]{1,0:T(8,128)(2,1)S(1)}, u32[]{:S(2)}, u32[]{:S(2)}) %collective-permute-start) | collective-permute-done | bytes 49184 | tf_op jit(solution)/shard_map/ppermute | solution.py:375
  10.1 0.0 collective-permute-done.1.near_row
  10.1 0.0 copy-done.1
  10.1 0.0 copy-start.7
  10.1 0.1 columns_out.1
  10.2 2.4 %collective-permute-start.2 = (bf16[96,512]{1,0:T(8,128)(2,1)S(1)}, bf16[96,512]{1,0:T(8,128)(2,1)S(1)}, u32[]{:S(2)}, u32[]{:S(2)}) collective-permute-start(bf16[96,512]{1,0:T(8,128)(2,1)S(1)} %get-tuple-element.39), channel_id=1, source_target_pairs={{1,2},{2,1},{3,4},{4,3},{5,6},{6,5},{9,10},{10,9},{11,12},{12,11},... | collective-permute-start | bytes 294920 | tf_op jit(solution)/shard_map/ppermute | solution.py:375
  12.6 4.9 %collective-permute-start.3 = (bf16[96,512]{1,0:T(8,128)(2,1)S(1)}, bf16[96,512]{1,0:T(8,128)(2,1)S(1)}, u32[]{:S(2)}, u32[]{:S(2)}) collective-permute-start(bf16[96,512]{1,0:T(8,128)(2,1)S(1)} %get-tuple-element.29.sent), channel_id=1, source_target_pairs={{0,1},{1,0},{2,3},{3,2},{4,5},{5,4},{6,7},{7,6},{8,9},{9,8},{10,11... | collective-permute-start | bytes 294920 | tf_op jit(solution)/shard_map/ppermute | solution.py:374
  17.5 0.0 copy-done.2
  17.5 0.0 copy-done.3
  17.5 0.0 copy-done.7
  17.5 3.6 %prepare.1 = (f32[64,512]{1,0:T(8,128)S(1)}, f32[64,512]{1,0:T(8,128)S(1)}, f32[128,512]{1,0:T(8,128)S(1)}, f32[64,512]{1,0:T(8,128)S(1)}, f32[64,512]{1,0:T(8,1...) custom-call(bf16[512,512]{1,0:T(8,128)(2,1)S(1)} %bitcast.12, ...), custom_call_target="tpu_custom_call" | custom-call | flops 16777216 | bytes 33554432 | tf_op jit(solution)/shard_map/prepare/pallas_call | solution.py:470
  21.1 0.0 collective-permute-done.2.far_column
  21.1 0.0 collective-permute-done.3.near_column
  21.1 2.8 %advance.1 = (bf16[512,128]{1,0:T(8,128)(2,1)}, bf16[512,128]{1,0:T(8,128)(2,1)S(1)}, f32[512,128]{1,0:T(8,128)S(1)}) custom-call(bf16[512,512]{1,0:T(8,128)(2,1)S(1)} %get-tuple-element.22.first, f32[4,512]{1,0:T(4,128)S(1)} %get-tuple-element.23.gains, bf16[128,256]{1,0:T(8,128)(2,1)S(1)} %get-tuple-element.24.four_links, ...), custom_call_target="tpu_custom_call", output_to_operand_aliasing={{2}: (8, {})} | custom-call | flops 2147483648 | bytes 8388608 | tf_op jit(solution)/shard_map/advance/pallas_call | solution.py:499
  23.9 0.0 copy-start.8
  23.9 17.3 %all_to_all.10.mine = bf16[8,64,128]{2,1,0:T(8,128)(2,1)S(1)} all-to-all(bf16[8,64,128]{2,1,0:T(8,128)(2,1)S(1)} %bitcast.17), channel_id=1, replica_groups=mesh['member'=8,'sx'=8,'sy'=8] {'member'}, dimensions={0} | all-to-all | bytes 262144 | tf_op jit(solution)/shard_map/all_to_all | solution.py:522
  41.2 0.0 copy-done.8
  41.2 0.1 score_share.1
  41.3 12.0 %all_to_all.11 = bf16[8,64,128]{2,1,0:T(8,128)(2,1)S(1)} all-to-all(bf16[8,64,128]{2,1,0:T(8,128)(2,1)S(1)} %score_share.1), channel_id=1, replica_groups=mesh['member'=8,'sx'=8,'sy'=8] {'member'}, dimensions={0} | all-to-all | bytes 262144 | tf_op jit(solution)/shard_map/all_to_all | solution.py:531
  53.3 0.7 %convert.1 = f32[32,16,128]{2,1,0:T(8,128)} convert(bf16[32,16,128]{2,1,0:T(8,128)(2,1)S(1)} %bitcast.18) | non-fusion elementwise | flops 65536 | bytes 393216 | tf_op jit(solution)/shard_map/reshape | solution.py:532
  (2 shorter events, 0.0 us)
Async XLA Ops:
  0.6 3.1 %copy-start.4 = (f32[2,32,512]{2,1,0:T(8,128)S(1)}, f32[2,32,512]{2,1,0:T(8,128)}, u32[]{:S(2)}) copy-start(f32[2,32,512]{2,1,0:T(8,128)} %others_2_.1) | copy-start | bytes 393220
  0.6 3.1 %copy-start.5 = (f32[2,32,512]{2,1,0:T(8,128)S(1)}, f32[2,32,512]{2,1,0:T(8,128)}, u32[]{:S(2)}) copy-start(f32[2,32,512]{2,1,0:T(8,128)} %others_3_.1) | copy-start | bytes 393220
  0.7 3.1 %copy-start.9 = (f32[1,32]{1,0:T(1,128)S(1)}, f32[1,32]{1,0:T(1,128)}, u32[]{:S(2)}) copy-start(f32[1,32]{1,0:T(1,128)} %others_1_.1) | copy-start | bytes 388
  0.7 5.1 %copy-start.6 = (s32[32,16,6]{0,1,2:T(8,128)S(1)}, s32[32,16,6]{0,1,2:T(8,128)}, u32[]{:S(2)}) copy-start(s32[32,16,6]{0,1,2:T(8,128)} %param.12) | copy-start | bytes 36868
  1.7 4.3 %copy-start = (bf16[1,32,16,512]{3,2,1,0:T(8,128)(2,1)S(1)}, bf16[1,32,16,512]{3,2,1,0:T(8,128)(2,1)}, u32[]{:S(2)}) copy-start(bf16[1,32,16,512]{3,2,1,0:T(8,128)(2,1)} %param.10) | copy-start | bytes 1572868
  1.7 8.4 %collective-permute-start.1 = (bf16[48,512]{1,0:T(8,128)(2,1)S(1)}, bf16[48,512]{1,0:T(8,128)(2,1)S(1)}, u32[]{:S(2)}, u32[]{:S(2)}) collective-permute-start(bf16[48,512]{1,0:T(8,128)(2,1)S(1)} %get-tuple-element.28.others_0_), channel_id=1, source_target_pairs={{0,8},{8,0},{16,24},{24,16},{32,40},{40,32},{48,56},{56,48},{1,9},... | collective-permute-start | bytes 147464 | tf_op jit(solution)/shard_map/ppermute | solution.py:374
  3.8 6.3 %collective-permute-start = (bf16[48,512]{1,0:T(8,128)(2,1)S(1)}, bf16[48,512]{1,0:T(8,128)(2,1)S(1)}, u32[]{:S(2)}, u32[]{:S(2)}) collective-permute-start(bf16[48,512]{1,0:T(8,128)(2,1)S(1)} %hand_on.1), channel_id=1, source_target_pairs={{8,16},{16,8},{24,32},{32,24},{40,48},{48,40},{9,17},{17,9},{25,33... | collective-permute-start | bytes 147464 | tf_op jit(solution)/shard_map/ppermute | solution.py:375
  6.0 4.1 %copy-start.1 = (bf16[2,512,512]{2,1,0:T(8,128)(2,1)S(1)}, bf16[2,512,512]{2,1,0:T(8,128)(2,1)}, u32[]{:S(2)}) copy-start(bf16[2,512,512]{2,1,0:T(8,128)(2,1)} %w_out.5) | copy-start | bytes 3145732
  6.2 11.3 %copy-start.2 = (bf16[2,512,512]{2,1,0:T(8,128)(2,1)S(1)}, bf16[2,512,512]{2,1,0:T(8,128)(2,1)}, u32[]{:S(2)}) copy-start(bf16[2,512,512]{2,1,0:T(8,128)(2,1)} %w_self.3) | copy-start | bytes 3145732
  6.2 11.3 %copy-start.3 = (bf16[2,512,512]{2,1,0:T(8,128)(2,1)S(1)}, bf16[2,512,512]{2,1,0:T(8,128)(2,1)}, u32[]{:S(2)}) copy-start(bf16[2,512,512]{2,1,0:T(8,128)(2,1)} %w_nbr.3) | copy-start | bytes 3145732
  10.1 7.4 %copy-start.7 = (bf16[512,128]{1,0:T(8,128)(2,1)S(1)}, bf16[512,128]{1,0:T(8,128)(2,1)}, u32[]{:S(2)}) copy-start(bf16[512,128]{1,0:T(8,128)(2,1)} %w_dec.3) | copy-start | bytes 393220
  10.2 10.9 %collective-permute-start.2 = (bf16[96,512]{1,0:T(8,128)(2,1)S(1)}, bf16[96,512]{1,0:T(8,128)(2,1)S(1)}, u32[]{:S(2)}, u32[]{:S(2)}) collective-permute-start(bf16[96,512]{1,0:T(8,128)(2,1)S(1)} %get-tuple-element.39), channel_id=1, source_target_pairs={{1,2},{2,1},{3,4},{4,3},{5,6},{6,5},{9,10},{10,9},{11,12},{12,11},... | collective-permute-start | bytes 294920 | tf_op jit(solution)/shard_map/ppermute | solution.py:375
  12.6 8.5 %collective-permute-start.3 = (bf16[96,512]{1,0:T(8,128)(2,1)S(1)}, bf16[96,512]{1,0:T(8,128)(2,1)S(1)}, u32[]{:S(2)}, u32[]{:S(2)}) collective-permute-start(bf16[96,512]{1,0:T(8,128)(2,1)S(1)} %get-tuple-element.29.sent), channel_id=1, source_target_pairs={{0,1},{1,0},{2,3},{3,2},{4,5},{5,4},{6,7},{7,6},{8,9},{9,8},{10,11... | collective-permute-start | bytes 294920 | tf_op jit(solution)/shard_map/ppermute | solution.py:374
  23.9 17.3 %copy-start.8 = (bf16[32,16,128]{2,1,0:T(8,128)(2,1)S(1)}, bf16[32,16,128]{2,1,0:T(8,128)(2,1)}, u32[]{:S(2)}) copy-start(bf16[32,16,128]{2,1,0:T(8,128)(2,1)} %param.13) | copy-start | bytes 393220
